TPU v7x, 128 devices: a whole 4x4x4 slice. The times are simulated.
128 devices in a mesh: seq: 16 (over x, z), mp: 8 (over y, core).
Axes of the slice: x: 4, y: 4, z: 4, core: 2. Of those that a mesh axis runs over, the one named last changes fastest.
Arguments:
- latents: bfloat16 [1024, 1280], P('seq'), may hold values from -6 to 6
- key_weight: bfloat16 [1280, 8192], P(None, 'mp'), may hold values from -0.15625 to 0.15625
- value_weight: bfloat16 [1280, 8192], P(None, 'mp'), may hold values from -0.15625 to 0.15625
- queries: bfloat16 [32768, 8192], P('seq', 'mp'), may hold values from -6 to 6
- upstream: bfloat16 [32768, 8192], P('seq', 'mp'), may hold values from -6 to 6
- gate: float32 [8192], P('mp'), may hold values from -1.5 to 1.5
- media: int32 [32, 4], P('seq'), may hold values from 0 to 15, all different within a row
- frame_slot: int32 [16], replicated, may hold values from 0 to 15, each once
- lengths: int32 [32], P('seq'), may hold values from 1 to 1024, 16384 in all
Outputs:
- query_grad: bfloat16 [32768, 8192], P('seq', 'mp')
- key_grad: float32 [1280, 8192], P('seq', 'mp')
- value_grad: float32 [1280, 8192], P('seq', 'mp')
Inputs may be any that keep to these rules, and one draw needn't show every extreme that they name: `media`: each group names 4 different frames; every frame is named by some group. `frame_slot`: each slot holds exactly one frame. `lengths`: some group is full.
All inputs are finite; a program needn't handle non-finite values.
Results may differ from a plain program's by a relative error of at most 0.009.
Values may be sent and summed in bfloat16 or wider, within the bound.
No kernel may reach another device: no remote copies, remote signals or barrier semaphores. Data moves between devices by JAX's collectives and lax.ppermute only.
A program may use at most 128 MiB of HBM per device.

v0:
```python
import functools
import math

import jax
import jax.numpy as jnp
from jax import lax
from jax.experimental import pallas as pl
from jax.experimental.pallas import tpu as pltpu
from jax.sharding import PartitionSpec as P

HEAD_DIM = 128
LATENTS = 64
SIDE = 4
PAIR = 2 * HEAD_DIM
TOKEN_BLOCK = 256
ONES = (((1,), (1,)), ((), ()))
ZEROS = (((0,), (0,)), ((), ()))


def shift(array, major, minor, mp):
    pairs = []
    for x in range(SIDE):
        for z in range(SIDE):
            for m in range(mp):
                dx, dz = (major, minor) if m % 2 == 0 else (minor, major)
                to = ((x + dx) % SIDE) * SIDE + (z + dz) % SIDE
                pairs.append(((x * SIDE + z) * mp + m, to * mp + m))
    return lax.ppermute(array, ("seq", "mp"), pairs)


def swap_cores(array, mp):
    return lax.ppermute(array, "mp", [(m, m ^ 1) for m in range(mp)])


def gather_latents(latents, mp):
    half = latents.shape[1] // 2
    mine = jnp.where(lax.axis_index("mp") % 2 == 0, latents[:, :half], latents[:, half:])
    far = shift(mine, 2, 0, mp)
    near = [shift(mine, step, 0, mp) for step in (1, 3)]
    line = jnp.concatenate([mine, near[0], far, near[1]], axis=0)
    far = shift(line, 0, 2, mp)
    near = [shift(line, 0, step, mp) for step in (1, 3)]
    fetched = [line, near[0], far, near[1]]
    return fetched + [swap_cores(part, mp) for part in fetched]


def attention_kernel(
    media, frame_slot, lengths, place, *refs
):
    parts = refs[:8]
    gate, key_weight, value_weight, queries, upstream, query_grad = refs[8:14]
    messages = refs[14:22]
    picked, picked_t, keys, values, key_sum, value_sum, key_part, value_part, rows_key, rows_value = refs[22:]
    groups, named = media.shape
    group_keys = named * LATENTS
    group_len = queries.shape[0] // groups
    half = parts[0].shape[1]
    seq, core = place[0], place[1]
    x, z = seq // SIDE, seq % SIDE
    scale = HEAD_DIM ** -0.5
    sharpness = scale * math.log2(math.e)

    @pl.when(pl.program_id(0) == 0)
    def _():
        for group in range(groups):
            for name in range(named):
                slot = frame_slot[media[group, name]]
                dx = (x - slot // SIDE + SIDE) % SIDE
                dz = (z - slot % SIDE + SIDE) % SIDE
                to = pl.ds((group * named + name) * LATENTS, LATENTS)
                for side in range(2):
                    minor, major = (dx, dz) if side == 0 else (dz, dx)
                    start = pl.ds(pl.multiple_of(minor * LATENTS, LATENTS), LATENTS)
                    first = jnp.where(core == side, 0, 4)
                    for at in range(8):

                        @pl.when(first + major == at)
                        def _():
                            picked[to, side * half : (side + 1) * half] = parts[at][start, :]

        picked_t[...] = picked[...].T

    keys[...] = jnp.dot(picked[...], key_weight[...], preferred_element_type=jnp.float32).astype(jnp.bfloat16)
    values[...] = jnp.dot(picked[...], value_weight[...], preferred_element_type=jnp.float32).astype(jnp.bfloat16)
    gate_tanh = jnp.tanh(gate[...])

    for group in range(groups):
        rows = slice(group * group_keys, (group + 1) * group_keys)
        length = lengths[group]
        blocks = (length + TOKEN_BLOCK - 1) // TOKEN_BLOCK
        key_sum[...] = jnp.zeros_like(key_sum)
        value_sum[...] = jnp.zeros_like(value_sum)

        def block(step, carry):
            at = pl.multiple_of(step * TOKEN_BLOCK, TOKEN_BLOCK)
            tokens = pl.ds(group * group_len + at, TOKEN_BLOCK)
            live = lax.broadcasted_iota(jnp.int32, (TOKEN_BLOCK, HEAD_DIM), 0) + at < length
            for head in range(2):
                cols = slice(head * HEAD_DIM, (head + 1) * HEAD_DIM)
                k, v = keys[rows, cols], values[rows, cols]
                q = queries[tokens, cols]
                gated = gate_tanh[:, cols] * upstream[tokens, cols].astype(jnp.float32)
                dout = jnp.where(live, gated, 0.0).astype(jnp.bfloat16)
                scores = lax.dot_general(k, q, ONES, preferred_element_type=jnp.float32)
                dprob = lax.dot_general(v, dout, ONES, preferred_element_type=jnp.float32)
                top = jnp.max(scores, axis=0, keepdims=True)
                powers = jnp.exp2((scores - top) * sharpness)
                probs = powers * (1.0 / jnp.sum(powers, axis=0, keepdims=True))
                delta = jnp.sum(probs * dprob, axis=0, keepdims=True)
                dscore = (probs * (dprob - delta)).astype(jnp.bfloat16)
                probs_b = probs.astype(jnp.bfloat16)
                key_sum[:, cols] += jnp.dot(dscore, q, preferred_element_type=jnp.float32)
                value_sum[:, cols] += jnp.dot(probs_b, dout, preferred_element_type=jnp.float32)
                grad = lax.dot_general(dscore, k, ZEROS, preferred_element_type=jnp.float32)
                query_grad[tokens, cols] = (grad * scale).astype(jnp.bfloat16)
            return carry

        lax.fori_loop(0, blocks, block, 0)

        def blank(step, carry):
            tokens = pl.ds(group * group_len + pl.multiple_of(step * TOKEN_BLOCK, TOKEN_BLOCK), TOKEN_BLOCK)
            query_grad[tokens, :] = jnp.zeros((TOKEN_BLOCK, PAIR), jnp.bfloat16)
            return carry

        lax.fori_loop(blocks, group_len // TOKEN_BLOCK, blank, 0)
        key_part[rows, :] = (key_sum[...] * scale).astype(jnp.bfloat16)
        value_part[rows, :] = value_sum[...].astype(jnp.bfloat16)

    rows_key[...] = jnp.dot(picked_t[...], key_part[...], preferred_element_type=jnp.float32).astype(jnp.bfloat16)
    rows_value[...] = jnp.dot(picked_t[...], value_part[...], preferred_element_type=jnp.float32).astype(jnp.bfloat16)
    share = rows_key.shape[0] // (SIDE * SIDE)
    for major in range(SIDE):
        for minor in range(SIDE):
            dx = jnp.where(core == 0, major, minor)
            dz = jnp.where(core == 0, minor, major)
            owner = ((x + dx) % SIDE) * SIDE + (z + dz) % SIDE
            source = pl.ds(pl.multiple_of(owner * share, 16), share)
            to = slice(minor * share, (minor + 1) * share)
            messages[major][to, :] = rows_key[source, :]
            messages[SIDE + major][to, :] = rows_value[source, :]


def attention(parts, key_weight, value_weight, queries, upstream, gate, media, frame_slot, lengths, place):
    tokens, width = queries.shape
    vision = key_weight.shape[0]
    steps = width // PAIR
    picked_rows = media.shape[0] * media.shape[1] * LATENTS
    group_keys = media.shape[1] * LATENTS
    whole = lambda array: pl.BlockSpec(array.shape, lambda step, *_: (0, 0))
    columns = lambda rows: pl.BlockSpec((rows, PAIR), lambda step, *_: (0, step))
    quarter = vision // SIDE
    bf16, f32 = jnp.bfloat16, jnp.float32
    return pl.pallas_call(
        attention_kernel,
        grid_spec=pltpu.PrefetchScalarGridSpec(
            num_scalar_prefetch=4,
            grid=(steps,),
            in_specs=[whole(part) for part in parts]
            + [columns(1), columns(vision), columns(vision), columns(tokens), columns(tokens)],
            out_specs=[columns(tokens)] + [columns(quarter)] * (2 * SIDE),
            scratch_shapes=[
                pltpu.VMEM((picked_rows, vision), bf16),
                pltpu.VMEM((vision, picked_rows), bf16),
                pltpu.VMEM((picked_rows, PAIR), bf16),
                pltpu.VMEM((picked_rows, PAIR), bf16),
                pltpu.VMEM((group_keys, PAIR), f32),
                pltpu.VMEM((group_keys, PAIR), f32),
                pltpu.VMEM((picked_rows, PAIR), bf16),
                pltpu.VMEM((picked_rows, PAIR), bf16),
                pltpu.VMEM((vision, PAIR), bf16),
                pltpu.VMEM((vision, PAIR), bf16),
            ],
        ),
        out_shape=[jax.ShapeDtypeStruct((tokens, width), bf16)]
        + [jax.ShapeDtypeStruct((quarter, width), bf16)] * (2 * SIDE),
        compiler_params=pltpu.CompilerParams(vmem_limit_bytes=48 * 1024 * 1024),
    )(media, frame_slot, lengths, place, *parts, gate[None, :], key_weight, value_weight, queries, upstream)


def add(*arrays):
    return functools.reduce(jnp.add, [array.astype(jnp.float32) for array in arrays])


def scatter_sum(messages, mp):
    key, value = messages[:SIDE], messages[SIDE:]
    share = key[0].shape[0] // SIDE
    bf16 = jnp.bfloat16
    key_far = shift(key[2], 1, 0, mp)
    value_far = shift(value[2], 3, 0, mp)
    value_near = shift(value[1], 1, 0, mp)
    key_near = shift(key[3], 3, 0, mp)
    key_on = shift(add(key[1], key_far).astype(bf16), 1, 0, mp)
    value_on = shift(add(value[3], value_far).astype(bf16), 3, 0, mp)
    key_rows = add(key[0], key_near, key_on)
    value_rows = add(value[0], value_near, value_on)
    both = [
        jnp.concatenate([key_rows[at * share : (at + 1) * share], value_rows[at * share : (at + 1) * share]], axis=0)
        for at in range(SIDE)
    ]
    came = [shift(both[at].astype(bf16), 0, at, mp) for at in (2, 1, 3)]
    total = add(both[0], *came)
    return total[:share], total[share:]


def local(latents, key_weight, value_weight, queries, upstream, gate, media, frame_slot, lengths, *, mp):
    parts = gather_latents(latents, mp)
    place = jnp.stack([lax.axis_index("seq"), lax.axis_index("mp") % 2]).astype(jnp.int32)
    query_grad, *messages = attention(
        parts, key_weight, value_weight, queries, upstream, gate, media, frame_slot, lengths, place
    )
    key_grad, value_grad = scatter_sum(messages, mp)
    return query_grad, key_grad, value_grad


def solution(mesh):
    in_specs = (
        P("seq", None),
        P(None, "mp"),
        P(None, "mp"),
        P("seq", "mp"),
        P("seq", "mp"),
        P("mp"),
        P("seq", None),
        P(),
        P("seq"),
    )
    out_specs = (P("seq", "mp"), P("seq", "mp"), P("seq", "mp"))
    body = functools.partial(local, mp=mesh.shape["mp"])
    return jax.shard_map(body, mesh=mesh, in_specs=in_specs, out_specs=out_specs, check_vma=False)
```

profile of v0, /device:TPU:0, one launch (start us, length us, event | category | flops | bytes accessed | tf_op | source)
XLA Modules:
  0.0 116.5 jit_solution(16209314063439109323)
XLA Ops:
  0.6 0.9 slice_select_fusion
  1.6 2.9 %collective-permute-start.2 = (bf16[64,640]{1,0:T(8,128)(2,1)S(1)}, bf16[64,640]{1,0:T(8,128)(2,1)S(1)}, u32[]{:S(2)}, u32[]{:S(2)}) collective-permute-start(bf16[64,640]{1,0:T(8,128)(2,1)S(1)} %slice_select_fusion), channel_id=1, source_target_pairs={{0,96},{1,25},{2,98},{3,27},{4,100},{5,29},{6,102},{7,31},{8,104},... | collective-permute-start | bytes 245768 | tf_op jit(solution)/shard_map/ppermute | solution.py:28
  6.6 3.9 %collective-permute-done.1 = bf16[64,640]{1,0:T(8,128)(2,1)S(1)} collective-permute-done((bf16[64,640]{1,0:T(8,128)(2,1)S(1)}, bf16[64,640]{1,0:T(8,128)(2,1)S(1)}, u32[]{:S(2)}, u32[]{:S(2)}) %collective-permute-start.1) | collective-permute-done | bytes 81952 | tf_op jit(solution)/shard_map/ppermute | solution.py:28
  11.4 4.1 %collective-permute-start.5 = (bf16[256,640]{1,0:T(8,128)(2,1)S(1)}, bf16[256,640]{1,0:T(8,128)(2,1)S(1)}, u32[]{:S(2)}, u32[]{:S(2)}) collective-permute-start(bf16[256,640]{1,0:T(8,128)(2,1)S(1)} %pad_maximum_fusion.refs_0_), channel_id=1, source_target_pairs={{0,24},{1,97},{2,26},{3,99},{4,28},{5,101},{6,30},{7,103},{8,0},{9... | collective-permute-start | bytes 983048 | tf_op jit(solution)/shard_map/ppermute | solution.py:28
  15.5 1.3 %collective-permute-start.3 = (bf16[256,640]{1,0:T(8,128)(2,1)S(1)}, bf16[256,640]{1,0:T(8,128)(2,1)S(1)}, u32[]{:S(2)}, u32[]{:S(2)}) collective-permute-start(bf16[256,640]{1,0:T(8,128)(2,1)S(1)} %pad_maximum_fusion.refs_0_), channel_id=1, source_target_pairs={{0,8},{1,33},{2,10},{3,35},{4,12},{5,37},{6,14},{7,39},{8,16},{9,4... | collective-permute-start | bytes 983048 | tf_op jit(solution)/shard_map/ppermute | solution.py:28
  16.7 6.8 %collective-permute-done.5.refs_3_ = bf16[256,640]{1,0:T(8,128)(2,1)S(1)} collective-permute-done((bf16[256,640]{1,0:T(8,128)(2,1)S(1)}, bf16[256,640]{1,0:T(8,128)(2,1)S(1)}, u32[]{:S(2)}, u32[]{:S(2)}) %collective-permute-start.5) | collective-permute-done | bytes 327712 | tf_op jit(solution)/shard_map/ppermute | solution.py:28
  24.1 3.1 %collective-permute-done.3.refs_1_ = bf16[256,640]{1,0:T(8,128)(2,1)S(1)} collective-permute-done((bf16[256,640]{1,0:T(8,128)(2,1)S(1)}, bf16[256,640]{1,0:T(8,128)(2,1)S(1)}, u32[]{:S(2)}, u32[]{:S(2)}) %collective-permute-start.3) | collective-permute-done | bytes 327712 | tf_op jit(solution)/shard_map/ppermute | solution.py:28
  27.4 1.5 %collective-permute-done.7.refs_5_ = bf16[256,640]{1,0:T(8,128)(2,1)S(1)} collective-permute-done((bf16[256,640]{1,0:T(8,128)(2,1)S(1)}, bf16[256,640]{1,0:T(8,128)(2,1)S(1)}, u32[]{:S(2)}, u32[]{:S(2)}) %collective-permute-start.7) | collective-permute-done | bytes 327712 | tf_op jit(solution)/shard_map/ppermute | solution.py:32
  31.6 24.6 %shard_map.112 = (bf16[2048,1024]{1,0:T(8,128)(2,1)}, bf16[320,1024]{1,0:T(8,128)(2,1)S(1)}, bf16[320,1024]{1,0:T(8,128)(2,1)S(1)}, bf16[320,1024]{1,0:T(8,128)(...) custom-call(s32[2,4]{1,0:T(2,128)S(1)} %copy-done.1, ...), custom_call_target="tpu_custom_call" | custom-call | tf_op jit(solution)/shard_map/pallas_call | solution.py:153
  56.2 3.2 %collective-permute-start.11 = (bf16[320,1024]{1,0:T(8,128)(2,1)S(1)}, bf16[320,1024]{1,0:T(8,128)(2,1)S(1)}, u32[]{:S(2)}, u32[]{:S(2)}) collective-permute-start(bf16[320,1024]{1,0:T(8,128)(2,1)S(1)} %get-tuple-element.16), channel_id=1, source_target_pairs={{0,32},{1,9},{2,34},{3,11},{4,36},{5,13},{6,38},{7,15},{8,40},{9,1... | collective-permute-start | bytes 1966088 | tf_op jit(solution)/shard_map/ppermute | solution.py:28
  59.5 5.2 %collective-permute-start.14 = (bf16[320,1024]{1,0:T(8,128)(2,1)}, bf16[320,1024]{1,0:T(8,128)(2,1)S(1)}, u32[]{:S(2)}, u32[]{:S(2)}) collective-permute-start(bf16[320,1024]{1,0:T(8,128)(2,1)} %get-tuple-element.20), channel_id=1, source_target_pairs={{0,96},{1,25},{2,98},{3,27},{4,100},{5,29},{6,102},{7,31},{8,104},... | collective-permute-start | bytes 1966088 | tf_op jit(solution)/shard_map/ppermute | solution.py:28
  64.7 1.9 %collective-permute-start.10 = (bf16[320,1024]{1,0:T(8,128)(2,1)S(1)}, bf16[320,1024]{1,0:T(8,128)(2,1)S(1)}, u32[]{:S(2)}, u32[]{:S(2)}) collective-permute-start(bf16[320,1024]{1,0:T(8,128)(2,1)S(1)} %get-tuple-element.14), channel_id=1, source_target_pairs={{0,96},{1,25},{2,98},{3,27},{4,100},{5,29},{6,102},{7,31},{8,104},... | collective-permute-start | bytes 1966088 | tf_op jit(solution)/shard_map/ppermute | solution.py:28
  66.6 6.5 %collective-permute-done.11 = bf16[320,1024]{1,0:T(8,128)(2,1)S(1)} collective-permute-done((bf16[320,1024]{1,0:T(8,128)(2,1)S(1)}, bf16[320,1024]{1,0:T(8,128)(2,1)S(1)}, u32[]{:S(2)}, u32[]{:S(2)}) %collective-permute-start.11) | collective-permute-done | bytes 655392 | tf_op jit(solution)/shard_map/ppermute | solution.py:28
  73.5 0.9 collective-permute-start.13
  74.7 2.4 %collective-permute-start.15 = (bf16[320,1024]{1,0:T(8,128)(2,1)S(1)}, bf16[320,1024]{1,0:T(8,128)(2,1)S(1)}, u32[]{:S(2)}, u32[]{:S(2)}) collective-permute-start(bf16[320,1024]{1,0:T(8,128)(2,1)S(1)} %add_convert_fusion), channel_id=1, source_target_pairs={{0,96},{1,25},{2,98},{3,27},{4,100},{5,29},{6,102},{7,31},{8,104},... | collective-permute-start | bytes 1966088 | tf_op jit(solution)/shard_map/ppermute | solution.py:28
  77.1 2.9 %collective-permute-done.10 = bf16[320,1024]{1,0:T(8,128)(2,1)S(1)} collective-permute-done((bf16[320,1024]{1,0:T(8,128)(2,1)S(1)}, bf16[320,1024]{1,0:T(8,128)(2,1)S(1)}, u32[]{:S(2)}, u32[]{:S(2)}) %collective-permute-start.10) | collective-permute-done | bytes 655392 | tf_op jit(solution)/shard_map/ppermute | solution.py:28
  80.0 5.3 %collective-permute-done.12 = bf16[320,1024]{1,0:T(8,128)(2,1)S(1)} collective-permute-done((bf16[320,1024]{1,0:T(8,128)(2,1)S(1)}, bf16[320,1024]{1,0:T(8,128)(2,1)S(1)}, u32[]{:S(2)}, u32[]{:S(2)}) %collective-permute-start.12) | collective-permute-done | bytes 655392 | tf_op jit(solution)/shard_map/ppermute | solution.py:28
  85.6 6.6 %collective-permute-done.13 = bf16[320,1024]{1,0:T(8,128)(2,1)S(1)} collective-permute-done((bf16[320,1024]{1,0:T(8,128)(2,1)S(1)}, bf16[320,1024]{1,0:T(8,128)(2,1)S(1)}, u32[]{:S(2)}, u32[]{:S(2)}) %collective-permute-start.13) | collective-permute-done | bytes 655392 | tf_op jit(solution)/shard_map/ppermute | solution.py:28
  92.8 1.5 %collective-permute-start.17 = (bf16[160,1024]{1,0:T(8,128)(2,1)S(1)}, bf16[160,1024]{1,0:T(8,128)(2,1)S(1)}, u32[]{:S(2)}, u32[]{:S(2)}) collective-permute-start(bf16[160,1024]{1,0:T(8,128)(2,1)S(1)} %pad_maximum_fusion.2), channel_id=1, source_target_pairs={{0,8},{1,33},{2,10},{3,35},{4,12},{5,37},{6,14},{7,39},{8,16},{9,4... | collective-permute-start | bytes 983048 | tf_op jit(solution)/shard_map/ppermute | solution.py:28
  94.3 11.2 %collective-permute-start.18 = (bf16[160,1024]{1,0:T(8,128)(2,1)S(1)}, bf16[160,1024]{1,0:T(8,128)(2,1)S(1)}, u32[]{:S(2)}, u32[]{:S(2)}) collective-permute-start(bf16[160,1024]{1,0:T(8,128)(2,1)S(1)} %pad_maximum_fusion.3), channel_id=1, source_target_pairs={{0,24},{1,97},{2,26},{3,99},{4,28},{5,101},{6,30},{7,103},{8,0},{9... | collective-permute-start | bytes 983048 | tf_op jit(solution)/shard_map/ppermute | solution.py:28
  105.5 1.5 %collective-permute-start.16 = (bf16[160,1024]{1,0:T(8,128)(2,1)S(1)}, bf16[160,1024]{1,0:T(8,128)(2,1)S(1)}, u32[]{:S(2)}, u32[]{:S(2)}) collective-permute-start(bf16[160,1024]{1,0:T(8,128)(2,1)S(1)} %pad_maximum_fusion.1), channel_id=1, source_target_pairs={{0,16},{1,65},{2,18},{3,67},{4,20},{5,69},{6,22},{7,71},{8,24},{9,... | collective-permute-start | bytes 983048 | tf_op jit(solution)/shard_map/ppermute | solution.py:28
  107.1 3.3 %collective-permute-done.17 = bf16[160,1024]{1,0:T(8,128)(2,1)S(1)} collective-permute-done((bf16[160,1024]{1,0:T(8,128)(2,1)S(1)}, bf16[160,1024]{1,0:T(8,128)(2,1)S(1)}, u32[]{:S(2)}, u32[]{:S(2)}) %collective-permute-start.17) | collective-permute-done | bytes 327712 | tf_op jit(solution)/shard_map/ppermute | solution.py:28
  110.4 3.2 %collective-permute-done.18 = bf16[160,1024]{1,0:T(8,128)(2,1)S(1)} collective-permute-done((bf16[160,1024]{1,0:T(8,128)(2,1)S(1)}, bf16[160,1024]{1,0:T(8,128)(2,1)S(1)}, u32[]{:S(2)}, u32[]{:S(2)}) %collective-permute-start.18) | collective-permute-done | bytes 327712 | tf_op jit(solution)/shard_map/ppermute | solution.py:28
  113.6 1.8 %collective-permute-done.16 = bf16[160,1024]{1,0:T(8,128)(2,1)S(1)} collective-permute-done((bf16[160,1024]{1,0:T(8,128)(2,1)S(1)}, bf16[160,1024]{1,0:T(8,128)(2,1)S(1)}, u32[]{:S(2)}, u32[]{:S(2)}) %collective-permute-start.16) | collective-permute-done | bytes 327712 | tf_op jit(solution)/shard_map/ppermute | solution.py:28
  (42 shorter events, 8.8 us)
Async XLA Ops:
  1.6 5.0 %collective-permute-start.2 = (bf16[64,640]{1,0:T(8,128)(2,1)S(1)}, bf16[64,640]{1,0:T(8,128)(2,1)S(1)}, u32[]{:S(2)}, u32[]{:S(2)}) collective-permute-start(bf16[64,640]{1,0:T(8,128)(2,1)S(1)} %slice_select_fusion), channel_id=1, source_target_pairs={{0,96},{1,25},{2,98},{3,27},{4,100},{5,29},{6,102},{7,31},{8,104},... | collective-permute-start | bytes 245768 | tf_op jit(solution)/shard_map/ppermute | solution.py:28
  4.5 6.0 %collective-permute-start.1 = (bf16[64,640]{1,0:T(8,128)(2,1)S(1)}, bf16[64,640]{1,0:T(8,128)(2,1)S(1)}, u32[]{:S(2)}, u32[]{:S(2)}) collective-permute-start(bf16[64,640]{1,0:T(8,128)(2,1)S(1)} %slice_select_fusion), channel_id=1, source_target_pairs={{0,64},{1,17},{2,66},{3,19},{4,68},{5,21},{6,70},{7,23},{8,72},{9,... | collective-permute-start | bytes 245768 | tf_op jit(solution)/shard_map/ppermute | solution.py:28
  5.3 6.0 %collective-permute-start = (bf16[64,640]{1,0:T(8,128)(2,1)S(1)}, bf16[64,640]{1,0:T(8,128)(2,1)S(1)}, u32[]{:S(2)}, u32[]{:S(2)}) collective-permute-start(bf16[64,640]{1,0:T(8,128)(2,1)S(1)} %slice_select_fusion), channel_id=1, source_target_pairs={{0,32},{1,9},{2,34},{3,11},{4,36},{5,13},{6,38},{7,15},{8,40},{9,1... | collective-permute-start | bytes 245768 | tf_op jit(solution)/shard_map/ppermute | solution.py:28
  11.4 12.2 %collective-permute-start.5 = (bf16[256,640]{1,0:T(8,128)(2,1)S(1)}, bf16[256,640]{1,0:T(8,128)(2,1)S(1)}, u32[]{:S(2)}, u32[]{:S(2)}) collective-permute-start(bf16[256,640]{1,0:T(8,128)(2,1)S(1)} %pad_maximum_fusion.refs_0_), channel_id=1, source_target_pairs={{0,24},{1,97},{2,26},{3,99},{4,28},{5,101},{6,30},{7,103},{8,0},{9... | collective-permute-start | bytes 983048 | tf_op jit(solution)/shard_map/ppermute | solution.py:28
  15.5 8.7 %collective-permute-start.4 = (bf16[256,640]{1,0:T(8,128)(2,1)S(1)}, bf16[256,640]{1,0:T(8,128)(2,1)S(1)}, u32[]{:S(2)}, u32[]{:S(2)}) collective-permute-start(bf16[256,640]{1,0:T(8,128)(2,1)S(1)} %pad_maximum_fusion.refs_0_), channel_id=1, source_target_pairs={{0,16},{1,65},{2,18},{3,67},{4,20},{5,69},{6,22},{7,71},{8,24},{9,... | collective-permute-start | bytes 983048 | tf_op jit(solution)/shard_map/ppermute | solution.py:28
  15.5 11.8 %collective-permute-start.3 = (bf16[256,640]{1,0:T(8,128)(2,1)S(1)}, bf16[256,640]{1,0:T(8,128)(2,1)S(1)}, u32[]{:S(2)}, u32[]{:S(2)}) collective-permute-start(bf16[256,640]{1,0:T(8,128)(2,1)S(1)} %pad_maximum_fusion.refs_0_), channel_id=1, source_target_pairs={{0,8},{1,33},{2,10},{3,35},{4,12},{5,37},{6,14},{7,39},{8,16},{9,4... | collective-permute-start | bytes 983048 | tf_op jit(solution)/shard_map/ppermute | solution.py:28
  16.7 10.6 %collective-permute-start.6 = (bf16[256,640]{1,0:T(8,128)(2,1)S(1)}, bf16[256,640]{1,0:T(8,128)(2,1)S(1)}, u32[]{:S(2)}, u32[]{:S(2)}) collective-permute-start(bf16[256,640]{1,0:T(8,128)(2,1)S(1)} %pad_maximum_fusion.refs_0_), channel_id=1, source_target_pairs={{0,1},{1,0},{2,3},{3,2},{4,5},{5,4},{6,7},{7,6},{8,9},{9,8},{10,11... | collective-permute-start | bytes 983048 | tf_op jit(solution)/shard_map/ppermute | solution.py:32
  23.6 3.8 %collective-permute-start.9 = (bf16[256,640]{1,0:T(8,128)(2,1)S(1)}, bf16[256,640]{1,0:T(8,128)(2,1)S(1)}, u32[]{:S(2)}, u32[]{:S(2)}) collective-permute-start(bf16[256,640]{1,0:T(8,128)(2,1)S(1)} %collective-permute-done.5.refs_3_), channel_id=1, source_target_pairs={{0,1},{1,0},{2,3},{3,2},{4,5},{5,4},{6,7},{7,6},{8,9},{9,8},{10,11... | collective-permute-start | bytes 983048 | tf_op jit(solution)/shard_map/ppermute | solution.py:32
  24.1 3.2 %collective-permute-start.8 = (bf16[256,640]{1,0:T(8,128)(2,1)S(1)}, bf16[256,640]{1,0:T(8,128)(2,1)S(1)}, u32[]{:S(2)}, u32[]{:S(2)}) collective-permute-start(bf16[256,640]{1,0:T(8,128)(2,1)S(1)} %collective-permute-done.4.refs_2_), channel_id=1, source_target_pairs={{0,1},{1,0},{2,3},{3,2},{4,5},{5,4},{6,7},{7,6},{8,9},{9,8},{10,11... | collective-permute-start | bytes 983048 | tf_op jit(solution)/shard_map/ppermute | solution.py:32
  27.3 1.6 %collective-permute-start.7 = (bf16[256,640]{1,0:T(8,128)(2,1)S(1)}, bf16[256,640]{1,0:T(8,128)(2,1)S(1)}, u32[]{:S(2)}, u32[]{:S(2)}) collective-permute-start(bf16[256,640]{1,0:T(8,128)(2,1)S(1)} %collective-permute-done.3.refs_1_), channel_id=1, source_target_pairs={{0,1},{1,0},{2,3},{3,2},{4,5},{5,4},{6,7},{7,6},{8,9},{9,8},{10,11... | collective-permute-start | bytes 983048 | tf_op jit(solution)/shard_map/ppermute | solution.py:32
  28.9 0.7 copy-start
  29.6 0.7 copy-start.1
  30.3 0.7 copy-start.2
  56.2 17.3 %copy-start.5 = (bf16[320,1024]{1,0:T(8,128)(2,1)S(1)}, bf16[320,1024]{1,0:T(8,128)(2,1)}, u32[]{:S(2)}) copy-start(bf16[320,1024]{1,0:T(8,128)(2,1)} %get-tuple-element.18) | copy-start | bytes 1966084
  56.2 18.2 %copy-start.4 = (bf16[320,1024]{1,0:T(8,128)(2,1)S(1)}, bf16[320,1024]{1,0:T(8,128)(2,1)}, u32[]{:S(2)}) copy-start(bf16[320,1024]{1,0:T(8,128)(2,1)} %get-tuple-element.19) | copy-start | bytes 1966084
  56.2 16.9 %collective-permute-start.11 = (bf16[320,1024]{1,0:T(8,128)(2,1)S(1)}, bf16[320,1024]{1,0:T(8,128)(2,1)S(1)}, u32[]{:S(2)}, u32[]{:S(2)}) collective-permute-start(bf16[320,1024]{1,0:T(8,128)(2,1)S(1)} %get-tuple-element.16), channel_id=1, source_target_pairs={{0,32},{1,9},{2,34},{3,11},{4,36},{5,13},{6,38},{7,15},{8,40},{9,1... | collective-permute-start | bytes 1966088 | tf_op jit(solution)/shard_map/ppermute | solution.py:28
  59.5 14.9 %collective-permute-start.14 = (bf16[320,1024]{1,0:T(8,128)(2,1)}, bf16[320,1024]{1,0:T(8,128)(2,1)S(1)}, u32[]{:S(2)}, u32[]{:S(2)}) collective-permute-start(bf16[320,1024]{1,0:T(8,128)(2,1)} %get-tuple-element.20), channel_id=1, source_target_pairs={{0,96},{1,25},{2,98},{3,27},{4,100},{5,29},{6,102},{7,31},{8,104},... | collective-permute-start | bytes 1966088 | tf_op jit(solution)/shard_map/ppermute | solution.py:28
  64.7 15.3 %collective-permute-start.10 = (bf16[320,1024]{1,0:T(8,128)(2,1)S(1)}, bf16[320,1024]{1,0:T(8,128)(2,1)S(1)}, u32[]{:S(2)}, u32[]{:S(2)}) collective-permute-start(bf16[320,1024]{1,0:T(8,128)(2,1)S(1)} %get-tuple-element.14), channel_id=1, source_target_pairs={{0,96},{1,25},{2,98},{3,27},{4,100},{5,29},{6,102},{7,31},{8,104},... | collective-permute-start | bytes 1966088 | tf_op jit(solution)/shard_map/ppermute | solution.py:28
  73.4 11.9 %collective-permute-start.12 = (bf16[320,1024]{1,0:T(8,128)(2,1)S(1)}, bf16[320,1024]{1,0:T(8,128)(2,1)S(1)}, u32[]{:S(2)}, u32[]{:S(2)}) collective-permute-start(bf16[320,1024]{1,0:T(8,128)(2,1)S(1)} %add_convert_fusion.1), channel_id=1, source_target_pairs={{0,32},{1,9},{2,34},{3,11},{4,36},{5,13},{6,38},{7,15},{8,40},{9,1... | collective-permute-start | bytes 1966088 | tf_op jit(solution)/shard_map/ppermute | solution.py:28
  73.5 18.8 %collective-permute-start.13 = (bf16[320,1024]{1,0:T(8,128)(2,1)S(1)}, bf16[320,1024]{1,0:T(8,128)(2,1)S(1)}, u32[]{:S(2)}, u32[]{:S(2)}) collective-permute-start(bf16[320,1024]{1,0:T(8,128)(2,1)S(1)} %copy-done.5), channel_id=1, source_target_pairs={{0,32},{1,9},{2,34},{3,11},{4,36},{5,13},{6,38},{7,15},{8,40},{9,1... | collective-permute-start | bytes 1966088 | tf_op jit(solution)/shard_map/ppermute | solution.py:28
  74.7 17.6 %collective-permute-start.15 = (bf16[320,1024]{1,0:T(8,128)(2,1)S(1)}, bf16[320,1024]{1,0:T(8,128)(2,1)S(1)}, u32[]{:S(2)}, u32[]{:S(2)}) collective-permute-start(bf16[320,1024]{1,0:T(8,128)(2,1)S(1)} %add_convert_fusion), channel_id=1, source_target_pairs={{0,96},{1,25},{2,98},{3,27},{4,100},{5,29},{6,102},{7,31},{8,104},... | collective-permute-start | bytes 1966088 | tf_op jit(solution)/shard_map/ppermute | solution.py:28
  92.8 17.7 %collective-permute-start.17 = (bf16[160,1024]{1,0:T(8,128)(2,1)S(1)}, bf16[160,1024]{1,0:T(8,128)(2,1)S(1)}, u32[]{:S(2)}, u32[]{:S(2)}) collective-permute-start(bf16[160,1024]{1,0:T(8,128)(2,1)S(1)} %pad_maximum_fusion.2), channel_id=1, source_target_pairs={{0,8},{1,33},{2,10},{3,35},{4,12},{5,37},{6,14},{7,39},{8,16},{9,4... | collective-permute-start | bytes 983048 | tf_op jit(solution)/shard_map/ppermute | solution.py:28
  94.3 19.3 %collective-permute-start.18 = (bf16[160,1024]{1,0:T(8,128)(2,1)S(1)}, bf16[160,1024]{1,0:T(8,128)(2,1)S(1)}, u32[]{:S(2)}, u32[]{:S(2)}) collective-permute-start(bf16[160,1024]{1,0:T(8,128)(2,1)S(1)} %pad_maximum_fusion.3), channel_id=1, source_target_pairs={{0,24},{1,97},{2,26},{3,99},{4,28},{5,101},{6,30},{7,103},{8,0},{9... | collective-permute-start | bytes 983048 | tf_op jit(solution)/shard_map/ppermute | solution.py:28
  105.5 9.9 %collective-permute-start.16 = (bf16[160,1024]{1,0:T(8,128)(2,1)S(1)}, bf16[160,1024]{1,0:T(8,128)(2,1)S(1)}, u32[]{:S(2)}, u32[]{:S(2)}) collective-permute-start(bf16[160,1024]{1,0:T(8,128)(2,1)S(1)} %pad_maximum_fusion.1), channel_id=1, source_target_pairs={{0,16},{1,65},{2,18},{3,67},{4,20},{5,69},{6,22},{7,71},{8,24},{9,... | collective-permute-start | bytes 983048 | tf_op jit(solution)/shard_map/ppermute | solution.py:28
  (1 other events, 0.7 us)
where the time goes:
time: 118 us; the launch traced here: 116 us
  waiting for transfers between devices  46.8 us (40%)
  starting transfers between devices  38 us (32%)
  Pallas kernels  24.6 us (21%)
  local copies, waits for them, and re-layouts  3.67 us (3%)
  other arithmetic  2.52 us (2%)
    ppermute x15, waiting for transfers between devices, shift(): return lax.ppermute(array, ('seq', 'mp'), pairs)  45.3 us
    ppermute x15, starting transfers between devices, shift(): return lax.ppermute(array, ('seq', 'mp'), pairs)  38 us
    pallas_call x1, Pallas kernels, attention(): pl.pallas_call(attention_kernel, grid_spec=pltpu.PrefetchScalarGridSpec(n...  24.6 us
    unnamed x12, local copies, waits for them, and re-layouts  2.68 us
  transfers between devices with their start and end apart: 19, of which 14 were waited for; matrix products, arithmetic and copies ran while one was open for 1% of the time, Pallas kernels for 0%

commit v1 on v0

v1 whole, which is shorter than its diff:
```python
import functools
import math

import jax
import jax.numpy as jnp
from jax import lax
from jax.experimental import pallas as pl
from jax.experimental.pallas import tpu as pltpu
from jax.sharding import PartitionSpec as P

HEAD_DIM = 128
LATENTS = 64
SIDE = 4
HEADS = 2
PAIR = HEADS * HEAD_DIM
TOKEN_BLOCK = 512
ONES = (((1,), (1,)), ((), ()))
ZEROS = (((0,), (0,)), ((), ()))
BF16 = jnp.bfloat16
F32 = jnp.float32


def shift(array, major, minor, mp):
    pairs = []
    for x in range(SIDE):
        for z in range(SIDE):
            for m in range(mp):
                dx, dz = (major, minor) if m % 2 == 0 else (minor, major)
                to = ((x + dx) % SIDE) * SIDE + (z + dz) % SIDE
                pairs.append(((x * SIDE + z) * mp + m, to * mp + m))
    return lax.ppermute(array, ("seq", "mp"), pairs)


def swap_cores(array, mp):
    return lax.ppermute(array, "mp", [(m, m ^ 1) for m in range(mp)])


def gather_latents(latents, aside, mp):
    half = latents.shape[1] // 2
    mine = jnp.where(lax.axis_index("mp") % 2 == 0, latents[:, :half], latents[:, half:])
    far = shift(mine, 2, 0, mp)
    near = [shift(mine, step, 0, mp) for step in (1, 3)]
    line = jnp.concatenate([mine, near[0], far, near[1]], axis=0)
    far = shift(line, 0, 2, mp)
    near = [shift(line, 0, step, mp) for step in (1, 3)]
    line, aside = lax.optimization_barrier((line, aside))
    fetched = [line, near[0], far, near[1]]
    return fetched + [swap_cores(part, mp) for part in fetched], aside


def numbers_at(groups, named, frames):
    slots = groups * named
    lengths = slots + frames
    return slots, lengths, lengths + groups


def pick(numbers, parts, picked, turned, picked_t, groups, named):
    slots_at, lengths_at, place_at = numbers_at(groups, named, SIDE * SIDE)
    half = parts[0].shape[1]
    seq, core = numbers[place_at], numbers[place_at + 1]
    x, z = seq // SIDE, seq % SIDE
    for name in range(groups * named):
        slot = numbers[slots_at + numbers[name]]
        dx = (x - slot // SIDE + SIDE) % SIDE
        dz = (z - slot % SIDE + SIDE) % SIDE
        to = pl.ds(name * LATENTS, LATENTS)
        for side in range(2):
            minor, major = (dx, dz) if side == 0 else (dz, dx)
            start = pl.ds(pl.multiple_of(minor * LATENTS, LATENTS), LATENTS)
            first = jnp.where(core == side, 0, 4)
            for at in range(8):

                @pl.when(first + major == at)
                def _():
                    picked[to, side * half : (side + 1) * half] = parts[at][start, :]

    turned[...] = picked[...].T
    share = turned.shape[0] // (SIDE * SIDE)
    for major in range(SIDE):
        for minor in range(SIDE):
            dx = jnp.where(core == 0, major, minor)
            dz = jnp.where(core == 0, minor, major)
            owner = ((x + dx) % SIDE) * SIDE + (z + dz) % SIDE
            to = (major * SIDE + minor) * share
            picked_t[to : to + share, :] = turned[pl.ds(pl.multiple_of(owner * share, 16), share), :]


def backward(numbers, picked, picked_t, gate_tanh, key_weight, value_weight, queries, upstream, query_grad, scratch, groups, named):
    keys, values, key_sum, value_sum, key_part, value_part = scratch
    lengths_at = numbers_at(groups, named, SIDE * SIDE)[1]
    group_keys = named * LATENTS
    group_len = queries.shape[0] // groups
    scale = HEAD_DIM**-0.5
    sharpness = scale * math.log2(math.e)
    keys[...] = jnp.dot(picked[...], key_weight[...], preferred_element_type=F32).astype(BF16)
    values[...] = jnp.dot(picked[...], value_weight[...], preferred_element_type=F32).astype(BF16)
    heads = [slice(head * HEAD_DIM, (head + 1) * HEAD_DIM) for head in range(HEADS)]

    for group in range(groups):
        rows = slice(group * group_keys, (group + 1) * group_keys)
        length = numbers[lengths_at + group]
        blocks = (length + TOKEN_BLOCK - 1) // TOKEN_BLOCK
        key_sum[...] = jnp.zeros_like(key_sum)
        value_sum[...] = jnp.zeros_like(value_sum)

        def block(step, carry):
            at = pl.multiple_of(step * TOKEN_BLOCK, TOKEN_BLOCK)
            tokens = pl.ds(group * group_len + at, TOKEN_BLOCK)
            live = lax.broadcasted_iota(jnp.int32, (TOKEN_BLOCK, HEAD_DIM), 0) + at < length
            made = []
            for cols in heads:
                q = queries[tokens, cols]
                gated = gate_tanh[:, cols] * upstream[tokens, cols].astype(F32)
                dout = jnp.where(live, gated, 0.0).astype(BF16)
                scores = lax.dot_general(keys[rows, cols], q, ONES, preferred_element_type=F32)
                dprob = lax.dot_general(values[rows, cols], dout, ONES, preferred_element_type=F32)
                made.append((cols, q, dout, scores, dprob))
            for cols, q, dout, scores, dprob in made:
                top = jnp.max(scores, axis=0, keepdims=True)
                powers = jnp.exp2((scores - top) * sharpness)
                probs = powers * (1.0 / jnp.sum(powers, axis=0, keepdims=True))
                delta = jnp.sum(probs * dprob, axis=0, keepdims=True)
                dscore = (probs * (dprob - delta)).astype(BF16)
                key_sum[:, cols] += jnp.dot(dscore, q, preferred_element_type=F32)
                value_sum[:, cols] += jnp.dot(probs.astype(BF16), dout, preferred_element_type=F32)
                grad = lax.dot_general(dscore, keys[rows, cols], ZEROS, preferred_element_type=F32)
                query_grad[tokens, cols] = (grad * scale).astype(BF16)
            return carry

        lax.fori_loop(0, blocks, block, 0)

        def blank(step, carry):
            tokens = pl.ds(group * group_len + pl.multiple_of(step * TOKEN_BLOCK, TOKEN_BLOCK), TOKEN_BLOCK)
            query_grad[tokens, :] = jnp.zeros((TOKEN_BLOCK, PAIR), BF16)
            return carry

        lax.fori_loop(blocks, group_len // TOKEN_BLOCK, blank, 0)
        key_part[rows, :] = (key_sum[...] * scale).astype(BF16)
        value_part[rows, :] = value_sum[...].astype(BF16)

    quarter = picked_t.shape[0] // SIDE
    for major in range(SIDE):
        rows = slice(major * quarter, (major + 1) * quarter)
        for part in (key_part, value_part):
            product = jnp.dot(picked_t[rows, :], part[...], preferred_element_type=F32)
            yield major, part is value_part, product.astype(BF16)


def first_kernel(groups, named, numbers, *refs):
    parts, (gate_tanh, key_weight, value_weight, queries, upstream) = refs[:8], refs[8:13]
    query_grad, messages, (picked, picked_t), turned, scratch = refs[13], refs[14:18], refs[18:20], refs[20], refs[21:]

    @pl.when(pl.program_id(0) == 0)
    def _():
        pick(numbers, parts, picked, turned, picked_t, groups, named)

    share = picked.shape[1] // (SIDE * SIDE)
    for major, second, product in backward(
        numbers, picked, picked_t, gate_tanh, key_weight, value_weight, queries, upstream, query_grad, scratch, groups, named
    ):
        for minor in range(SIDE):
            to = (2 * minor + second) * share
            messages[major][to : to + share, :] = product[minor * share : (minor + 1) * share]


def second_kernel(groups, named, numbers, *refs):
    picked, picked_t, gate_tanh, key_weight, value_weight, queries, upstream = refs[:7]
    query_grad, messages, scratch = refs[8], refs[9:17], refs[17:]
    for major, second, product in backward(
        numbers, picked, picked_t, gate_tanh, key_weight, value_weight, queries, upstream, query_grad, scratch, groups, named
    ):
        messages[second * SIDE + major][...] = product


def attention(numbers, latents, gate_tanh, key_weight, value_weight, queries, upstream, query_grad, groups, named):
    first = query_grad is None
    tokens, width = queries.shape
    vision = key_weight.shape[0]
    steps = width // PAIR // 2
    offset = 0 if first else steps
    picked_rows = groups * named * LATENTS
    group_keys = named * LATENTS
    quarter = vision // SIDE
    whole = lambda shape: pl.BlockSpec(shape, lambda step, *_: (0, 0))
    columns = lambda rows: pl.BlockSpec((rows, PAIR), lambda step, *_: (0, step + offset))
    message = lambda rows: pl.BlockSpec((rows, PAIR), lambda step, *_: (0, step))
    shape = jax.ShapeDtypeStruct
    in_specs = [whole(part.shape) for part in latents]
    in_specs += [columns(1), columns(vision), columns(vision), columns(tokens), columns(tokens)]
    inputs = [numbers, *latents, gate_tanh, key_weight, value_weight, queries, upstream]
    out_specs, out_shape = [columns(tokens)], [shape((tokens, width), BF16)]
    scratch = [
        pltpu.VMEM((picked_rows, PAIR), BF16),
        pltpu.VMEM((picked_rows, PAIR), BF16),
        pltpu.VMEM((group_keys, PAIR), F32),
        pltpu.VMEM((group_keys, PAIR), F32),
        pltpu.VMEM((picked_rows, PAIR), BF16),
        pltpu.VMEM((picked_rows, PAIR), BF16),
    ]
    if first:
        out_specs += [message(2 * quarter)] * SIDE + [whole((picked_rows, vision)), whole((vision, picked_rows))]
        out_shape += [shape((2 * quarter, width // 2), BF16)] * SIDE
        out_shape += [shape((picked_rows, vision), BF16), shape((vision, picked_rows), BF16)]
        scratch = [pltpu.VMEM((vision, picked_rows), BF16)] + scratch
        aliases = {}
    else:
        in_specs.append(pl.BlockSpec(memory_space=pl.ANY))
        inputs.append(query_grad)
        out_specs += [message(quarter)] * (2 * SIDE)
        out_shape += [shape((quarter, width // 2), BF16)] * (2 * SIDE)
        aliases = {len(inputs) - 1: 0}
    return pl.pallas_call(
        functools.partial(first_kernel if first else second_kernel, groups, named),
        grid_spec=pltpu.PrefetchScalarGridSpec(
            num_scalar_prefetch=1, grid=(steps,), in_specs=in_specs, out_specs=out_specs, scratch_shapes=scratch
        ),
        out_shape=out_shape,
        input_output_aliases=aliases,
        compiler_params=pltpu.CompilerParams(vmem_limit_bytes=40 * 1024 * 1024),
        cost_estimate=pl.CostEstimate(flops=10**10, bytes_accessed=10**7, transcendentals=0),
    )(*inputs)


def add(*arrays):
    return functools.reduce(jnp.add, [array.astype(F32) for array in arrays])


def last_sum(shares, mp):
    came = [shift(shares[at].astype(BF16), 0, at, mp) for at in (2, 1, 3)]
    total = add(shares[0], *came)
    rows = total.shape[0] // 2
    return total[:rows], total[rows:]


def local(latents, key_weight, value_weight, queries, upstream, gate, media, frame_slot, lengths, *, mp):
    groups, named = media.shape
    place = jnp.stack([lax.axis_index("seq"), lax.axis_index("mp") % 2]).astype(jnp.int32)
    aside = (jnp.concatenate([media.reshape(-1), frame_slot, lengths, place]), jnp.tanh(gate)[None, :])
    parts, (numbers, gate_tanh) = gather_latents(latents, aside, mp)
    rest = (gate_tanh, key_weight, value_weight, queries, upstream)
    query_grad, *joined, picked, picked_t = attention(numbers, parts, *rest, None, groups, named)
    came = [shift(joined[at], at, 0, mp) for at in (2, 1, 3)]

    query_grad, *messages = attention(numbers, (picked, picked_t), *rest, query_grad, groups, named)
    rows, messages = lax.optimization_barrier((add(joined[0], *came), messages))
    key, value = messages[:SIDE], messages[SIDE:]
    key_far = shift(key[2], 1, 0, mp)
    value_far = shift(value[2], 3, 0, mp)
    value_near = shift(value[1], 1, 0, mp)
    key_near = shift(key[3], 3, 0, mp)

    share = rows.shape[0] // SIDE
    first = last_sum([rows[at * share : (at + 1) * share] for at in range(SIDE)], mp)

    key_on = shift(add(key[1], key_far).astype(BF16), 1, 0, mp)
    value_on = shift(add(value[3], value_far).astype(BF16), 3, 0, mp)
    key_rows = add(key[0], key_near, key_on)
    value_rows = add(value[0], value_near, value_on)
    share //= 2
    cut = lambda array, at: array[at * share : (at + 1) * share]
    second = last_sum([jnp.concatenate([cut(key_rows, at), cut(value_rows, at)], axis=0) for at in range(SIDE)], mp)
    key_grad, value_grad = [jnp.concatenate(halves, axis=1) for halves in zip(first, second)]
    return query_grad, key_grad, value_grad


def solution(mesh):
    in_specs = (
        P("seq", None),
        P(None, "mp"),
        P(None, "mp"),
        P("seq", "mp"),
        P("seq", "mp"),
        P("mp"),
        P("seq", None),
        P(),
        P("seq"),
    )
    out_specs = (P("seq", "mp"), P("seq", "mp"), P("seq", "mp"))
    body = functools.partial(local, mp=mesh.shape["mp"])
    return jax.shard_map(body, mesh=mesh, in_specs=in_specs, out_specs=out_specs, check_vma=False)
```

time: 118 us -> 103 us (0.87)
  waiting for transfers between devices: 46.8 us -> 23.9 us
  Pallas kernels: 24.6 us -> 28.5 us
  local copies, waits for them, and re-layouts: 3.67 us -> 5.82 us
    ppermute x15 -> x21, waiting for transfers between devices: 45.3 us -> 22.4 us  [shift(): return lax.ppermute(array, ('seq', 'mp'), pairs)]
    pallas_call x1 -> x2, Pallas kernels: 24.6 us -> 28.5 us  [attention(): pl.pallas_call(functools.partial(first_kernel if first else second_kernel...]
    concatenate x3 -> x5, other arithmetic: 0.07 us -> 1.53 us  [the longest x2 1.5 us: local(): jnp.concatenate(halves, axis=1)]
    unnamed x12 -> x8, local copies, waits for them, and re-layouts: 2.68 us -> 3.49 us
    ppermute x15 -> x21, starting transfers between devices: 38 us -> 37.7 us  [shift(): return lax.ppermute(array, ('seq', 'mp'), pairs)]
  transfers between devices with their start and end apart: 19 -> 25, of which waited for: 14 -> 14; matrix products, arithmetic and copies ran while one was open for 1% -> 3% of each run, Pallas kernels for 0% -> 13%
where the time goes in v1:
time: 103 us; the launch traced here: 101 us
  starting transfers between devices  38.3 us (37%)
  Pallas kernels  28.5 us (28%)
  waiting for transfers between devices  23.9 us (23%)
  local copies, waits for them, and re-layouts  5.82 us (6%)
  other arithmetic  3.53 us (3%)
    ppermute x21, starting transfers between devices, shift(): return lax.ppermute(array, ('seq', 'mp'), pairs)  37.7 us
    pallas_call x2, Pallas kernels, attention(): pl.pallas_call(functools.partial(first_kernel if first else second_kernel...  28.5 us
    ppermute x21, waiting for transfers between devices, shift(): return lax.ppermute(array, ('seq', 'mp'), pairs)  22.4 us
    unnamed x8, local copies, waits for them, and re-layouts  3.49 us
  transfers between devices with their start and end apart: 25, of which 14 were waited for; matrix products, arithmetic and copies ran while one was open for 3% of the time, Pallas kernels for 13%

profile of v1, /device:TPU:0, one launch (start us, length us, event | category | flops | bytes accessed | tf_op | source)
XLA Modules:
  0.0 100.9 jit_solution(10856888353404384865)
XLA Ops:
  1.6 1.6 %collective-permute-start = (bf16[64,640]{1,0:T(8,128)(2,1)S(1)}, bf16[64,640]{1,0:T(8,128)(2,1)S(1)}, u32[]{:S(2)}, u32[]{:S(2)}) collective-permute-start(bf16[64,640]{1,0:T(8,128)(2,1)S(1)} %slice_select_fusion), channel_id=1, source_target_pairs={{0,32},{1,9},{2,34},{3,11},{4,36},{5,13},{6,38},{7,15},{8,40},{9,1... | collective-permute-start | bytes 245768 | tf_op jit(solution)/shard_map/ppermute | solution.py:31
  3.2 2.7 %collective-permute-start.1 = (bf16[64,640]{1,0:T(8,128)(2,1)S(1)}, bf16[64,640]{1,0:T(8,128)(2,1)S(1)}, u32[]{:S(2)}, u32[]{:S(2)}) collective-permute-start(bf16[64,640]{1,0:T(8,128)(2,1)S(1)} %slice_select_fusion), channel_id=1, source_target_pairs={{0,64},{1,17},{2,66},{3,19},{4,68},{5,21},{6,70},{7,23},{8,72},{9,... | collective-permute-start | bytes 245768 | tf_op jit(solution)/shard_map/ppermute | solution.py:31
  6.0 1.4 %collective-permute-start.2 = (bf16[64,640]{1,0:T(8,128)(2,1)S(1)}, bf16[64,640]{1,0:T(8,128)(2,1)S(1)}, u32[]{:S(2)}, u32[]{:S(2)}) collective-permute-start(bf16[64,640]{1,0:T(8,128)(2,1)S(1)} %slice_select_fusion), channel_id=1, source_target_pairs={{0,96},{1,25},{2,98},{3,27},{4,100},{5,29},{6,102},{7,31},{8,104},... | collective-permute-start | bytes 245768 | tf_op jit(solution)/shard_map/ppermute | solution.py:31
  7.4 1.9 %collective-permute-done.1 = bf16[64,640]{1,0:T(8,128)(2,1)S(1)} collective-permute-done((bf16[64,640]{1,0:T(8,128)(2,1)S(1)}, bf16[64,640]{1,0:T(8,128)(2,1)S(1)}, u32[]{:S(2)}, u32[]{:S(2)}) %collective-permute-start.1) | collective-permute-done | bytes 81952 | tf_op jit(solution)/shard_map/ppermute | solution.py:31
  10.4 2.0 %collective-permute-start.3 = (bf16[256,640]{1,0:T(8,128)(2,1)S(1)}, bf16[256,640]{1,0:T(8,128)(2,1)S(1)}, u32[]{:S(2)}, u32[]{:S(2)}) collective-permute-start(bf16[256,640]{1,0:T(8,128)(2,1)S(1)} %pad_maximum_fusion.refs_0_), channel_id=1, source_target_pairs={{0,8},{1,33},{2,10},{3,35},{4,12},{5,37},{6,14},{7,39},{8,16},{9,4... | collective-permute-start | bytes 983048 | tf_op jit(solution)/shard_map/ppermute | solution.py:31
  12.4 3.6 %collective-permute-start.4 = (bf16[256,640]{1,0:T(8,128)(2,1)S(1)}, bf16[256,640]{1,0:T(8,128)(2,1)S(1)}, u32[]{:S(2)}, u32[]{:S(2)}) collective-permute-start(bf16[256,640]{1,0:T(8,128)(2,1)S(1)} %pad_maximum_fusion.refs_0_), channel_id=1, source_target_pairs={{0,16},{1,65},{2,18},{3,67},{4,20},{5,69},{6,22},{7,71},{8,24},{9,... | collective-permute-start | bytes 983048 | tf_op jit(solution)/shard_map/ppermute | solution.py:31
  19.7 4.8 %collective-permute-done.4.refs_2_ = bf16[256,640]{1,0:T(8,128)(2,1)S(1)} collective-permute-done((bf16[256,640]{1,0:T(8,128)(2,1)S(1)}, bf16[256,640]{1,0:T(8,128)(2,1)S(1)}, u32[]{:S(2)}, u32[]{:S(2)}) %collective-permute-start.4) | collective-permute-done | bytes 327712 | tf_op jit(solution)/shard_map/ppermute | solution.py:31
  26.7 1.7 %copy-done = bf16[1280,1024]{1,0:T(8,128)(2,1)S(1)} copy-done((bf16[1280,1024]{1,0:T(8,128)(2,1)S(1)}, bf16[1280,1024]{1,0:T(8,128)(2,1)}, u32[]{:S(2)}) %copy-start) | copy-done | bytes 2621464
  28.4 1.7 %copy-done.2 = bf16[1280,1024]{1,0:T(8,128)(2,1)S(1)} copy-done((bf16[1280,1024]{1,0:T(8,128)(2,1)S(1)}, bf16[1280,1024]{1,0:T(8,128)(2,1)}, u32[]{:S(2)}) %copy-start.2) | copy-done | bytes 2621464
  30.1 15.5 %shard_map.112 = (bf16[2048,1024]{1,0:T(8,128)(2,1)}, bf16[640,512]{1,0:T(8,128)(2,1)S(1)}, bf16[640,512]{1,0:T(8,128)(2,1)S(1)}, bf16[640,512]{1,0:T(8,128)(2,1...) custom-call(s32[28]{0:T(128)S(1)} %concatenate.28.numbers, ...), custom_call_target="tpu_custom_call" | custom-call | flops 10000000000 | bytes 10000000 | tf_op jit(solution)/shard_map/pallas_call | solution.py:212
  45.7 1.8 %collective-permute-start.10 = (bf16[640,512]{1,0:T(8,128)(2,1)S(1)}, bf16[640,512]{1,0:T(8,128)(2,1)S(1)}, u32[]{:S(2)}, u32[]{:S(2)}) collective-permute-start(bf16[640,512]{1,0:T(8,128)(2,1)S(1)} %get-tuple-element.39), channel_id=1, source_target_pairs={{0,64},{1,17},{2,66},{3,19},{4,68},{5,21},{6,70},{7,23},{8,72},{9,... | collective-permute-start | bytes 1966088 | tf_op jit(solution)/shard_map/ppermute | solution.py:31
  47.4 1.8 %collective-permute-start.11 = (bf16[640,512]{1,0:T(8,128)(2,1)S(1)}, bf16[640,512]{1,0:T(8,128)(2,1)S(1)}, u32[]{:S(2)}, u32[]{:S(2)}) collective-permute-start(bf16[640,512]{1,0:T(8,128)(2,1)S(1)} %get-tuple-element.40), channel_id=1, source_target_pairs={{0,32},{1,9},{2,34},{3,11},{4,36},{5,13},{6,38},{7,15},{8,40},{9,1... | collective-permute-start | bytes 1966088 | tf_op jit(solution)/shard_map/ppermute | solution.py:31
  49.2 1.5 %collective-permute-start.12 = (bf16[640,512]{1,0:T(8,128)(2,1)S(1)}, bf16[640,512]{1,0:T(8,128)(2,1)S(1)}, u32[]{:S(2)}, u32[]{:S(2)}) collective-permute-start(bf16[640,512]{1,0:T(8,128)(2,1)S(1)} %get-tuple-element.41), channel_id=1, source_target_pairs={{0,96},{1,25},{2,98},{3,27},{4,100},{5,29},{6,102},{7,31},{8,104},... | collective-permute-start | bytes 1966088 | tf_op jit(solution)/shard_map/ppermute | solution.py:31
  50.7 12.9 %shard_map.113 = (bf16[2048,1024]{1,0:T(8,128)(2,1)}, bf16[320,512]{1,0:T(8,128)(2,1)S(1)}, bf16[320,512]{1,0:T(8,128)(2,1)S(1)}, bf16[320,512]{1,0:T(8,128)(2,1...) custom-call(s32[28]{0:T(128)S(1)} %concatenate.28.numbers, ...), custom_call_target="tpu_custom_call", output_to_operand_aliasing={{0}: (8, {})} | custom-call | flops 10000000000 | bytes 10000000 | tf_op jit(solution)/shard_map/pallas_call | solution.py:212
  66.1 2.6 %collective-permute-start.20 = (bf16[320,512]{1,0:T(8,128)(2,1)S(1)}, bf16[320,512]{1,0:T(8,128)(2,1)S(1)}, u32[]{:S(2)}, u32[]{:S(2)}) collective-permute-start(bf16[320,512]{1,0:T(8,128)(2,1)S(1)} %get-tuple-element.58), channel_id=1, source_target_pairs={{0,96},{1,25},{2,98},{3,27},{4,100},{5,29},{6,102},{7,31},{8,104},... | collective-permute-start | bytes 983048 | tf_op jit(solution)/shard_map/ppermute | solution.py:31
  68.7 3.2 %collective-permute-start.13 = (bf16[160,512]{1,0:T(8,128)(2,1)S(1)}, bf16[160,512]{1,0:T(8,128)(2,1)S(1)}, u32[]{:S(2)}, u32[]{:S(2)}) collective-permute-start(bf16[160,512]{1,0:T(8,128)(2,1)S(1)} %get-tuple-element.63), channel_id=1, source_target_pairs={{0,16},{1,65},{2,18},{3,67},{4,20},{5,69},{6,22},{7,71},{8,24},{9,... | collective-permute-start | bytes 491528 | tf_op jit(solution)/shard_map/ppermute | solution.py:31
  71.9 3.2 %collective-permute-start.15 = (bf16[160,512]{1,0:T(8,128)(2,1)S(1)}, bf16[160,512]{1,0:T(8,128)(2,1)S(1)}, u32[]{:S(2)}, u32[]{:S(2)}) collective-permute-start(bf16[160,512]{1,0:T(8,128)(2,1)S(1)} %get-tuple-element.64), channel_id=1, source_target_pairs={{0,24},{1,97},{2,26},{3,99},{4,28},{5,101},{6,30},{7,103},{8,0},{9... | collective-permute-start | bytes 491528 | tf_op jit(solution)/shard_map/ppermute | solution.py:31
  75.9 1.9 %collective-permute-start.16 = (bf16[320,512]{1,0:T(8,128)(2,1)S(1)}, bf16[320,512]{1,0:T(8,128)(2,1)S(1)}, u32[]{:S(2)}, u32[]{:S(2)}) collective-permute-start(bf16[320,512]{1,0:T(8,128)(2,1)S(1)} %get-tuple-element.52), channel_id=1, source_target_pairs={{0,96},{1,25},{2,98},{3,27},{4,100},{5,29},{6,102},{7,31},{8,104},... | collective-permute-start | bytes 983048 | tf_op jit(solution)/shard_map/ppermute | solution.py:31
  79.9 1.6 %collective-permute-start.21 = (bf16[320,512]{1,0:T(8,128)(2,1)S(1)}, bf16[320,512]{1,0:T(8,128)(2,1)S(1)}, u32[]{:S(2)}, u32[]{:S(2)}) collective-permute-start(bf16[320,512]{1,0:T(8,128)(2,1)S(1)} %add_convert_fusion), channel_id=1, source_target_pairs={{0,96},{1,25},{2,98},{3,27},{4,100},{5,29},{6,102},{7,31},{8,104},... | collective-permute-start | bytes 983048 | tf_op jit(solution)/shard_map/ppermute | solution.py:31
  82.9 3.3 %collective-permute-done.18 = bf16[320,512]{1,0:T(8,128)(2,1)S(1)} collective-permute-done((bf16[320,512]{1,0:T(8,128)(2,1)S(1)}, bf16[320,512]{1,0:T(8,128)(2,1)S(1)}, u32[]{:S(2)}, u32[]{:S(2)}) %collective-permute-start.18) | collective-permute-done | bytes 327712 | tf_op jit(solution)/shard_map/ppermute | solution.py:31
  86.4 3.4 %collective-permute-done.19 = bf16[320,512]{1,0:T(8,128)(2,1)S(1)} collective-permute-done((bf16[320,512]{1,0:T(8,128)(2,1)S(1)}, bf16[320,512]{1,0:T(8,128)(2,1)S(1)}, u32[]{:S(2)}, u32[]{:S(2)}) %collective-permute-start.19) | collective-permute-done | bytes 327712 | tf_op jit(solution)/shard_map/ppermute | solution.py:31
  90.0 2.7 %collective-permute-start.22 = (bf16[160,512]{1,0:T(8,128)(2,1)S(1)}, bf16[160,512]{1,0:T(8,128)(2,1)S(1)}, u32[]{:S(2)}, u32[]{:S(2)}) collective-permute-start(bf16[160,512]{1,0:T(8,128)(2,1)S(1)} %pad_maximum_fusion.3), channel_id=1, source_target_pairs={{0,16},{1,65},{2,18},{3,67},{4,20},{5,69},{6,22},{7,71},{8,24},{9,... | collective-permute-start | bytes 491528 | tf_op jit(solution)/shard_map/ppermute | solution.py:31
  92.8 3.3 %collective-permute-start.24 = (bf16[160,512]{1,0:T(8,128)(2,1)S(1)}, bf16[160,512]{1,0:T(8,128)(2,1)S(1)}, u32[]{:S(2)}, u32[]{:S(2)}) collective-permute-start(bf16[160,512]{1,0:T(8,128)(2,1)S(1)} %pad_maximum_fusion.5), channel_id=1, source_target_pairs={{0,24},{1,97},{2,26},{3,99},{4,28},{5,101},{6,30},{7,103},{8,0},{9... | collective-permute-start | bytes 491528 | tf_op jit(solution)/shard_map/ppermute | solution.py:31
  96.9 2.4 %collective-permute-done.23 = bf16[160,512]{1,0:T(8,128)(2,1)S(1)} collective-permute-done((bf16[160,512]{1,0:T(8,128)(2,1)S(1)}, bf16[160,512]{1,0:T(8,128)(2,1)S(1)}, u32[]{:S(2)}, u32[]{:S(2)}) %collective-permute-start.23) | collective-permute-done | bytes 163872 | tf_op jit(solution)/shard_map/ppermute | solution.py:31
  (60 shorter events, 17.4 us)
Async XLA Ops:
  1.6 5.8 %collective-permute-start = (bf16[64,640]{1,0:T(8,128)(2,1)S(1)}, bf16[64,640]{1,0:T(8,128)(2,1)S(1)}, u32[]{:S(2)}, u32[]{:S(2)}) collective-permute-start(bf16[64,640]{1,0:T(8,128)(2,1)S(1)} %slice_select_fusion), channel_id=1, source_target_pairs={{0,32},{1,9},{2,34},{3,11},{4,36},{5,13},{6,38},{7,15},{8,40},{9,1... | collective-permute-start | bytes 245768 | tf_op jit(solution)/shard_map/ppermute | solution.py:31
  3.2 6.0 %collective-permute-start.1 = (bf16[64,640]{1,0:T(8,128)(2,1)S(1)}, bf16[64,640]{1,0:T(8,128)(2,1)S(1)}, u32[]{:S(2)}, u32[]{:S(2)}) collective-permute-start(bf16[64,640]{1,0:T(8,128)(2,1)S(1)} %slice_select_fusion), channel_id=1, source_target_pairs={{0,64},{1,17},{2,66},{3,19},{4,68},{5,21},{6,70},{7,23},{8,72},{9,... | collective-permute-start | bytes 245768 | tf_op jit(solution)/shard_map/ppermute | solution.py:31
  6.0 4.4 %collective-permute-start.2 = (bf16[64,640]{1,0:T(8,128)(2,1)S(1)}, bf16[64,640]{1,0:T(8,128)(2,1)S(1)}, u32[]{:S(2)}, u32[]{:S(2)}) collective-permute-start(bf16[64,640]{1,0:T(8,128)(2,1)S(1)} %slice_select_fusion), channel_id=1, source_target_pairs={{0,96},{1,25},{2,98},{3,27},{4,100},{5,29},{6,102},{7,31},{8,104},... | collective-permute-start | bytes 245768 | tf_op jit(solution)/shard_map/ppermute | solution.py:31
  10.4 9.2 %collective-permute-start.3 = (bf16[256,640]{1,0:T(8,128)(2,1)S(1)}, bf16[256,640]{1,0:T(8,128)(2,1)S(1)}, u32[]{:S(2)}, u32[]{:S(2)}) collective-permute-start(bf16[256,640]{1,0:T(8,128)(2,1)S(1)} %pad_maximum_fusion.refs_0_), channel_id=1, source_target_pairs={{0,8},{1,33},{2,10},{3,35},{4,12},{5,37},{6,14},{7,39},{8,16},{9,4... | collective-permute-start | bytes 983048 | tf_op jit(solution)/shard_map/ppermute | solution.py:31
  12.4 12.1 %collective-permute-start.4 = (bf16[256,640]{1,0:T(8,128)(2,1)S(1)}, bf16[256,640]{1,0:T(8,128)(2,1)S(1)}, u32[]{:S(2)}, u32[]{:S(2)}) collective-permute-start(bf16[256,640]{1,0:T(8,128)(2,1)S(1)} %pad_maximum_fusion.refs_0_), channel_id=1, source_target_pairs={{0,16},{1,65},{2,18},{3,67},{4,20},{5,69},{6,22},{7,71},{8,24},{9,... | collective-permute-start | bytes 983048 | tf_op jit(solution)/shard_map/ppermute | solution.py:31
  16.0 8.6 %collective-permute-start.5 = (bf16[256,640]{1,0:T(8,128)(2,1)S(1)}, bf16[256,640]{1,0:T(8,128)(2,1)S(1)}, u32[]{:S(2)}, u32[]{:S(2)}) collective-permute-start(bf16[256,640]{1,0:T(8,128)(2,1)S(1)} %pad_maximum_fusion.refs_0_), channel_id=1, source_target_pairs={{0,24},{1,97},{2,26},{3,99},{4,28},{5,101},{6,30},{7,103},{8,0},{9... | collective-permute-start | bytes 983048 | tf_op jit(solution)/shard_map/ppermute | solution.py:31
  19.2 5.9 %collective-permute-start.6 = (bf16[256,640]{1,0:T(8,128)(2,1)S(1)}, bf16[256,640]{1,0:T(8,128)(2,1)S(1)}, u32[]{:S(2)}, u32[]{:S(2)}) collective-permute-start(bf16[256,640]{1,0:T(8,128)(2,1)S(1)} %pad_maximum_fusion.refs_0_), channel_id=1, source_target_pairs={{0,1},{1,0},{2,3},{3,2},{4,5},{5,4},{6,7},{7,6},{8,9},{9,8},{10,11... | collective-permute-start | bytes 983048 | tf_op jit(solution)/shard_map/ppermute | solution.py:35
  19.6 5.5 %collective-permute-start.7 = (bf16[256,640]{1,0:T(8,128)(2,1)S(1)}, bf16[256,640]{1,0:T(8,128)(2,1)S(1)}, u32[]{:S(2)}, u32[]{:S(2)}) collective-permute-start(bf16[256,640]{1,0:T(8,128)(2,1)S(1)} %collective-permute-done.3.refs_1_), channel_id=1, source_target_pairs={{0,1},{1,0},{2,3},{3,2},{4,5},{5,4},{6,7},{7,6},{8,9},{9,8},{10,11... | collective-permute-start | bytes 983048 | tf_op jit(solution)/shard_map/ppermute | solution.py:35
  24.6 2.1 %collective-permute-start.9 = (bf16[256,640]{1,0:T(8,128)(2,1)S(1)}, bf16[256,640]{1,0:T(8,128)(2,1)S(1)}, u32[]{:S(2)}, u32[]{:S(2)}) collective-permute-start(bf16[256,640]{1,0:T(8,128)(2,1)S(1)} %collective-permute-done.5.refs_3_), channel_id=1, source_target_pairs={{0,1},{1,0},{2,3},{3,2},{4,5},{5,4},{6,7},{7,6},{8,9},{9,8},{10,11... | collective-permute-start | bytes 983048 | tf_op jit(solution)/shard_map/ppermute | solution.py:35
  45.7 17.9 %collective-permute-start.10 = (bf16[640,512]{1,0:T(8,128)(2,1)S(1)}, bf16[640,512]{1,0:T(8,128)(2,1)S(1)}, u32[]{:S(2)}, u32[]{:S(2)}) collective-permute-start(bf16[640,512]{1,0:T(8,128)(2,1)S(1)} %get-tuple-element.39), channel_id=1, source_target_pairs={{0,64},{1,17},{2,66},{3,19},{4,68},{5,21},{6,70},{7,23},{8,72},{9,... | collective-permute-start | bytes 1966088 | tf_op jit(solution)/shard_map/ppermute | solution.py:31
  47.4 17.4 %collective-permute-start.11 = (bf16[640,512]{1,0:T(8,128)(2,1)S(1)}, bf16[640,512]{1,0:T(8,128)(2,1)S(1)}, u32[]{:S(2)}, u32[]{:S(2)}) collective-permute-start(bf16[640,512]{1,0:T(8,128)(2,1)S(1)} %get-tuple-element.40), channel_id=1, source_target_pairs={{0,32},{1,9},{2,34},{3,11},{4,36},{5,13},{6,38},{7,15},{8,40},{9,1... | collective-permute-start | bytes 1966088 | tf_op jit(solution)/shard_map/ppermute | solution.py:31
  49.2 15.6 %collective-permute-start.12 = (bf16[640,512]{1,0:T(8,128)(2,1)S(1)}, bf16[640,512]{1,0:T(8,128)(2,1)S(1)}, u32[]{:S(2)}, u32[]{:S(2)}) collective-permute-start(bf16[640,512]{1,0:T(8,128)(2,1)S(1)} %get-tuple-element.41), channel_id=1, source_target_pairs={{0,96},{1,25},{2,98},{3,27},{4,100},{5,29},{6,102},{7,31},{8,104},... | collective-permute-start | bytes 1966088 | tf_op jit(solution)/shard_map/ppermute | solution.py:31
  65.2 10.7 %collective-permute-start.17 = (bf16[320,512]{1,0:T(8,128)(2,1)S(1)}, bf16[320,512]{1,0:T(8,128)(2,1)S(1)}, u32[]{:S(2)}, u32[]{:S(2)}) collective-permute-start(bf16[320,512]{1,0:T(8,128)(2,1)S(1)} %get-tuple-element.54), channel_id=1, source_target_pairs={{0,32},{1,9},{2,34},{3,11},{4,36},{5,13},{6,38},{7,15},{8,40},{9,1... | collective-permute-start | bytes 983048 | tf_op jit(solution)/shard_map/ppermute | solution.py:31
  66.1 11.8 %collective-permute-start.20 = (bf16[320,512]{1,0:T(8,128)(2,1)S(1)}, bf16[320,512]{1,0:T(8,128)(2,1)S(1)}, u32[]{:S(2)}, u32[]{:S(2)}) collective-permute-start(bf16[320,512]{1,0:T(8,128)(2,1)S(1)} %get-tuple-element.58), channel_id=1, source_target_pairs={{0,96},{1,25},{2,98},{3,27},{4,100},{5,29},{6,102},{7,31},{8,104},... | collective-permute-start | bytes 983048 | tf_op jit(solution)/shard_map/ppermute | solution.py:31
  68.7 9.5 %collective-permute-start.13 = (bf16[160,512]{1,0:T(8,128)(2,1)S(1)}, bf16[160,512]{1,0:T(8,128)(2,1)S(1)}, u32[]{:S(2)}, u32[]{:S(2)}) collective-permute-start(bf16[160,512]{1,0:T(8,128)(2,1)S(1)} %get-tuple-element.63), channel_id=1, source_target_pairs={{0,16},{1,65},{2,18},{3,67},{4,20},{5,69},{6,22},{7,71},{8,24},{9,... | collective-permute-start | bytes 491528 | tf_op jit(solution)/shard_map/ppermute | solution.py:31
  71.9 8.0 %collective-permute-start.14 = (bf16[160,512]{1,0:T(8,128)(2,1)S(1)}, bf16[160,512]{1,0:T(8,128)(2,1)S(1)}, u32[]{:S(2)}, u32[]{:S(2)}) collective-permute-start(bf16[160,512]{1,0:T(8,128)(2,1)S(1)} %get-tuple-element.65), channel_id=1, source_target_pairs={{0,8},{1,33},{2,10},{3,35},{4,12},{5,37},{6,14},{7,39},{8,16},{9,4... | collective-permute-start | bytes 491528 | tf_op jit(solution)/shard_map/ppermute | solution.py:31
  71.9 9.6 %collective-permute-start.15 = (bf16[160,512]{1,0:T(8,128)(2,1)S(1)}, bf16[160,512]{1,0:T(8,128)(2,1)S(1)}, u32[]{:S(2)}, u32[]{:S(2)}) collective-permute-start(bf16[160,512]{1,0:T(8,128)(2,1)S(1)} %get-tuple-element.64), channel_id=1, source_target_pairs={{0,24},{1,97},{2,26},{3,99},{4,28},{5,101},{6,30},{7,103},{8,0},{9... | collective-permute-start | bytes 491528 | tf_op jit(solution)/shard_map/ppermute | solution.py:31
  75.9 7.1 %collective-permute-start.16 = (bf16[320,512]{1,0:T(8,128)(2,1)S(1)}, bf16[320,512]{1,0:T(8,128)(2,1)S(1)}, u32[]{:S(2)}, u32[]{:S(2)}) collective-permute-start(bf16[320,512]{1,0:T(8,128)(2,1)S(1)} %get-tuple-element.52), channel_id=1, source_target_pairs={{0,96},{1,25},{2,98},{3,27},{4,100},{5,29},{6,102},{7,31},{8,104},... | collective-permute-start | bytes 983048 | tf_op jit(solution)/shard_map/ppermute | solution.py:31
  77.9 8.4 %collective-permute-start.18 = (bf16[320,512]{1,0:T(8,128)(2,1)S(1)}, bf16[320,512]{1,0:T(8,128)(2,1)S(1)}, u32[]{:S(2)}, u32[]{:S(2)}) collective-permute-start(bf16[320,512]{1,0:T(8,128)(2,1)S(1)} %add_convert_fusion.1), channel_id=1, source_target_pairs={{0,32},{1,9},{2,34},{3,11},{4,36},{5,13},{6,38},{7,15},{8,40},{9,1... | collective-permute-start | bytes 983048 | tf_op jit(solution)/shard_map/ppermute | solution.py:31
  78.2 11.6 %collective-permute-start.19 = (bf16[320,512]{1,0:T(8,128)(2,1)S(1)}, bf16[320,512]{1,0:T(8,128)(2,1)S(1)}, u32[]{:S(2)}, u32[]{:S(2)}) collective-permute-start(bf16[320,512]{1,0:T(8,128)(2,1)S(1)} %get-tuple-element.56), channel_id=1, source_target_pairs={{0,32},{1,9},{2,34},{3,11},{4,36},{5,13},{6,38},{7,15},{8,40},{9,1... | collective-permute-start | bytes 983048 | tf_op jit(solution)/shard_map/ppermute | solution.py:31
  79.9 9.9 %collective-permute-start.21 = (bf16[320,512]{1,0:T(8,128)(2,1)S(1)}, bf16[320,512]{1,0:T(8,128)(2,1)S(1)}, u32[]{:S(2)}, u32[]{:S(2)}) collective-permute-start(bf16[320,512]{1,0:T(8,128)(2,1)S(1)} %add_convert_fusion), channel_id=1, source_target_pairs={{0,96},{1,25},{2,98},{3,27},{4,100},{5,29},{6,102},{7,31},{8,104},... | collective-permute-start | bytes 983048 | tf_op jit(solution)/shard_map/ppermute | solution.py:31
  90.0 6.9 %collective-permute-start.22 = (bf16[160,512]{1,0:T(8,128)(2,1)S(1)}, bf16[160,512]{1,0:T(8,128)(2,1)S(1)}, u32[]{:S(2)}, u32[]{:S(2)}) collective-permute-start(bf16[160,512]{1,0:T(8,128)(2,1)S(1)} %pad_maximum_fusion.3), channel_id=1, source_target_pairs={{0,16},{1,65},{2,18},{3,67},{4,20},{5,69},{6,22},{7,71},{8,24},{9,... | collective-permute-start | bytes 491528 | tf_op jit(solution)/shard_map/ppermute | solution.py:31
  92.7 6.6 %collective-permute-start.23 = (bf16[160,512]{1,0:T(8,128)(2,1)S(1)}, bf16[160,512]{1,0:T(8,128)(2,1)S(1)}, u32[]{:S(2)}, u32[]{:S(2)}) collective-permute-start(bf16[160,512]{1,0:T(8,128)(2,1)S(1)} %pad_maximum_fusion.4), channel_id=1, source_target_pairs={{0,8},{1,33},{2,10},{3,35},{4,12},{5,37},{6,14},{7,39},{8,16},{9,4... | collective-permute-start | bytes 491528 | tf_op jit(solution)/shard_map/ppermute | solution.py:31
  92.8 6.5 %collective-permute-start.24 = (bf16[160,512]{1,0:T(8,128)(2,1)S(1)}, bf16[160,512]{1,0:T(8,128)(2,1)S(1)}, u32[]{:S(2)}, u32[]{:S(2)}) collective-permute-start(bf16[160,512]{1,0:T(8,128)(2,1)S(1)} %pad_maximum_fusion.5), channel_id=1, source_target_pairs={{0,24},{1,97},{2,26},{3,99},{4,28},{5,101},{6,30},{7,103},{8,0},{9... | collective-permute-start | bytes 491528 | tf_op jit(solution)/shard_map/ppermute | solution.py:31
  (5 other events, 46.2 us)

commit v2 on v1

--- a/solution.py
+++ b/solution.py
@@ -35,17 +35,18 @@
     return lax.ppermute(array, "mp", [(m, m ^ 1) for m in range(mp)])
 
 
-def gather_latents(latents, aside, mp):
+def gather_latents(latents, numbers, gate_tanh, arrays, groups, named, mp):
     half = latents.shape[1] // 2
     mine = jnp.where(lax.axis_index("mp") % 2 == 0, latents[:, :half], latents[:, half:])
     far = shift(mine, 2, 0, mp)
     near = [shift(mine, step, 0, mp) for step in (1, 3)]
     line = jnp.concatenate([mine, near[0], far, near[1]], axis=0)
+    line, numbers, gate_tanh = lax.optimization_barrier((line, numbers, gate_tanh))
     far = shift(line, 0, 2, mp)
     near = [shift(line, 0, step, mp) for step in (1, 3)]
-    line, aside = lax.optimization_barrier((line, aside))
-    fetched = [line, near[0], far, near[1]]
-    return fetched + [swap_cores(part, mp) for part in fetched], aside
+    *arrays, numbers = stage(numbers, gate_tanh, *arrays, groups, named)
+    *fetched, numbers = lax.optimization_barrier((line, near[0], far, near[1], numbers))
+    return fetched + [swap_cores(part, mp) for part in fetched], numbers, arrays
 
 
 def numbers_at(groups, named, frames):
@@ -85,7 +86,7 @@
             picked_t[to : to + share, :] = turned[pl.ds(pl.multiple_of(owner * share, 16), share), :]
 
 
-def backward(numbers, picked, picked_t, gate_tanh, key_weight, value_weight, queries, upstream, query_grad, scratch, groups, named):
+def backward(numbers, picked, picked_t, key_weight, value_weight, queries, upstream, query_grad, scratch, groups, named):
     keys, values, key_sum, value_sum, key_part, value_part = scratch
     lengths_at = numbers_at(groups, named, SIDE * SIDE)[1]
     group_keys = named * LATENTS
@@ -106,12 +107,10 @@
         def block(step, carry):
             at = pl.multiple_of(step * TOKEN_BLOCK, TOKEN_BLOCK)
             tokens = pl.ds(group * group_len + at, TOKEN_BLOCK)
-            live = lax.broadcasted_iota(jnp.int32, (TOKEN_BLOCK, HEAD_DIM), 0) + at < length
             made = []
             for cols in heads:
                 q = queries[tokens, cols]
-                gated = gate_tanh[:, cols] * upstream[tokens, cols].astype(F32)
-                dout = jnp.where(live, gated, 0.0).astype(BF16)
+                dout = upstream[tokens, cols]
                 scores = lax.dot_general(keys[rows, cols], q, ONES, preferred_element_type=F32)
                 dprob = lax.dot_general(values[rows, cols], dout, ONES, preferred_element_type=F32)
                 made.append((cols, q, dout, scores, dprob))
@@ -146,9 +145,56 @@
             yield major, part is value_part, product.astype(BF16)
 
 
+def stage_kernel(groups, named, numbers, gate_tanh, key_weight, value_weight, queries, upstream, *refs):
+    key_out, value_out, queries_out, dout, numbers_out, raw, copied, arrived = refs
+    tokens = upstream.shape[0]
+    lengths_at = numbers_at(groups, named, SIDE * SIDE)[1]
+    moves = [
+        pltpu.make_async_copy(source, target, copied.at[at])
+        for at, (source, target) in enumerate(
+            ((key_weight, key_out), (value_weight, value_out), (queries, queries_out))
+        )
+    ]
+    chunk = tokens // arrived.shape[0]
+    loads = [
+        pltpu.make_async_copy(upstream.at[pl.ds(at * chunk, chunk)], raw.at[pl.ds(at * chunk, chunk)], arrived.at[at])
+        for at in range(arrived.shape[0])
+    ]
+    for move in loads + moves:
+        move.start()
+    for at, load in enumerate(loads):
+        load.wait()
+        group, first = divmod(at * chunk, tokens // groups)
+        rows = slice(at * chunk, (at + 1) * chunk)
+        live = lax.broadcasted_iota(jnp.int32, (chunk, upstream.shape[1]), 0) + first < numbers[lengths_at + group]
+        dout[rows, :] = jnp.where(live, gate_tanh[...] * raw[rows, :].astype(F32), 0.0).astype(BF16)
+    for move in moves:
+        move.wait()
+    for at in range(numbers.shape[0]):
+        numbers_out[at] = numbers[at]
+
+
+def stage(numbers, gate_tanh, key_weight, value_weight, queries, upstream, groups, named):
+    arrays = [pltpu.with_memory_space_constraint(a, pltpu.HBM) for a in (key_weight, value_weight, queries, upstream)]
+    return pl.pallas_call(
+        functools.partial(stage_kernel, groups, named),
+        in_specs=[pl.BlockSpec(memory_space=pltpu.SMEM), pl.BlockSpec(memory_space=pltpu.VMEM)]
+        + [pl.BlockSpec(memory_space=pltpu.HBM)] * 4,
+        out_specs=[pl.BlockSpec(memory_space=pltpu.VMEM)] * 4 + [pl.BlockSpec(memory_space=pltpu.SMEM)],
+        out_shape=[pltpu.VMEM(array.shape, array.dtype) for array in arrays] + [jax.ShapeDtypeStruct(numbers.shape, numbers.dtype)],
+        scratch_shapes=[
+            pltpu.VMEM(upstream.shape, BF16),
+            pltpu.SemaphoreType.DMA((3,)),
+            pltpu.SemaphoreType.DMA((8,)),
+        ],
+        compiler_params=pltpu.CompilerParams(vmem_limit_bytes=24 * 1024 * 1024),
+        cost_estimate=pl.CostEstimate(flops=10**7, bytes_accessed=2 * 10**7, transcendentals=0),
+    )(numbers, gate_tanh, *arrays)
+
+
 def first_kernel(groups, named, numbers, *refs):
-    parts, (gate_tanh, key_weight, value_weight, queries, upstream) = refs[:8], refs[8:13]
-    query_grad, messages, (picked, picked_t), turned, scratch = refs[13], refs[14:18], refs[18:20], refs[20], refs[21:]
+    parts, (key_weight, value_weight, queries, upstream) = refs[:8], refs[8:12]
+    query_grad, messages, (picked, picked_t), turned, scratch = refs[12], refs[13:17], refs[17:19], refs[19], refs[20:]
 
     @pl.when(pl.program_id(0) == 0)
     def _():
@@ -156,7 +202,7 @@
 
     share = picked.shape[1] // (SIDE * SIDE)
     for major, second, product in backward(
-        numbers, picked, picked_t, gate_tanh, key_weight, value_weight, queries, upstream, query_grad, scratch, groups, named
+        numbers, picked, picked_t, key_weight, value_weight, queries, upstream, query_grad, scratch, groups, named
     ):
         for minor in range(SIDE):
             to = (2 * minor + second) * share
@@ -164,15 +210,15 @@
 
 
 def second_kernel(groups, named, numbers, *refs):
-    picked, picked_t, gate_tanh, key_weight, value_weight, queries, upstream = refs[:7]
-    query_grad, messages, scratch = refs[8], refs[9:17], refs[17:]
+    picked, picked_t, key_weight, value_weight, queries, upstream = refs[:6]
+    query_grad, messages, scratch = refs[7], refs[8:16], refs[16:]
     for major, second, product in backward(
-        numbers, picked, picked_t, gate_tanh, key_weight, value_weight, queries, upstream, query_grad, scratch, groups, named
+        numbers, picked, picked_t, key_weight, value_weight, queries, upstream, query_grad, scratch, groups, named
     ):
         messages[second * SIDE + major][...] = product
 
 
-def attention(numbers, latents, gate_tanh, key_weight, value_weight, queries, upstream, query_grad, groups, named):
+def attention(numbers, latents, key_weight, value_weight, queries, upstream, query_grad, groups, named):
     first = query_grad is None
     tokens, width = queries.shape
     vision = key_weight.shape[0]
@@ -181,13 +227,13 @@
     picked_rows = groups * named * LATENTS
     group_keys = named * LATENTS
     quarter = vision // SIDE
-    whole = lambda shape: pl.BlockSpec(shape, lambda step, *_: (0, 0))
+    whole = lambda shape: pl.BlockSpec(shape, lambda step, *_: (0, 0), pipeline_mode=pl.Buffered(1))
     columns = lambda rows: pl.BlockSpec((rows, PAIR), lambda step, *_: (0, step + offset))
     message = lambda rows: pl.BlockSpec((rows, PAIR), lambda step, *_: (0, step))
     shape = jax.ShapeDtypeStruct
     in_specs = [whole(part.shape) for part in latents]
-    in_specs += [columns(1), columns(vision), columns(vision), columns(tokens), columns(tokens)]
-    inputs = [numbers, *latents, gate_tanh, key_weight, value_weight, queries, upstream]
+    in_specs += [columns(vision), columns(vision), columns(tokens), columns(tokens)]
+    inputs = [numbers, *latents, key_weight, value_weight, queries, upstream]
     out_specs, out_shape = [columns(tokens)], [shape((tokens, width), BF16)]
     scratch = [
         pltpu.VMEM((picked_rows, PAIR), BF16),
@@ -216,7 +262,7 @@
         ),
         out_shape=out_shape,
         input_output_aliases=aliases,
-        compiler_params=pltpu.CompilerParams(vmem_limit_bytes=40 * 1024 * 1024),
+        compiler_params=pltpu.CompilerParams(vmem_limit_bytes=28 * 1024 * 1024),
         cost_estimate=pl.CostEstimate(flops=10**10, bytes_accessed=10**7, transcendentals=0),
     )(*inputs)
 
@@ -235,9 +281,9 @@
 def local(latents, key_weight, value_weight, queries, upstream, gate, media, frame_slot, lengths, *, mp):
     groups, named = media.shape
     place = jnp.stack([lax.axis_index("seq"), lax.axis_index("mp") % 2]).astype(jnp.int32)
-    aside = (jnp.concatenate([media.reshape(-1), frame_slot, lengths, place]), jnp.tanh(gate)[None, :])
-    parts, (numbers, gate_tanh) = gather_latents(latents, aside, mp)
-    rest = (gate_tanh, key_weight, value_weight, queries, upstream)
+    numbers = jnp.concatenate([media.reshape(-1), frame_slot, lengths, place])
+    arrays = (key_weight, value_weight, queries, upstream)
+    parts, numbers, rest = gather_latents(latents, numbers, jnp.tanh(gate)[None, :], arrays, groups, named, mp)
     query_grad, *joined, picked, picked_t = attention(numbers, parts, *rest, None, groups, named)
     came = [shift(joined[at], at, 0, mp) for at in (2, 1, 3)]
 

time: 103 us -> 99.2 us (0.963); the launches traced: 101 us -> 98.6 us
  starting transfers between devices: 38.3 us -> 44.5 us
  waiting for transfers between devices: 23.9 us -> 19.6 us
  local copies, waits for them, and re-layouts: 5.82 us -> 2.34 us
    pallas_call x2, Pallas kernels: 28.5 us -> 21.6 us  [attention(): pl.pallas_call(functools.partial(first_kernel if first else second_kernel...]
    pallas_call x0 -> x1, Pallas kernels: none -> 6.2 us  [stage(): pl.pallas_call(functools.partial(stage_kernel, groups, named), in_specs=[...]
    ppermute x21, starting transfers between devices: 37.7 us -> 43.5 us  [shift(): return lax.ppermute(array, ('seq', 'mp'), pairs)]
    ppermute x21, waiting for transfers between devices: 22.4 us -> 17.6 us  [shift(): return lax.ppermute(array, ('seq', 'mp'), pairs)]
    unnamed x8 -> x0, local copies, waits for them, and re-layouts: 3.49 us -> none
  transfers between devices with their start and end apart: 25 -> 25, of which waited for: 14 -> 12; matrix products, arithmetic and copies ran while one was open for 3% -> 3% of each run, Pallas kernels for 13% -> 16%
where the time goes in v2:
time: 99.2 us; the launch traced here: 98.6 us
  starting transfers between devices  44.5 us (45%)
  Pallas kernels  27.8 us (28%)
  waiting for transfers between devices  19.6 us (20%)
  other arithmetic  3.51 us (4%)
  local copies, waits for them, and re-layouts  2.34 us (2%)
    ppermute x21, starting transfers between devices, shift(): return lax.ppermute(array, ('seq', 'mp'), pairs)  43.5 us
    pallas_call x2, Pallas kernels, attention(): pl.pallas_call(functools.partial(first_kernel if first else second_kernel...  21.6 us
    ppermute x21, waiting for transfers between devices, shift(): return lax.ppermute(array, ('seq', 'mp'), pairs)  17.6 us
    pallas_call x1, Pallas kernels, stage(): pl.pallas_call(functools.partial(stage_kernel, groups, named), in_specs=[...  6.2 us
    ppermute x4, waiting for transfers between devices, swap_cores(): return lax.ppermute(array, 'mp', [(m, m ^ 1) for m in range(mp)])  2.01 us
  transfers between devices with their start and end apart: 25, of which 12 were waited for; matrix products, arithmetic and copies ran while one was open for 3% of the time, Pallas kernels for 16%

profile of v2, /device:TPU:0, one launch (start us, length us, event | category | flops | bytes accessed | tf_op | source)
XLA Modules:
  0.0 98.6 jit_solution(8255553653691647386)
XLA Ops:
  1.6 1.6 %collective-permute-start = (bf16[64,640]{1,0:T(8,128)(2,1)S(1)}, bf16[64,640]{1,0:T(8,128)(2,1)S(1)}, u32[]{:S(2)}, u32[]{:S(2)}) collective-permute-start(bf16[64,640]{1,0:T(8,128)(2,1)S(1)} %slice_select_fusion), channel_id=1, source_target_pairs={{0,32},{1,9},{2,34},{3,11},{4,36},{5,13},{6,38},{7,15},{8,40},{9,1... | collective-permute-start | bytes 245768 | tf_op jit(solution)/shard_map/ppermute | solution.py:31
  3.2 2.7 %collective-permute-start.1 = (bf16[64,640]{1,0:T(8,128)(2,1)S(1)}, bf16[64,640]{1,0:T(8,128)(2,1)S(1)}, u32[]{:S(2)}, u32[]{:S(2)}) collective-permute-start(bf16[64,640]{1,0:T(8,128)(2,1)S(1)} %slice_select_fusion), channel_id=1, source_target_pairs={{0,64},{1,17},{2,66},{3,19},{4,68},{5,21},{6,70},{7,23},{8,72},{9,... | collective-permute-start | bytes 245768 | tf_op jit(solution)/shard_map/ppermute | solution.py:31
  6.0 1.4 %collective-permute-start.2 = (bf16[64,640]{1,0:T(8,128)(2,1)S(1)}, bf16[64,640]{1,0:T(8,128)(2,1)S(1)}, u32[]{:S(2)}, u32[]{:S(2)}) collective-permute-start(bf16[64,640]{1,0:T(8,128)(2,1)S(1)} %slice_select_fusion), channel_id=1, source_target_pairs={{0,96},{1,25},{2,98},{3,27},{4,100},{5,29},{6,102},{7,31},{8,104},... | collective-permute-start | bytes 245768 | tf_op jit(solution)/shard_map/ppermute | solution.py:31
  10.4 2.0 %collective-permute-start.3 = (bf16[256,640]{1,0:T(8,128)(2,1)S(1)}, bf16[256,640]{1,0:T(8,128)(2,1)S(1)}, u32[]{:S(2)}, u32[]{:S(2)}) collective-permute-start(bf16[256,640]{1,0:T(8,128)(2,1)S(1)} %pad_maximum_fusion.refs_0_), channel_id=1, source_target_pairs={{0,8},{1,33},{2,10},{3,35},{4,12},{5,37},{6,14},{7,39},{8,16},{9,4... | collective-permute-start | bytes 983048 | tf_op jit(solution)/shard_map/ppermute | solution.py:31
  12.4 3.6 %collective-permute-start.4 = (bf16[256,640]{1,0:T(8,128)(2,1)S(1)}, bf16[256,640]{1,0:T(8,128)(2,1)S(1)}, u32[]{:S(2)}, u32[]{:S(2)}) collective-permute-start(bf16[256,640]{1,0:T(8,128)(2,1)S(1)} %pad_maximum_fusion.refs_0_), channel_id=1, source_target_pairs={{0,16},{1,65},{2,18},{3,67},{4,20},{5,69},{6,22},{7,71},{8,24},{9,... | collective-permute-start | bytes 983048 | tf_op jit(solution)/shard_map/ppermute | solution.py:31
  17.0 6.2 %shard_map.112 = (bf16[1280,1024]{1,0:T(8,128)(2,1)S(1)}, bf16[1280,1024]{1,0:T(8,128)(2,1)S(1)}, bf16[2048,1024]{1,0:T(8,128)(2,1)S(1)}, bf16[2048,1024]{1,0:T(8,128)(2,1)S(1)}, s32[28]{0:T(128)S(1)}) custom-call(s32[28]{0:T(128)S(1)} %concatenate.28.numbers, f32[1,1024]{1,0:T(1,128)S(1)} %bitcast.3, bf16[1280,1024]{1,0:T(8,128)(2,1)} %key_weight.1, ...), custom_call_target="tpu_custom_call" | custom-call | flops 10000000 | bytes 20000000 | tf_op jit(solution)/shard_map/pallas_call | solution.py:179
  23.2 1.3 %collective-permute-done.4.refs_2_ = bf16[256,640]{1,0:T(8,128)(2,1)S(1)} collective-permute-done((bf16[256,640]{1,0:T(8,128)(2,1)S(1)}, bf16[256,640]{1,0:T(8,128)(2,1)S(1)}, u32[]{:S(2)}, u32[]{:S(2)}) %collective-permute-start.4) | collective-permute-done | bytes 327712 | tf_op jit(solution)/shard_map/ppermute | solution.py:31
  27.6 11.7 %shard_map.113 = (bf16[2048,1024]{1,0:T(8,128)(2,1)}, bf16[640,512]{1,0:T(8,128)(2,1)S(1)}, bf16[640,512]{1,0:T(8,128)(2,1)S(1)}, bf16[640,512]{1,0:T(8,128)(2,1...) custom-call(s32[28]{0:T(128)S(1)} %get-tuple-element.45.numbers, ...), custom_call_target="tpu_custom_call" | custom-call | flops 10000000000 | bytes 10000000 | tf_op jit(solution)/shard_map/pallas_call | solution.py:258
  39.3 1.7 %collective-permute-start.10 = (bf16[640,512]{1,0:T(8,128)(2,1)S(1)}, bf16[640,512]{1,0:T(8,128)(2,1)S(1)}, u32[]{:S(2)}, u32[]{:S(2)}) collective-permute-start(bf16[640,512]{1,0:T(8,128)(2,1)S(1)} %get-tuple-element.59), channel_id=1, source_target_pairs={{0,64},{1,17},{2,66},{3,19},{4,68},{5,21},{6,70},{7,23},{8,72},{9,... | collective-permute-start | bytes 1966088 | tf_op jit(solution)/shard_map/ppermute | solution.py:31
  41.1 1.8 %collective-permute-start.11 = (bf16[640,512]{1,0:T(8,128)(2,1)S(1)}, bf16[640,512]{1,0:T(8,128)(2,1)S(1)}, u32[]{:S(2)}, u32[]{:S(2)}) collective-permute-start(bf16[640,512]{1,0:T(8,128)(2,1)S(1)} %get-tuple-element.60), channel_id=1, source_target_pairs={{0,32},{1,9},{2,34},{3,11},{4,36},{5,13},{6,38},{7,15},{8,40},{9,1... | collective-permute-start | bytes 1966088 | tf_op jit(solution)/shard_map/ppermute | solution.py:31
  42.8 2.1 %collective-permute-start.12 = (bf16[640,512]{1,0:T(8,128)(2,1)S(1)}, bf16[640,512]{1,0:T(8,128)(2,1)S(1)}, u32[]{:S(2)}, u32[]{:S(2)}) collective-permute-start(bf16[640,512]{1,0:T(8,128)(2,1)S(1)} %get-tuple-element.61), channel_id=1, source_target_pairs={{0,96},{1,25},{2,98},{3,27},{4,100},{5,29},{6,102},{7,31},{8,104},... | collective-permute-start | bytes 1966088 | tf_op jit(solution)/shard_map/ppermute | solution.py:31
  45.0 9.8 %shard_map.114 = (bf16[2048,1024]{1,0:T(8,128)(2,1)}, bf16[320,512]{1,0:T(8,128)(2,1)S(1)}, bf16[320,512]{1,0:T(8,128)(2,1)S(1)}, bf16[320,512]{1,0:T(8,128)(2,1...) custom-call(s32[28]{0:T(128)S(1)} %get-tuple-element.45.numbers, ...), custom_call_target="tpu_custom_call", output_to_operand_aliasing={{0}: (7, {})} | custom-call | flops 10000000000 | bytes 10000000 | tf_op jit(solution)/shard_map/pallas_call | solution.py:258
  54.8 3.6 %collective-permute-done.11 = bf16[640,512]{1,0:T(8,128)(2,1)S(1)} collective-permute-done((bf16[640,512]{1,0:T(8,128)(2,1)S(1)}, bf16[640,512]{1,0:T(8,128)(2,1)S(1)}, u32[]{:S(2)}, u32[]{:S(2)}) %collective-permute-start.11) | collective-permute-done | bytes 655392 | tf_op jit(solution)/shard_map/ppermute | solution.py:31
  58.8 3.0 %collective-permute-start.17 = (bf16[320,512]{1,0:T(8,128)(2,1)S(1)}, bf16[320,512]{1,0:T(8,128)(2,1)S(1)}, u32[]{:S(2)}, u32[]{:S(2)}) collective-permute-start(bf16[320,512]{1,0:T(8,128)(2,1)S(1)} %get-tuple-element.74), channel_id=1, source_target_pairs={{0,32},{1,9},{2,34},{3,11},{4,36},{5,13},{6,38},{7,15},{8,40},{9,1... | collective-permute-start | bytes 983048 | tf_op jit(solution)/shard_map/ppermute | solution.py:31
  62.3 5.2 %collective-permute-start.13 = (bf16[160,512]{1,0:T(8,128)(2,1)S(1)}, bf16[160,512]{1,0:T(8,128)(2,1)S(1)}, u32[]{:S(2)}, u32[]{:S(2)}) collective-permute-start(bf16[160,512]{1,0:T(8,128)(2,1)S(1)} %get-tuple-element.83), channel_id=1, source_target_pairs={{0,16},{1,65},{2,18},{3,67},{4,20},{5,69},{6,22},{7,71},{8,24},{9,... | collective-permute-start | bytes 491528 | tf_op jit(solution)/shard_map/ppermute | solution.py:31
  67.6 3.2 %collective-permute-start.15 = (bf16[160,512]{1,0:T(8,128)(2,1)S(1)}, bf16[160,512]{1,0:T(8,128)(2,1)S(1)}, u32[]{:S(2)}, u32[]{:S(2)}) collective-permute-start(bf16[160,512]{1,0:T(8,128)(2,1)S(1)} %get-tuple-element.84), channel_id=1, source_target_pairs={{0,24},{1,97},{2,26},{3,99},{4,28},{5,101},{6,30},{7,103},{8,0},{9... | collective-permute-start | bytes 491528 | tf_op jit(solution)/shard_map/ppermute | solution.py:31
  71.9 1.1 %collective-permute-start.18 = (bf16[320,512]{1,0:T(8,128)(2,1)S(1)}, bf16[320,512]{1,0:T(8,128)(2,1)S(1)}, u32[]{:S(2)}, u32[]{:S(2)}) collective-permute-start(bf16[320,512]{1,0:T(8,128)(2,1)S(1)} %add_convert_fusion.1), channel_id=1, source_target_pairs={{0,32},{1,9},{2,34},{3,11},{4,36},{5,13},{6,38},{7,15},{8,40},{9,1... | collective-permute-start | bytes 983048 | tf_op jit(solution)/shard_map/ppermute | solution.py:31
  74.0 1.5 %collective-permute-done.14 = bf16[160,512]{1,0:T(8,128)(2,1)S(1)} collective-permute-done((bf16[160,512]{1,0:T(8,128)(2,1)S(1)}, bf16[160,512]{1,0:T(8,128)(2,1)S(1)}, u32[]{:S(2)}, u32[]{:S(2)}) %collective-permute-start.14) | collective-permute-done | bytes 163872 | tf_op jit(solution)/shard_map/ppermute | solution.py:31
  76.5 1.4 %collective-permute-done.16 = bf16[320,512]{1,0:T(8,128)(2,1)S(1)} collective-permute-done((bf16[320,512]{1,0:T(8,128)(2,1)S(1)}, bf16[320,512]{1,0:T(8,128)(2,1)S(1)}, u32[]{:S(2)}, u32[]{:S(2)}) %collective-permute-start.16) | collective-permute-done | bytes 327712 | tf_op jit(solution)/shard_map/ppermute | solution.py:31
  77.8 2.4 %collective-permute-done.18 = bf16[320,512]{1,0:T(8,128)(2,1)S(1)} collective-permute-done((bf16[320,512]{1,0:T(8,128)(2,1)S(1)}, bf16[320,512]{1,0:T(8,128)(2,1)S(1)}, u32[]{:S(2)}, u32[]{:S(2)}) %collective-permute-start.18) | collective-permute-done | bytes 327712 | tf_op jit(solution)/shard_map/ppermute | solution.py:31
  80.4 3.4 %collective-permute-done.19 = bf16[320,512]{1,0:T(8,128)(2,1)S(1)} collective-permute-done((bf16[320,512]{1,0:T(8,128)(2,1)S(1)}, bf16[320,512]{1,0:T(8,128)(2,1)S(1)}, u32[]{:S(2)}, u32[]{:S(2)}) %collective-permute-start.19) | collective-permute-done | bytes 327712 | tf_op jit(solution)/shard_map/ppermute | solution.py:31
  83.9 6.4 %collective-permute-start.22 = (bf16[160,512]{1,0:T(8,128)(2,1)S(1)}, bf16[160,512]{1,0:T(8,128)(2,1)S(1)}, u32[]{:S(2)}, u32[]{:S(2)}) collective-permute-start(bf16[160,512]{1,0:T(8,128)(2,1)S(1)} %pad_maximum_fusion.3), channel_id=1, source_target_pairs={{0,16},{1,65},{2,18},{3,67},{4,20},{5,69},{6,22},{7,71},{8,24},{9,... | collective-permute-start | bytes 491528 | tf_op jit(solution)/shard_map/ppermute | solution.py:31
  90.4 3.3 %collective-permute-start.24 = (bf16[160,512]{1,0:T(8,128)(2,1)S(1)}, bf16[160,512]{1,0:T(8,128)(2,1)S(1)}, u32[]{:S(2)}, u32[]{:S(2)}) collective-permute-start(bf16[160,512]{1,0:T(8,128)(2,1)S(1)} %pad_maximum_fusion.5), channel_id=1, source_target_pairs={{0,24},{1,97},{2,26},{3,99},{4,28},{5,101},{6,30},{7,103},{8,0},{9... | collective-permute-start | bytes 491528 | tf_op jit(solution)/shard_map/ppermute | solution.py:31
  93.8 3.1 %collective-permute-done.23 = bf16[160,512]{1,0:T(8,128)(2,1)S(1)} collective-permute-done((bf16[160,512]{1,0:T(8,128)(2,1)S(1)}, bf16[160,512]{1,0:T(8,128)(2,1)S(1)}, u32[]{:S(2)}, u32[]{:S(2)}) %collective-permute-start.23) | collective-permute-done | bytes 163872 | tf_op jit(solution)/shard_map/ppermute | solution.py:31
  (53 shorter events, 14.1 us)
Async XLA Ops:
  1.6 8.0 %collective-permute-start = (bf16[64,640]{1,0:T(8,128)(2,1)S(1)}, bf16[64,640]{1,0:T(8,128)(2,1)S(1)}, u32[]{:S(2)}, u32[]{:S(2)}) collective-permute-start(bf16[64,640]{1,0:T(8,128)(2,1)S(1)} %slice_select_fusion), channel_id=1, source_target_pairs={{0,32},{1,9},{2,34},{3,11},{4,36},{5,13},{6,38},{7,15},{8,40},{9,1... | collective-permute-start | bytes 245768 | tf_op jit(solution)/shard_map/ppermute | solution.py:31
  3.2 6.4 %collective-permute-start.1 = (bf16[64,640]{1,0:T(8,128)(2,1)S(1)}, bf16[64,640]{1,0:T(8,128)(2,1)S(1)}, u32[]{:S(2)}, u32[]{:S(2)}) collective-permute-start(bf16[64,640]{1,0:T(8,128)(2,1)S(1)} %slice_select_fusion), channel_id=1, source_target_pairs={{0,64},{1,17},{2,66},{3,19},{4,68},{5,21},{6,70},{7,23},{8,72},{9,... | collective-permute-start | bytes 245768 | tf_op jit(solution)/shard_map/ppermute | solution.py:31
  6.0 4.4 %collective-permute-start.2 = (bf16[64,640]{1,0:T(8,128)(2,1)S(1)}, bf16[64,640]{1,0:T(8,128)(2,1)S(1)}, u32[]{:S(2)}, u32[]{:S(2)}) collective-permute-start(bf16[64,640]{1,0:T(8,128)(2,1)S(1)} %slice_select_fusion), channel_id=1, source_target_pairs={{0,96},{1,25},{2,98},{3,27},{4,100},{5,29},{6,102},{7,31},{8,104},... | collective-permute-start | bytes 245768 | tf_op jit(solution)/shard_map/ppermute | solution.py:31
  10.4 12.8 %collective-permute-start.3 = (bf16[256,640]{1,0:T(8,128)(2,1)S(1)}, bf16[256,640]{1,0:T(8,128)(2,1)S(1)}, u32[]{:S(2)}, u32[]{:S(2)}) collective-permute-start(bf16[256,640]{1,0:T(8,128)(2,1)S(1)} %pad_maximum_fusion.refs_0_), channel_id=1, source_target_pairs={{0,8},{1,33},{2,10},{3,35},{4,12},{5,37},{6,14},{7,39},{8,16},{9,4... | collective-permute-start | bytes 983048 | tf_op jit(solution)/shard_map/ppermute | solution.py:31
  12.4 12.1 %collective-permute-start.4 = (bf16[256,640]{1,0:T(8,128)(2,1)S(1)}, bf16[256,640]{1,0:T(8,128)(2,1)S(1)}, u32[]{:S(2)}, u32[]{:S(2)}) collective-permute-start(bf16[256,640]{1,0:T(8,128)(2,1)S(1)} %pad_maximum_fusion.refs_0_), channel_id=1, source_target_pairs={{0,16},{1,65},{2,18},{3,67},{4,20},{5,69},{6,22},{7,71},{8,24},{9,... | collective-permute-start | bytes 983048 | tf_op jit(solution)/shard_map/ppermute | solution.py:31
  16.0 8.6 %collective-permute-start.5 = (bf16[256,640]{1,0:T(8,128)(2,1)S(1)}, bf16[256,640]{1,0:T(8,128)(2,1)S(1)}, u32[]{:S(2)}, u32[]{:S(2)}) collective-permute-start(bf16[256,640]{1,0:T(8,128)(2,1)S(1)} %pad_maximum_fusion.refs_0_), channel_id=1, source_target_pairs={{0,24},{1,97},{2,26},{3,99},{4,28},{5,101},{6,30},{7,103},{8,0},{9... | collective-permute-start | bytes 983048 | tf_op jit(solution)/shard_map/ppermute | solution.py:31
  24.6 2.1 %collective-permute-start.7 = (bf16[256,640]{1,0:T(8,128)(2,1)S(1)}, bf16[256,640]{1,0:T(8,128)(2,1)S(1)}, u32[]{:S(2)}, u32[]{:S(2)}) collective-permute-start(bf16[256,640]{1,0:T(8,128)(2,1)S(1)} %collective-permute-done.3.refs_1_), channel_id=1, source_target_pairs={{0,1},{1,0},{2,3},{3,2},{4,5},{5,4},{6,7},{7,6},{8,9},{9,8},{10,11... | collective-permute-start | bytes 983048 | tf_op jit(solution)/shard_map/ppermute | solution.py:35
  25.1 2.1 %collective-permute-start.8 = (bf16[256,640]{1,0:T(8,128)(2,1)S(1)}, bf16[256,640]{1,0:T(8,128)(2,1)S(1)}, u32[]{:S(2)}, u32[]{:S(2)}) collective-permute-start(bf16[256,640]{1,0:T(8,128)(2,1)S(1)} %collective-permute-done.4.refs_2_), channel_id=1, source_target_pairs={{0,1},{1,0},{2,3},{3,2},{4,5},{5,4},{6,7},{7,6},{8,9},{9,8},{10,11... | collective-permute-start | bytes 983048 | tf_op jit(solution)/shard_map/ppermute | solution.py:35
  25.1 2.5 %collective-permute-start.9 = (bf16[256,640]{1,0:T(8,128)(2,1)S(1)}, bf16[256,640]{1,0:T(8,128)(2,1)S(1)}, u32[]{:S(2)}, u32[]{:S(2)}) collective-permute-start(bf16[256,640]{1,0:T(8,128)(2,1)S(1)} %collective-permute-done.5.refs_3_), channel_id=1, source_target_pairs={{0,1},{1,0},{2,3},{3,2},{4,5},{5,4},{6,7},{7,6},{8,9},{9,8},{10,11... | collective-permute-start | bytes 983048 | tf_op jit(solution)/shard_map/ppermute | solution.py:35
  39.3 15.5 %collective-permute-start.10 = (bf16[640,512]{1,0:T(8,128)(2,1)S(1)}, bf16[640,512]{1,0:T(8,128)(2,1)S(1)}, u32[]{:S(2)}, u32[]{:S(2)}) collective-permute-start(bf16[640,512]{1,0:T(8,128)(2,1)S(1)} %get-tuple-element.59), channel_id=1, source_target_pairs={{0,64},{1,17},{2,66},{3,19},{4,68},{5,21},{6,70},{7,23},{8,72},{9,... | collective-permute-start | bytes 1966088 | tf_op jit(solution)/shard_map/ppermute | solution.py:31
  41.1 17.4 %collective-permute-start.11 = (bf16[640,512]{1,0:T(8,128)(2,1)S(1)}, bf16[640,512]{1,0:T(8,128)(2,1)S(1)}, u32[]{:S(2)}, u32[]{:S(2)}) collective-permute-start(bf16[640,512]{1,0:T(8,128)(2,1)S(1)} %get-tuple-element.60), channel_id=1, source_target_pairs={{0,32},{1,9},{2,34},{3,11},{4,36},{5,13},{6,38},{7,15},{8,40},{9,1... | collective-permute-start | bytes 1966088 | tf_op jit(solution)/shard_map/ppermute | solution.py:31
  42.8 15.6 %collective-permute-start.12 = (bf16[640,512]{1,0:T(8,128)(2,1)S(1)}, bf16[640,512]{1,0:T(8,128)(2,1)S(1)}, u32[]{:S(2)}, u32[]{:S(2)}) collective-permute-start(bf16[640,512]{1,0:T(8,128)(2,1)S(1)} %get-tuple-element.61), channel_id=1, source_target_pairs={{0,96},{1,25},{2,98},{3,27},{4,100},{5,29},{6,102},{7,31},{8,104},... | collective-permute-start | bytes 1966088 | tf_op jit(solution)/shard_map/ppermute | solution.py:31
  58.8 12.0 %collective-permute-start.17 = (bf16[320,512]{1,0:T(8,128)(2,1)S(1)}, bf16[320,512]{1,0:T(8,128)(2,1)S(1)}, u32[]{:S(2)}, u32[]{:S(2)}) collective-permute-start(bf16[320,512]{1,0:T(8,128)(2,1)S(1)} %get-tuple-element.74), channel_id=1, source_target_pairs={{0,32},{1,9},{2,34},{3,11},{4,36},{5,13},{6,38},{7,15},{8,40},{9,1... | collective-permute-start | bytes 983048 | tf_op jit(solution)/shard_map/ppermute | solution.py:31
  61.9 10.0 %collective-permute-start.20 = (bf16[320,512]{1,0:T(8,128)(2,1)S(1)}, bf16[320,512]{1,0:T(8,128)(2,1)S(1)}, u32[]{:S(2)}, u32[]{:S(2)}) collective-permute-start(bf16[320,512]{1,0:T(8,128)(2,1)S(1)} %get-tuple-element.78), channel_id=1, source_target_pairs={{0,96},{1,25},{2,98},{3,27},{4,100},{5,29},{6,102},{7,31},{8,104},... | collective-permute-start | bytes 983048 | tf_op jit(solution)/shard_map/ppermute | solution.py:31
  62.3 10.7 %collective-permute-start.13 = (bf16[160,512]{1,0:T(8,128)(2,1)S(1)}, bf16[160,512]{1,0:T(8,128)(2,1)S(1)}, u32[]{:S(2)}, u32[]{:S(2)}) collective-permute-start(bf16[160,512]{1,0:T(8,128)(2,1)S(1)} %get-tuple-element.83), channel_id=1, source_target_pairs={{0,16},{1,65},{2,18},{3,67},{4,20},{5,69},{6,22},{7,71},{8,24},{9,... | collective-permute-start | bytes 491528 | tf_op jit(solution)/shard_map/ppermute | solution.py:31
  67.5 8.0 %collective-permute-start.14 = (bf16[160,512]{1,0:T(8,128)(2,1)S(1)}, bf16[160,512]{1,0:T(8,128)(2,1)S(1)}, u32[]{:S(2)}, u32[]{:S(2)}) collective-permute-start(bf16[160,512]{1,0:T(8,128)(2,1)S(1)} %get-tuple-element.85), channel_id=1, source_target_pairs={{0,8},{1,33},{2,10},{3,35},{4,12},{5,37},{6,14},{7,39},{8,16},{9,4... | collective-permute-start | bytes 491528 | tf_op jit(solution)/shard_map/ppermute | solution.py:31
  67.6 8.8 %collective-permute-start.15 = (bf16[160,512]{1,0:T(8,128)(2,1)S(1)}, bf16[160,512]{1,0:T(8,128)(2,1)S(1)}, u32[]{:S(2)}, u32[]{:S(2)}) collective-permute-start(bf16[160,512]{1,0:T(8,128)(2,1)S(1)} %get-tuple-element.84), channel_id=1, source_target_pairs={{0,24},{1,97},{2,26},{3,99},{4,28},{5,101},{6,30},{7,103},{8,0},{9... | collective-permute-start | bytes 491528 | tf_op jit(solution)/shard_map/ppermute | solution.py:31
  70.8 7.1 %collective-permute-start.16 = (bf16[320,512]{1,0:T(8,128)(2,1)S(1)}, bf16[320,512]{1,0:T(8,128)(2,1)S(1)}, u32[]{:S(2)}, u32[]{:S(2)}) collective-permute-start(bf16[320,512]{1,0:T(8,128)(2,1)S(1)} %get-tuple-element.72), channel_id=1, source_target_pairs={{0,96},{1,25},{2,98},{3,27},{4,100},{5,29},{6,102},{7,31},{8,104},... | collective-permute-start | bytes 983048 | tf_op jit(solution)/shard_map/ppermute | solution.py:31
  71.9 8.4 %collective-permute-start.18 = (bf16[320,512]{1,0:T(8,128)(2,1)S(1)}, bf16[320,512]{1,0:T(8,128)(2,1)S(1)}, u32[]{:S(2)}, u32[]{:S(2)}) collective-permute-start(bf16[320,512]{1,0:T(8,128)(2,1)S(1)} %add_convert_fusion.1), channel_id=1, source_target_pairs={{0,32},{1,9},{2,34},{3,11},{4,36},{5,13},{6,38},{7,15},{8,40},{9,1... | collective-permute-start | bytes 983048 | tf_op jit(solution)/shard_map/ppermute | solution.py:31
  73.1 10.7 %collective-permute-start.19 = (bf16[320,512]{1,0:T(8,128)(2,1)S(1)}, bf16[320,512]{1,0:T(8,128)(2,1)S(1)}, u32[]{:S(2)}, u32[]{:S(2)}) collective-permute-start(bf16[320,512]{1,0:T(8,128)(2,1)S(1)} %get-tuple-element.76), channel_id=1, source_target_pairs={{0,32},{1,9},{2,34},{3,11},{4,36},{5,13},{6,38},{7,15},{8,40},{9,1... | collective-permute-start | bytes 983048 | tf_op jit(solution)/shard_map/ppermute | solution.py:31
  75.5 8.3 %collective-permute-start.21 = (bf16[320,512]{1,0:T(8,128)(2,1)S(1)}, bf16[320,512]{1,0:T(8,128)(2,1)S(1)}, u32[]{:S(2)}, u32[]{:S(2)}) collective-permute-start(bf16[320,512]{1,0:T(8,128)(2,1)S(1)} %add_convert_fusion), channel_id=1, source_target_pairs={{0,96},{1,25},{2,98},{3,27},{4,100},{5,29},{6,102},{7,31},{8,104},... | collective-permute-start | bytes 983048 | tf_op jit(solution)/shard_map/ppermute | solution.py:31
  83.9 9.9 %collective-permute-start.22 = (bf16[160,512]{1,0:T(8,128)(2,1)S(1)}, bf16[160,512]{1,0:T(8,128)(2,1)S(1)}, u32[]{:S(2)}, u32[]{:S(2)}) collective-permute-start(bf16[160,512]{1,0:T(8,128)(2,1)S(1)} %pad_maximum_fusion.3), channel_id=1, source_target_pairs={{0,16},{1,65},{2,18},{3,67},{4,20},{5,69},{6,22},{7,71},{8,24},{9,... | collective-permute-start | bytes 491528 | tf_op jit(solution)/shard_map/ppermute | solution.py:31
  90.3 6.6 %collective-permute-start.23 = (bf16[160,512]{1,0:T(8,128)(2,1)S(1)}, bf16[160,512]{1,0:T(8,128)(2,1)S(1)}, u32[]{:S(2)}, u32[]{:S(2)}) collective-permute-start(bf16[160,512]{1,0:T(8,128)(2,1)S(1)} %pad_maximum_fusion.4), channel_id=1, source_target_pairs={{0,8},{1,33},{2,10},{3,35},{4,12},{5,37},{6,14},{7,39},{8,16},{9,4... | collective-permute-start | bytes 491528 | tf_op jit(solution)/shard_map/ppermute | solution.py:31
  90.4 6.5 %collective-permute-start.24 = (bf16[160,512]{1,0:T(8,128)(2,1)S(1)}, bf16[160,512]{1,0:T(8,128)(2,1)S(1)}, u32[]{:S(2)}, u32[]{:S(2)}) collective-permute-start(bf16[160,512]{1,0:T(8,128)(2,1)S(1)} %pad_maximum_fusion.5), channel_id=1, source_target_pairs={{0,24},{1,97},{2,26},{3,99},{4,28},{5,101},{6,30},{7,103},{8,0},{9... | collective-permute-start | bytes 491528 | tf_op jit(solution)/shard_map/ppermute | solution.py:31
  (1 other events, 1.6 us)

commit v3 on v2

--- a/solution.py
+++ b/solution.py
@@ -11,9 +11,9 @@
 HEAD_DIM = 128
 LATENTS = 64
 SIDE = 4
-HEADS = 2
+HEADS = 4
 PAIR = HEADS * HEAD_DIM
-TOKEN_BLOCK = 512
+TOKEN_BLOCK = 256
 ONES = (((1,), (1,)), ((), ()))
 ZEROS = (((0,), (0,)), ((), ()))
 BF16 = jnp.bfloat16
@@ -193,7 +193,7 @@
 
 
 def first_kernel(groups, named, numbers, *refs):
-    parts, (key_weight, value_weight, queries, upstream) = refs[:8], refs[8:12]
+    parts, staged = refs[:8], [ref.at[:, :PAIR] for ref in refs[8:12]]
     query_grad, messages, (picked, picked_t), turned, scratch = refs[12], refs[13:17], refs[17:19], refs[19], refs[20:]
 
     @pl.when(pl.program_id(0) == 0)
@@ -202,7 +202,7 @@
 
     share = picked.shape[1] // (SIDE * SIDE)
     for major, second, product in backward(
-        numbers, picked, picked_t, key_weight, value_weight, queries, upstream, query_grad, scratch, groups, named
+        numbers, picked, picked_t, *staged, query_grad, scratch, groups, named
     ):
         for minor in range(SIDE):
             to = (2 * minor + second) * share
@@ -210,10 +210,10 @@
 
 
 def second_kernel(groups, named, numbers, *refs):
-    picked, picked_t, key_weight, value_weight, queries, upstream = refs[:6]
+    picked, picked_t, *staged = refs[:2] + tuple(ref.at[:, PAIR:] for ref in refs[2:6])
     query_grad, messages, scratch = refs[7], refs[8:16], refs[16:]
     for major, second, product in backward(
-        numbers, picked, picked_t, key_weight, value_weight, queries, upstream, query_grad, scratch, groups, named
+        numbers, picked, picked_t, *staged, query_grad, scratch, groups, named
     ):
         messages[second * SIDE + major][...] = product
 
@@ -232,8 +232,9 @@
     message = lambda rows: pl.BlockSpec((rows, PAIR), lambda step, *_: (0, step))
     shape = jax.ShapeDtypeStruct
     in_specs = [whole(part.shape) for part in latents]
-    in_specs += [columns(vision), columns(vision), columns(tokens), columns(tokens)]
-    inputs = [numbers, *latents, key_weight, value_weight, queries, upstream]
+    in_specs += [pl.BlockSpec(memory_space=pltpu.VMEM)] * 4
+    staged = [pltpu.with_memory_space_constraint(array, pltpu.VMEM) for array in (key_weight, value_weight, queries, upstream)]
+    inputs = [numbers, *latents, *staged]
     out_specs, out_shape = [columns(tokens)], [shape((tokens, width), BF16)]
     scratch = [
         pltpu.VMEM((picked_rows, PAIR), BF16),

time: 99.2 us -> 98.7 us (level)
  starting transfers between devices: 44.5 us -> 39.9 us
  Pallas kernels: 27.8 us -> 29.8 us
  waiting for transfers between devices: 19.6 us -> 20.8 us
    ppermute x21, starting transfers between devices: 43.5 us -> 38.9 us  [shift(): return lax.ppermute(array, ('seq', 'mp'), pairs)]
    pallas_call x2, Pallas kernels: 21.6 us -> 23.6 us  [attention(): pl.pallas_call(functools.partial(first_kernel if first else second_kernel...]
    ppermute x21, waiting for transfers between devices: 17.6 us -> 18.8 us  [shift(): return lax.ppermute(array, ('seq', 'mp'), pairs)]
  transfers between devices with their start and end apart: 25 -> 25, of which waited for: 12 -> 12; matrix products, arithmetic and copies ran while one was open for 3% -> 3% of each run, Pallas kernels for 16% -> 18%
where the time goes in v3:
time: 98.7 us; the launch traced here: 97.2 us
  starting transfers between devices  39.9 us (40%)
  Pallas kernels  29.8 us (30%)
  waiting for transfers between devices  20.8 us (21%)
  other arithmetic  3.51 us (4%)
  local copies, waits for them, and re-layouts  2.34 us (2%)
    ppermute x21, starting transfers between devices, shift(): return lax.ppermute(array, ('seq', 'mp'), pairs)  38.9 us
    pallas_call x2, Pallas kernels, attention(): pl.pallas_call(functools.partial(first_kernel if first else second_kernel...  23.6 us
    ppermute x21, waiting for transfers between devices, shift(): return lax.ppermute(array, ('seq', 'mp'), pairs)  18.8 us
    pallas_call x1, Pallas kernels, stage(): pl.pallas_call(functools.partial(stage_kernel, groups, named), in_specs=[...  6.2 us
    ppermute x4, waiting for transfers between devices, swap_cores(): return lax.ppermute(array, 'mp', [(m, m ^ 1) for m in range(mp)])  2.01 us
  transfers between devices with their start and end apart: 25, of which 12 were waited for; matrix products, arithmetic and copies ran while one was open for 3% of the time, Pallas kernels for 18%

profile of v3, /device:TPU:0, one launch (start us, length us, event | category | flops | bytes accessed | tf_op | source)
XLA Modules:
  0.0 97.2 jit_solution(4277448608139471255)
XLA Ops:
  1.6 1.6 %collective-permute-start = (bf16[64,640]{1,0:T(8,128)(2,1)S(1)}, bf16[64,640]{1,0:T(8,128)(2,1)S(1)}, u32[]{:S(2)}, u32[]{:S(2)}) collective-permute-start(bf16[64,640]{1,0:T(8,128)(2,1)S(1)} %slice_select_fusion), channel_id=1, source_target_pairs={{0,32},{1,9},{2,34},{3,11},{4,36},{5,13},{6,38},{7,15},{8,40},{9,1... | collective-permute-start | bytes 245768 | tf_op jit(solution)/shard_map/ppermute | solution.py:31
  3.2 2.7 %collective-permute-start.1 = (bf16[64,640]{1,0:T(8,128)(2,1)S(1)}, bf16[64,640]{1,0:T(8,128)(2,1)S(1)}, u32[]{:S(2)}, u32[]{:S(2)}) collective-permute-start(bf16[64,640]{1,0:T(8,128)(2,1)S(1)} %slice_select_fusion), channel_id=1, source_target_pairs={{0,64},{1,17},{2,66},{3,19},{4,68},{5,21},{6,70},{7,23},{8,72},{9,... | collective-permute-start | bytes 245768 | tf_op jit(solution)/shard_map/ppermute | solution.py:31
  6.0 1.4 %collective-permute-start.2 = (bf16[64,640]{1,0:T(8,128)(2,1)S(1)}, bf16[64,640]{1,0:T(8,128)(2,1)S(1)}, u32[]{:S(2)}, u32[]{:S(2)}) collective-permute-start(bf16[64,640]{1,0:T(8,128)(2,1)S(1)} %slice_select_fusion), channel_id=1, source_target_pairs={{0,96},{1,25},{2,98},{3,27},{4,100},{5,29},{6,102},{7,31},{8,104},... | collective-permute-start | bytes 245768 | tf_op jit(solution)/shard_map/ppermute | solution.py:31
  10.4 2.0 %collective-permute-start.3 = (bf16[256,640]{1,0:T(8,128)(2,1)S(1)}, bf16[256,640]{1,0:T(8,128)(2,1)S(1)}, u32[]{:S(2)}, u32[]{:S(2)}) collective-permute-start(bf16[256,640]{1,0:T(8,128)(2,1)S(1)} %pad_maximum_fusion.refs_0_), channel_id=1, source_target_pairs={{0,8},{1,33},{2,10},{3,35},{4,12},{5,37},{6,14},{7,39},{8,16},{9,4... | collective-permute-start | bytes 983048 | tf_op jit(solution)/shard_map/ppermute | solution.py:31
  12.4 3.6 %collective-permute-start.4 = (bf16[256,640]{1,0:T(8,128)(2,1)S(1)}, bf16[256,640]{1,0:T(8,128)(2,1)S(1)}, u32[]{:S(2)}, u32[]{:S(2)}) collective-permute-start(bf16[256,640]{1,0:T(8,128)(2,1)S(1)} %pad_maximum_fusion.refs_0_), channel_id=1, source_target_pairs={{0,16},{1,65},{2,18},{3,67},{4,20},{5,69},{6,22},{7,71},{8,24},{9,... | collective-permute-start | bytes 983048 | tf_op jit(solution)/shard_map/ppermute | solution.py:31
  17.0 6.2 %shard_map.112 = (bf16[1280,1024]{1,0:T(8,128)(2,1)S(1)}, bf16[1280,1024]{1,0:T(8,128)(2,1)S(1)}, bf16[2048,1024]{1,0:T(8,128)(2,1)S(1)}, bf16[2048,1024]{1,0:T(8,128)(2,1)S(1)}, s32[28]{0:T(128)S(1)}) custom-call(s32[28]{0:T(128)S(1)} %concatenate.28.numbers, f32[1,1024]{1,0:T(1,128)S(1)} %bitcast.3, bf16[1280,1024]{1,0:T(8,128)(2,1)} %key_weight.1, ...), custom_call_target="tpu_custom_call" | custom-call | flops 10000000 | bytes 20000000 | tf_op jit(solution)/shard_map/pallas_call | solution.py:179
  23.2 1.3 %collective-permute-done.4.refs_2_ = bf16[256,640]{1,0:T(8,128)(2,1)S(1)} collective-permute-done((bf16[256,640]{1,0:T(8,128)(2,1)S(1)}, bf16[256,640]{1,0:T(8,128)(2,1)S(1)}, u32[]{:S(2)}, u32[]{:S(2)}) %collective-permute-start.4) | collective-permute-done | bytes 327712 | tf_op jit(solution)/shard_map/ppermute | solution.py:31
  27.6 12.6 %shard_map.113 = (bf16[2048,1024]{1,0:T(8,128)(2,1)}, bf16[640,512]{1,0:T(8,128)(2,1)S(1)}, bf16[640,512]{1,0:T(8,128)(2,1)S(1)}, bf16[640,512]{1,0:T(8,128)(2,1...) custom-call(s32[28]{0:T(128)S(1)} %get-tuple-element.45.numbers, ...), custom_call_target="tpu_custom_call" | custom-call | flops 10000000000 | bytes 10000000 | tf_op jit(solution)/shard_map/pallas_call | solution.py:259
  40.9 3.2 %collective-permute-start.12 = (bf16[640,512]{1,0:T(8,128)(2,1)S(1)}, bf16[640,512]{1,0:T(8,128)(2,1)S(1)}, u32[]{:S(2)}, u32[]{:S(2)}) collective-permute-start(bf16[640,512]{1,0:T(8,128)(2,1)S(1)} %get-tuple-element.61), channel_id=1, source_target_pairs={{0,96},{1,25},{2,98},{3,27},{4,100},{5,29},{6,102},{7,31},{8,104},... | collective-permute-start | bytes 1966088 | tf_op jit(solution)/shard_map/ppermute | solution.py:31
  44.1 11.0 %shard_map.114 = (bf16[2048,1024]{1,0:T(8,128)(2,1)}, bf16[320,512]{1,0:T(8,128)(2,1)S(1)}, bf16[320,512]{1,0:T(8,128)(2,1)S(1)}, bf16[320,512]{1,0:T(8,128)(2,1...) custom-call(s32[28]{0:T(128)S(1)} %get-tuple-element.45.numbers, ...), custom_call_target="tpu_custom_call", output_to_operand_aliasing={{0}: (7, {})} | custom-call | flops 10000000000 | bytes 10000000 | tf_op jit(solution)/shard_map/pallas_call | solution.py:259
  55.1 4.2 %collective-permute-done.11 = bf16[640,512]{1,0:T(8,128)(2,1)S(1)} collective-permute-done((bf16[640,512]{1,0:T(8,128)(2,1)S(1)}, bf16[640,512]{1,0:T(8,128)(2,1)S(1)}, u32[]{:S(2)}, u32[]{:S(2)}) %collective-permute-start.11) | collective-permute-done | bytes 655392 | tf_op jit(solution)/shard_map/ppermute | solution.py:31
  59.9 3.3 %collective-permute-start.20 = (bf16[320,512]{1,0:T(8,128)(2,1)S(1)}, bf16[320,512]{1,0:T(8,128)(2,1)S(1)}, u32[]{:S(2)}, u32[]{:S(2)}) collective-permute-start(bf16[320,512]{1,0:T(8,128)(2,1)S(1)} %get-tuple-element.78), channel_id=1, source_target_pairs={{0,96},{1,25},{2,98},{3,27},{4,100},{5,29},{6,102},{7,31},{8,104},... | collective-permute-start | bytes 983048 | tf_op jit(solution)/shard_map/ppermute | solution.py:31
  63.2 1.9 %collective-permute-start.13 = (bf16[160,512]{1,0:T(8,128)(2,1)S(1)}, bf16[160,512]{1,0:T(8,128)(2,1)S(1)}, u32[]{:S(2)}, u32[]{:S(2)}) collective-permute-start(bf16[160,512]{1,0:T(8,128)(2,1)S(1)} %get-tuple-element.83), channel_id=1, source_target_pairs={{0,16},{1,65},{2,18},{3,67},{4,20},{5,69},{6,22},{7,71},{8,24},{9,... | collective-permute-start | bytes 491528 | tf_op jit(solution)/shard_map/ppermute | solution.py:31
  65.1 1.2 %collective-permute-start.14 = (bf16[160,512]{1,0:T(8,128)(2,1)S(1)}, bf16[160,512]{1,0:T(8,128)(2,1)S(1)}, u32[]{:S(2)}, u32[]{:S(2)}) collective-permute-start(bf16[160,512]{1,0:T(8,128)(2,1)S(1)} %get-tuple-element.85), channel_id=1, source_target_pairs={{0,8},{1,33},{2,10},{3,35},{4,12},{5,37},{6,14},{7,39},{8,16},{9,4... | collective-permute-start | bytes 491528 | tf_op jit(solution)/shard_map/ppermute | solution.py:31
  66.3 2.1 %collective-permute-start.15 = (bf16[160,512]{1,0:T(8,128)(2,1)S(1)}, bf16[160,512]{1,0:T(8,128)(2,1)S(1)}, u32[]{:S(2)}, u32[]{:S(2)}) collective-permute-start(bf16[160,512]{1,0:T(8,128)(2,1)S(1)} %get-tuple-element.84), channel_id=1, source_target_pairs={{0,24},{1,97},{2,26},{3,99},{4,28},{5,101},{6,30},{7,103},{8,0},{9... | collective-permute-start | bytes 491528 | tf_op jit(solution)/shard_map/ppermute | solution.py:31
  68.3 2.8 %collective-permute-done.17 = bf16[320,512]{1,0:T(8,128)(2,1)S(1)} collective-permute-done((bf16[320,512]{1,0:T(8,128)(2,1)S(1)}, bf16[320,512]{1,0:T(8,128)(2,1)S(1)}, u32[]{:S(2)}, u32[]{:S(2)}) %collective-permute-start.17) | collective-permute-done | bytes 327712 | tf_op jit(solution)/shard_map/ppermute | solution.py:31
  71.2 2.1 %collective-permute-start.18 = (bf16[320,512]{1,0:T(8,128)(2,1)S(1)}, bf16[320,512]{1,0:T(8,128)(2,1)S(1)}, u32[]{:S(2)}, u32[]{:S(2)}) collective-permute-start(bf16[320,512]{1,0:T(8,128)(2,1)S(1)} %add_convert_fusion.1), channel_id=1, source_target_pairs={{0,32},{1,9},{2,34},{3,11},{4,36},{5,13},{6,38},{7,15},{8,40},{9,1... | collective-permute-start | bytes 983048 | tf_op jit(solution)/shard_map/ppermute | solution.py:31
  73.5 3.2 %collective-permute-start.21 = (bf16[320,512]{1,0:T(8,128)(2,1)S(1)}, bf16[320,512]{1,0:T(8,128)(2,1)S(1)}, u32[]{:S(2)}, u32[]{:S(2)}) collective-permute-start(bf16[320,512]{1,0:T(8,128)(2,1)S(1)} %add_convert_fusion), channel_id=1, source_target_pairs={{0,96},{1,25},{2,98},{3,27},{4,100},{5,29},{6,102},{7,31},{8,104},... | collective-permute-start | bytes 983048 | tf_op jit(solution)/shard_map/ppermute | solution.py:31
  76.8 1.4 %collective-permute-done.16 = bf16[320,512]{1,0:T(8,128)(2,1)S(1)} collective-permute-done((bf16[320,512]{1,0:T(8,128)(2,1)S(1)}, bf16[320,512]{1,0:T(8,128)(2,1)S(1)}, u32[]{:S(2)}, u32[]{:S(2)}) %collective-permute-start.16) | collective-permute-done | bytes 327712 | tf_op jit(solution)/shard_map/ppermute | solution.py:31
  78.2 1.7 %collective-permute-done.18 = bf16[320,512]{1,0:T(8,128)(2,1)S(1)} collective-permute-done((bf16[320,512]{1,0:T(8,128)(2,1)S(1)}, bf16[320,512]{1,0:T(8,128)(2,1)S(1)}, u32[]{:S(2)}, u32[]{:S(2)}) %collective-permute-start.18) | collective-permute-done | bytes 327712 | tf_op jit(solution)/shard_map/ppermute | solution.py:31
  80.1 3.4 %collective-permute-done.19 = bf16[320,512]{1,0:T(8,128)(2,1)S(1)} collective-permute-done((bf16[320,512]{1,0:T(8,128)(2,1)S(1)}, bf16[320,512]{1,0:T(8,128)(2,1)S(1)}, u32[]{:S(2)}, u32[]{:S(2)}) %collective-permute-start.19) | collective-permute-done | bytes 327712 | tf_op jit(solution)/shard_map/ppermute | solution.py:31
  83.6 5.4 %collective-permute-start.22 = (bf16[160,512]{1,0:T(8,128)(2,1)S(1)}, bf16[160,512]{1,0:T(8,128)(2,1)S(1)}, u32[]{:S(2)}, u32[]{:S(2)}) collective-permute-start(bf16[160,512]{1,0:T(8,128)(2,1)S(1)} %pad_maximum_fusion.3), channel_id=1, source_target_pairs={{0,16},{1,65},{2,18},{3,67},{4,20},{5,69},{6,22},{7,71},{8,24},{9,... | collective-permute-start | bytes 491528 | tf_op jit(solution)/shard_map/ppermute | solution.py:31
  89.8 2.6 %collective-permute-start.24 = (bf16[160,512]{1,0:T(8,128)(2,1)S(1)}, bf16[160,512]{1,0:T(8,128)(2,1)S(1)}, u32[]{:S(2)}, u32[]{:S(2)}) collective-permute-start(bf16[160,512]{1,0:T(8,128)(2,1)S(1)} %pad_maximum_fusion.5), channel_id=1, source_target_pairs={{0,24},{1,97},{2,26},{3,99},{4,28},{5,101},{6,30},{7,103},{8,0},{9... | collective-permute-start | bytes 491528 | tf_op jit(solution)/shard_map/ppermute | solution.py:31
  92.5 3.1 %collective-permute-done.23 = bf16[160,512]{1,0:T(8,128)(2,1)S(1)} collective-permute-done((bf16[160,512]{1,0:T(8,128)(2,1)S(1)}, bf16[160,512]{1,0:T(8,128)(2,1)S(1)}, u32[]{:S(2)}, u32[]{:S(2)}) %collective-permute-start.23) | collective-permute-done | bytes 163872 | tf_op jit(solution)/shard_map/ppermute | solution.py:31
  (53 shorter events, 12.3 us)
Async XLA Ops:
  1.6 8.0 %collective-permute-start = (bf16[64,640]{1,0:T(8,128)(2,1)S(1)}, bf16[64,640]{1,0:T(8,128)(2,1)S(1)}, u32[]{:S(2)}, u32[]{:S(2)}) collective-permute-start(bf16[64,640]{1,0:T(8,128)(2,1)S(1)} %slice_select_fusion), channel_id=1, source_target_pairs={{0,32},{1,9},{2,34},{3,11},{4,36},{5,13},{6,38},{7,15},{8,40},{9,1... | collective-permute-start | bytes 245768 | tf_op jit(solution)/shard_map/ppermute | solution.py:31
  3.2 6.4 %collective-permute-start.1 = (bf16[64,640]{1,0:T(8,128)(2,1)S(1)}, bf16[64,640]{1,0:T(8,128)(2,1)S(1)}, u32[]{:S(2)}, u32[]{:S(2)}) collective-permute-start(bf16[64,640]{1,0:T(8,128)(2,1)S(1)} %slice_select_fusion), channel_id=1, source_target_pairs={{0,64},{1,17},{2,66},{3,19},{4,68},{5,21},{6,70},{7,23},{8,72},{9,... | collective-permute-start | bytes 245768 | tf_op jit(solution)/shard_map/ppermute | solution.py:31
  6.0 4.4 %collective-permute-start.2 = (bf16[64,640]{1,0:T(8,128)(2,1)S(1)}, bf16[64,640]{1,0:T(8,128)(2,1)S(1)}, u32[]{:S(2)}, u32[]{:S(2)}) collective-permute-start(bf16[64,640]{1,0:T(8,128)(2,1)S(1)} %slice_select_fusion), channel_id=1, source_target_pairs={{0,96},{1,25},{2,98},{3,27},{4,100},{5,29},{6,102},{7,31},{8,104},... | collective-permute-start | bytes 245768 | tf_op jit(solution)/shard_map/ppermute | solution.py:31
  10.4 12.8 %collective-permute-start.3 = (bf16[256,640]{1,0:T(8,128)(2,1)S(1)}, bf16[256,640]{1,0:T(8,128)(2,1)S(1)}, u32[]{:S(2)}, u32[]{:S(2)}) collective-permute-start(bf16[256,640]{1,0:T(8,128)(2,1)S(1)} %pad_maximum_fusion.refs_0_), channel_id=1, source_target_pairs={{0,8},{1,33},{2,10},{3,35},{4,12},{5,37},{6,14},{7,39},{8,16},{9,4... | collective-permute-start | bytes 983048 | tf_op jit(solution)/shard_map/ppermute | solution.py:31
  12.4 12.1 %collective-permute-start.4 = (bf16[256,640]{1,0:T(8,128)(2,1)S(1)}, bf16[256,640]{1,0:T(8,128)(2,1)S(1)}, u32[]{:S(2)}, u32[]{:S(2)}) collective-permute-start(bf16[256,640]{1,0:T(8,128)(2,1)S(1)} %pad_maximum_fusion.refs_0_), channel_id=1, source_target_pairs={{0,16},{1,65},{2,18},{3,67},{4,20},{5,69},{6,22},{7,71},{8,24},{9,... | collective-permute-start | bytes 983048 | tf_op jit(solution)/shard_map/ppermute | solution.py:31
  16.0 8.6 %collective-permute-start.5 = (bf16[256,640]{1,0:T(8,128)(2,1)S(1)}, bf16[256,640]{1,0:T(8,128)(2,1)S(1)}, u32[]{:S(2)}, u32[]{:S(2)}) collective-permute-start(bf16[256,640]{1,0:T(8,128)(2,1)S(1)} %pad_maximum_fusion.refs_0_), channel_id=1, source_target_pairs={{0,24},{1,97},{2,26},{3,99},{4,28},{5,101},{6,30},{7,103},{8,0},{9... | collective-permute-start | bytes 983048 | tf_op jit(solution)/shard_map/ppermute | solution.py:31
  24.6 2.1 %collective-permute-start.7 = (bf16[256,640]{1,0:T(8,128)(2,1)S(1)}, bf16[256,640]{1,0:T(8,128)(2,1)S(1)}, u32[]{:S(2)}, u32[]{:S(2)}) collective-permute-start(bf16[256,640]{1,0:T(8,128)(2,1)S(1)} %collective-permute-done.3.refs_1_), channel_id=1, source_target_pairs={{0,1},{1,0},{2,3},{3,2},{4,5},{5,4},{6,7},{7,6},{8,9},{9,8},{10,11... | collective-permute-start | bytes 983048 | tf_op jit(solution)/shard_map/ppermute | solution.py:35
  25.1 2.1 %collective-permute-start.8 = (bf16[256,640]{1,0:T(8,128)(2,1)S(1)}, bf16[256,640]{1,0:T(8,128)(2,1)S(1)}, u32[]{:S(2)}, u32[]{:S(2)}) collective-permute-start(bf16[256,640]{1,0:T(8,128)(2,1)S(1)} %collective-permute-done.4.refs_2_), channel_id=1, source_target_pairs={{0,1},{1,0},{2,3},{3,2},{4,5},{5,4},{6,7},{7,6},{8,9},{9,8},{10,11... | collective-permute-start | bytes 983048 | tf_op jit(solution)/shard_map/ppermute | solution.py:35
  25.1 2.5 %collective-permute-start.9 = (bf16[256,640]{1,0:T(8,128)(2,1)S(1)}, bf16[256,640]{1,0:T(8,128)(2,1)S(1)}, u32[]{:S(2)}, u32[]{:S(2)}) collective-permute-start(bf16[256,640]{1,0:T(8,128)(2,1)S(1)} %collective-permute-done.5.refs_3_), channel_id=1, source_target_pairs={{0,1},{1,0},{2,3},{3,2},{4,5},{5,4},{6,7},{7,6},{8,9},{9,8},{10,11... | collective-permute-start | bytes 983048 | tf_op jit(solution)/shard_map/ppermute | solution.py:35
  40.2 14.9 %collective-permute-start.10 = (bf16[640,512]{1,0:T(8,128)(2,1)S(1)}, bf16[640,512]{1,0:T(8,128)(2,1)S(1)}, u32[]{:S(2)}, u32[]{:S(2)}) collective-permute-start(bf16[640,512]{1,0:T(8,128)(2,1)S(1)} %get-tuple-element.59), channel_id=1, source_target_pairs={{0,64},{1,17},{2,66},{3,19},{4,68},{5,21},{6,70},{7,23},{8,72},{9,... | collective-permute-start | bytes 1966088 | tf_op jit(solution)/shard_map/ppermute | solution.py:31
  40.9 18.5 %collective-permute-start.11 = (bf16[640,512]{1,0:T(8,128)(2,1)S(1)}, bf16[640,512]{1,0:T(8,128)(2,1)S(1)}, u32[]{:S(2)}, u32[]{:S(2)}) collective-permute-start(bf16[640,512]{1,0:T(8,128)(2,1)S(1)} %get-tuple-element.60), channel_id=1, source_target_pairs={{0,32},{1,9},{2,34},{3,11},{4,36},{5,13},{6,38},{7,15},{8,40},{9,1... | collective-permute-start | bytes 1966088 | tf_op jit(solution)/shard_map/ppermute | solution.py:31
  40.9 18.5 %collective-permute-start.12 = (bf16[640,512]{1,0:T(8,128)(2,1)S(1)}, bf16[640,512]{1,0:T(8,128)(2,1)S(1)}, u32[]{:S(2)}, u32[]{:S(2)}) collective-permute-start(bf16[640,512]{1,0:T(8,128)(2,1)S(1)} %get-tuple-element.61), channel_id=1, source_target_pairs={{0,96},{1,25},{2,98},{3,27},{4,100},{5,29},{6,102},{7,31},{8,104},... | collective-permute-start | bytes 1966088 | tf_op jit(solution)/shard_map/ppermute | solution.py:31
  59.7 11.4 %collective-permute-start.17 = (bf16[320,512]{1,0:T(8,128)(2,1)S(1)}, bf16[320,512]{1,0:T(8,128)(2,1)S(1)}, u32[]{:S(2)}, u32[]{:S(2)}) collective-permute-start(bf16[320,512]{1,0:T(8,128)(2,1)S(1)} %get-tuple-element.74), channel_id=1, source_target_pairs={{0,32},{1,9},{2,34},{3,11},{4,36},{5,13},{6,38},{7,15},{8,40},{9,1... | collective-permute-start | bytes 983048 | tf_op jit(solution)/shard_map/ppermute | solution.py:31
  59.9 11.4 %collective-permute-start.20 = (bf16[320,512]{1,0:T(8,128)(2,1)S(1)}, bf16[320,512]{1,0:T(8,128)(2,1)S(1)}, u32[]{:S(2)}, u32[]{:S(2)}) collective-permute-start(bf16[320,512]{1,0:T(8,128)(2,1)S(1)} %get-tuple-element.78), channel_id=1, source_target_pairs={{0,96},{1,25},{2,98},{3,27},{4,100},{5,29},{6,102},{7,31},{8,104},... | collective-permute-start | bytes 983048 | tf_op jit(solution)/shard_map/ppermute | solution.py:31
  63.2 10.2 %collective-permute-start.13 = (bf16[160,512]{1,0:T(8,128)(2,1)S(1)}, bf16[160,512]{1,0:T(8,128)(2,1)S(1)}, u32[]{:S(2)}, u32[]{:S(2)}) collective-permute-start(bf16[160,512]{1,0:T(8,128)(2,1)S(1)} %get-tuple-element.83), channel_id=1, source_target_pairs={{0,16},{1,65},{2,18},{3,67},{4,20},{5,69},{6,22},{7,71},{8,24},{9,... | collective-permute-start | bytes 491528 | tf_op jit(solution)/shard_map/ppermute | solution.py:31
  65.1 8.4 %collective-permute-start.14 = (bf16[160,512]{1,0:T(8,128)(2,1)S(1)}, bf16[160,512]{1,0:T(8,128)(2,1)S(1)}, u32[]{:S(2)}, u32[]{:S(2)}) collective-permute-start(bf16[160,512]{1,0:T(8,128)(2,1)S(1)} %get-tuple-element.85), channel_id=1, source_target_pairs={{0,8},{1,33},{2,10},{3,35},{4,12},{5,37},{6,14},{7,39},{8,16},{9,4... | collective-permute-start | bytes 491528 | tf_op jit(solution)/shard_map/ppermute | solution.py:31
  66.3 10.5 %collective-permute-start.15 = (bf16[160,512]{1,0:T(8,128)(2,1)S(1)}, bf16[160,512]{1,0:T(8,128)(2,1)S(1)}, u32[]{:S(2)}, u32[]{:S(2)}) collective-permute-start(bf16[160,512]{1,0:T(8,128)(2,1)S(1)} %get-tuple-element.84), channel_id=1, source_target_pairs={{0,24},{1,97},{2,26},{3,99},{4,28},{5,101},{6,30},{7,103},{8,0},{9... | collective-permute-start | bytes 491528 | tf_op jit(solution)/shard_map/ppermute | solution.py:31
  71.1 7.1 %collective-permute-start.16 = (bf16[320,512]{1,0:T(8,128)(2,1)S(1)}, bf16[320,512]{1,0:T(8,128)(2,1)S(1)}, u32[]{:S(2)}, u32[]{:S(2)}) collective-permute-start(bf16[320,512]{1,0:T(8,128)(2,1)S(1)} %get-tuple-element.72), channel_id=1, source_target_pairs={{0,96},{1,25},{2,98},{3,27},{4,100},{5,29},{6,102},{7,31},{8,104},... | collective-permute-start | bytes 983048 | tf_op jit(solution)/shard_map/ppermute | solution.py:31
  71.2 8.7 %collective-permute-start.18 = (bf16[320,512]{1,0:T(8,128)(2,1)S(1)}, bf16[320,512]{1,0:T(8,128)(2,1)S(1)}, u32[]{:S(2)}, u32[]{:S(2)}) collective-permute-start(bf16[320,512]{1,0:T(8,128)(2,1)S(1)} %add_convert_fusion.1), channel_id=1, source_target_pairs={{0,32},{1,9},{2,34},{3,11},{4,36},{5,13},{6,38},{7,15},{8,40},{9,1... | collective-permute-start | bytes 983048 | tf_op jit(solution)/shard_map/ppermute | solution.py:31
  73.4 10.0 %collective-permute-start.19 = (bf16[320,512]{1,0:T(8,128)(2,1)S(1)}, bf16[320,512]{1,0:T(8,128)(2,1)S(1)}, u32[]{:S(2)}, u32[]{:S(2)}) collective-permute-start(bf16[320,512]{1,0:T(8,128)(2,1)S(1)} %get-tuple-element.76), channel_id=1, source_target_pairs={{0,32},{1,9},{2,34},{3,11},{4,36},{5,13},{6,38},{7,15},{8,40},{9,1... | collective-permute-start | bytes 983048 | tf_op jit(solution)/shard_map/ppermute | solution.py:31
  73.5 9.9 %collective-permute-start.21 = (bf16[320,512]{1,0:T(8,128)(2,1)S(1)}, bf16[320,512]{1,0:T(8,128)(2,1)S(1)}, u32[]{:S(2)}, u32[]{:S(2)}) collective-permute-start(bf16[320,512]{1,0:T(8,128)(2,1)S(1)} %add_convert_fusion), channel_id=1, source_target_pairs={{0,96},{1,25},{2,98},{3,27},{4,100},{5,29},{6,102},{7,31},{8,104},... | collective-permute-start | bytes 983048 | tf_op jit(solution)/shard_map/ppermute | solution.py:31
  83.6 8.8 %collective-permute-start.22 = (bf16[160,512]{1,0:T(8,128)(2,1)S(1)}, bf16[160,512]{1,0:T(8,128)(2,1)S(1)}, u32[]{:S(2)}, u32[]{:S(2)}) collective-permute-start(bf16[160,512]{1,0:T(8,128)(2,1)S(1)} %pad_maximum_fusion.3), channel_id=1, source_target_pairs={{0,16},{1,65},{2,18},{3,67},{4,20},{5,69},{6,22},{7,71},{8,24},{9,... | collective-permute-start | bytes 491528 | tf_op jit(solution)/shard_map/ppermute | solution.py:31
  89.0 6.6 %collective-permute-start.23 = (bf16[160,512]{1,0:T(8,128)(2,1)S(1)}, bf16[160,512]{1,0:T(8,128)(2,1)S(1)}, u32[]{:S(2)}, u32[]{:S(2)}) collective-permute-start(bf16[160,512]{1,0:T(8,128)(2,1)S(1)} %pad_maximum_fusion.4), channel_id=1, source_target_pairs={{0,8},{1,33},{2,10},{3,35},{4,12},{5,37},{6,14},{7,39},{8,16},{9,4... | collective-permute-start | bytes 491528 | tf_op jit(solution)/shard_map/ppermute | solution.py:31
  89.8 5.8 %collective-permute-start.24 = (bf16[160,512]{1,0:T(8,128)(2,1)S(1)}, bf16[160,512]{1,0:T(8,128)(2,1)S(1)}, u32[]{:S(2)}, u32[]{:S(2)}) collective-permute-start(bf16[160,512]{1,0:T(8,128)(2,1)S(1)} %pad_maximum_fusion.5), channel_id=1, source_target_pairs={{0,24},{1,97},{2,26},{3,99},{4,28},{5,101},{6,30},{7,103},{8,0},{9... | collective-permute-start | bytes 491528 | tf_op jit(solution)/shard_map/ppermute | solution.py:31
  (1 other events, 1.6 us)

commit v4 on v3

--- a/solution.py
+++ b/solution.py
@@ -211,11 +211,14 @@
 
 def second_kernel(groups, named, numbers, *refs):
     picked, picked_t, *staged = refs[:2] + tuple(ref.at[:, PAIR:] for ref in refs[2:6])
-    query_grad, messages, scratch = refs[7], refs[8:16], refs[16:]
+    query_grad, messages, scratch = refs[7], refs[8:12], refs[12:]
+    share = picked.shape[1] // (SIDE * SIDE)
     for major, second, product in backward(
         numbers, picked, picked_t, *staged, query_grad, scratch, groups, named
     ):
-        messages[second * SIDE + major][...] = product
+        for minor in range(SIDE):
+            to = (2 * minor + second) * share
+            messages[major][to : to + share, :] = product[minor * share : (minor + 1) * share]
 
 
 def attention(numbers, latents, key_weight, value_weight, queries, upstream, query_grad, groups, named):
@@ -253,8 +256,8 @@
     else:
         in_specs.append(pl.BlockSpec(memory_space=pl.ANY))
         inputs.append(query_grad)
-        out_specs += [message(quarter)] * (2 * SIDE)
-        out_shape += [shape((quarter, width // 2), BF16)] * (2 * SIDE)
+        out_specs += [message(2 * quarter)] * SIDE
+        out_shape += [shape((2 * quarter, width // 2), BF16)] * SIDE
         aliases = {len(inputs) - 1: 0}
     return pl.pallas_call(
         functools.partial(first_kernel if first else second_kernel, groups, named),
@@ -272,11 +275,26 @@
     return functools.reduce(jnp.add, [array.astype(F32) for array in arrays])
 
 
-def last_sum(shares, mp):
-    came = [shift(shares[at].astype(BF16), 0, at, mp) for at in (2, 1, 3)]
-    total = add(shares[0], *came)
-    rows = total.shape[0] // 2
-    return total[:rows], total[rows:]
+def last_hop(shares, mp):
+    return [shares[0]] + [shift(shares[at].astype(BF16), 0, at, mp) for at in (2, 1, 3)]
+
+
+def finish_kernel(*refs):
+    *came, key_grad, value_grad = refs
+    rows, width = key_grad.shape[0], key_grad.shape[1] // 2
+    for at in range(2):
+        total = functools.reduce(jnp.add, [ref[...].astype(F32) for ref in came[at * SIDE : (at + 1) * SIDE]])
+        key_grad[:, at * width : (at + 1) * width] = total[:rows]
+        value_grad[:, at * width : (at + 1) * width] = total[rows:]
+
+
+def finish(first, second):
+    rows, width = first[0].shape
+    return pl.pallas_call(
+        finish_kernel,
+        out_shape=[jax.ShapeDtypeStruct((rows // 2, 2 * width), F32)] * 2,
+        compiler_params=pltpu.CompilerParams(vmem_limit_bytes=8 * 1024 * 1024),
+    )(*first, *second)
 
 
 def local(latents, key_weight, value_weight, queries, upstream, gate, media, frame_slot, lengths, *, mp):
@@ -290,23 +308,12 @@
 
     query_grad, *messages = attention(numbers, (picked, picked_t), *rest, query_grad, groups, named)
     rows, messages = lax.optimization_barrier((add(joined[0], *came), messages))
-    key, value = messages[:SIDE], messages[SIDE:]
-    key_far = shift(key[2], 1, 0, mp)
-    value_far = shift(value[2], 3, 0, mp)
-    value_near = shift(value[1], 1, 0, mp)
-    key_near = shift(key[3], 3, 0, mp)
-
+    came = [shift(messages[at], at, 0, mp) for at in (2, 1, 3)]
     share = rows.shape[0] // SIDE
-    first = last_sum([rows[at * share : (at + 1) * share] for at in range(SIDE)], mp)
-
-    key_on = shift(add(key[1], key_far).astype(BF16), 1, 0, mp)
-    value_on = shift(add(value[3], value_far).astype(BF16), 3, 0, mp)
-    key_rows = add(key[0], key_near, key_on)
-    value_rows = add(value[0], value_near, value_on)
-    share //= 2
-    cut = lambda array, at: array[at * share : (at + 1) * share]
-    second = last_sum([jnp.concatenate([cut(key_rows, at), cut(value_rows, at)], axis=0) for at in range(SIDE)], mp)
-    key_grad, value_grad = [jnp.concatenate(halves, axis=1) for halves in zip(first, second)]
+    cut = lambda array: [array[at * share : (at + 1) * share] for at in range(SIDE)]
+    first = last_hop(cut(rows), mp)
+    second = last_hop(cut(add(messages[0], *came)), mp)
+    key_grad, value_grad = finish(first, second)
     return query_grad, key_grad, value_grad
 
 

time: 98.7 us -> 94 us (0.952); the launches traced: 97.2 us -> 94 us
  starting transfers between devices: 39.9 us -> 35.3 us
  waiting for transfers between devices: 20.8 us -> 23 us
  other arithmetic: 3.51 us -> 1.77 us
  Pallas kernels: 29.8 us -> 30.9 us
    ppermute x21 -> x18, starting transfers between devices: 38.9 us -> 34.2 us  [shift(): return lax.ppermute(array, ('seq', 'mp'), pairs)]
    ppermute x21 -> x18, waiting for transfers between devices: 18.8 us -> 21 us  [shift(): return lax.ppermute(array, ('seq', 'mp'), pairs)]
    concatenate x5 -> x0, other arithmetic: 1.53 us -> none  [the longest x2 1.5 us: local(): jnp.concatenate(halves, axis=1)]
  transfers between devices with their start and end apart: 25 -> 22, of which waited for: 12 -> 11; matrix products, arithmetic and copies ran while one was open for 3% -> 3% of each run, Pallas kernels for 18% -> 18%
where the time goes in v4:
time: 94 us
  starting transfers between devices  35.3 us (38%)
  Pallas kernels  30.9 us (33%)
  waiting for transfers between devices  23 us (24%)
  local copies, waits for them, and re-layouts  2.31 us (2%)
  other arithmetic  1.77 us (2%)
    ppermute x18, starting transfers between devices, shift(): return lax.ppermute(array, ('seq', 'mp'), pairs)  34.2 us
    pallas_call x2, Pallas kernels, attention(): pl.pallas_call(functools.partial(first_kernel if first else second_kernel...  23.8 us
    ppermute x18, waiting for transfers between devices, shift(): return lax.ppermute(array, ('seq', 'mp'), pairs)  21 us
    pallas_call x1, Pallas kernels, stage(): pl.pallas_call(functools.partial(stage_kernel, groups, named), in_specs=[...  6.2 us
    ppermute x4, waiting for transfers between devices, swap_cores(): return lax.ppermute(array, 'mp', [(m, m ^ 1) for m in range(mp)])  2.01 us
  transfers between devices with their start and end apart: 22, of which 11 were waited for; matrix products, arithmetic and copies ran while one was open for 3% of the time, Pallas kernels for 18%

profile of v4, /device:TPU:0, one launch (start us, length us, event | category | flops | bytes accessed | tf_op | source)
XLA Modules:
  0.0 94.0 jit_solution(13788158410712421737)
XLA Ops:
  0.6 0.9 %slice_select_fusion = bf16[64,640]{1,0:T(8,128)(2,1)S(1)} fusion(bf16[64,1280]{1,0:T(8,128)(2,1)} %param.9, pred[]{:T(512)S(6)} %eq.6), kind=kLoop, calls=%fused_computation.3 | loop fusion | flops 40960 | bytes 245761 | tf_op jit(solution)/shard_map/jit(_where)/select_n | solution.py:40
  1.6 1.6 %collective-permute-start = (bf16[64,640]{1,0:T(8,128)(2,1)S(1)}, bf16[64,640]{1,0:T(8,128)(2,1)S(1)}, u32[]{:S(2)}, u32[]{:S(2)}) collective-permute-start(bf16[64,640]{1,0:T(8,128)(2,1)S(1)} %slice_select_fusion), channel_id=1, source_target_pairs={{0,32},{1,9},{2,34},{3,11},{4,36},{5,13},{6,38},{7,15},{8,40},{9,1... | collective-permute-start | bytes 245768 | tf_op jit(solution)/shard_map/ppermute | solution.py:31
  3.2 2.7 %collective-permute-start.1 = (bf16[64,640]{1,0:T(8,128)(2,1)S(1)}, bf16[64,640]{1,0:T(8,128)(2,1)S(1)}, u32[]{:S(2)}, u32[]{:S(2)}) collective-permute-start(bf16[64,640]{1,0:T(8,128)(2,1)S(1)} %slice_select_fusion), channel_id=1, source_target_pairs={{0,64},{1,17},{2,66},{3,19},{4,68},{5,21},{6,70},{7,23},{8,72},{9,... | collective-permute-start | bytes 245768 | tf_op jit(solution)/shard_map/ppermute | solution.py:31
  6.0 1.4 %collective-permute-start.2 = (bf16[64,640]{1,0:T(8,128)(2,1)S(1)}, bf16[64,640]{1,0:T(8,128)(2,1)S(1)}, u32[]{:S(2)}, u32[]{:S(2)}) collective-permute-start(bf16[64,640]{1,0:T(8,128)(2,1)S(1)} %slice_select_fusion), channel_id=1, source_target_pairs={{0,96},{1,25},{2,98},{3,27},{4,100},{5,29},{6,102},{7,31},{8,104},... | collective-permute-start | bytes 245768 | tf_op jit(solution)/shard_map/ppermute | solution.py:31
  7.4 0.8 reshape.9
  9.6 0.8 collective-permute-done.2
  10.4 2.0 %collective-permute-start.3 = (bf16[256,640]{1,0:T(8,128)(2,1)S(1)}, bf16[256,640]{1,0:T(8,128)(2,1)S(1)}, u32[]{:S(2)}, u32[]{:S(2)}) collective-permute-start(bf16[256,640]{1,0:T(8,128)(2,1)S(1)} %pad_maximum_fusion.refs_0_), channel_id=1, source_target_pairs={{0,8},{1,33},{2,10},{3,35},{4,12},{5,37},{6,14},{7,39},{8,16},{9,4... | collective-permute-start | bytes 983048 | tf_op jit(solution)/shard_map/ppermute | solution.py:31
  12.4 3.6 %collective-permute-start.4 = (bf16[256,640]{1,0:T(8,128)(2,1)S(1)}, bf16[256,640]{1,0:T(8,128)(2,1)S(1)}, u32[]{:S(2)}, u32[]{:S(2)}) collective-permute-start(bf16[256,640]{1,0:T(8,128)(2,1)S(1)} %pad_maximum_fusion.refs_0_), channel_id=1, source_target_pairs={{0,16},{1,65},{2,18},{3,67},{4,20},{5,69},{6,22},{7,71},{8,24},{9,... | collective-permute-start | bytes 983048 | tf_op jit(solution)/shard_map/ppermute | solution.py:31
  16.0 1.0 %collective-permute-start.5 = (bf16[256,640]{1,0:T(8,128)(2,1)S(1)}, bf16[256,640]{1,0:T(8,128)(2,1)S(1)}, u32[]{:S(2)}, u32[]{:S(2)}) collective-permute-start(bf16[256,640]{1,0:T(8,128)(2,1)S(1)} %pad_maximum_fusion.refs_0_), channel_id=1, source_target_pairs={{0,24},{1,97},{2,26},{3,99},{4,28},{5,101},{6,30},{7,103},{8,0},{9... | collective-permute-start | bytes 983048 | tf_op jit(solution)/shard_map/ppermute | solution.py:31
  17.0 6.2 %shard_map.112 = (bf16[1280,1024]{1,0:T(8,128)(2,1)S(1)}, bf16[1280,1024]{1,0:T(8,128)(2,1)S(1)}, bf16[2048,1024]{1,0:T(8,128)(2,1)S(1)}, bf16[2048,1024]{1,0:T(8,128)(2,1)S(1)}, s32[28]{0:T(128)S(1)}) custom-call(s32[28]{0:T(128)S(1)} %concatenate.7.numbers, f32[1,1024]{1,0:T(1,128)S(1)} %bitcast.3, bf16[1280,1024]{1,0:T(8,128)(2,1)} %key_weight.1, ...), custom_call_target="tpu_custom_call" | custom-call | flops 10000000 | bytes 20000000 | tf_op jit(solution)/shard_map/pallas_call | solution.py:179
  23.2 1.3 %collective-permute-done.4.refs_2_ = bf16[256,640]{1,0:T(8,128)(2,1)S(1)} collective-permute-done((bf16[256,640]{1,0:T(8,128)(2,1)S(1)}, bf16[256,640]{1,0:T(8,128)(2,1)S(1)}, u32[]{:S(2)}, u32[]{:S(2)}) %collective-permute-start.4) | collective-permute-done | bytes 327712 | tf_op jit(solution)/shard_map/ppermute | solution.py:31
  27.6 12.6 %shard_map.113 = (bf16[2048,1024]{1,0:T(8,128)(2,1)}, bf16[640,512]{1,0:T(8,128)(2,1)S(1)}, bf16[640,512]{1,0:T(8,128)(2,1)S(1)}, bf16[640,512]{1,0:T(8,128)(2,1...) custom-call(s32[28]{0:T(128)S(1)} %get-tuple-element.39.numbers, ...), custom_call_target="tpu_custom_call" | custom-call | flops 10000000000 | bytes 10000000 | tf_op jit(solution)/shard_map/pallas_call | solution.py:262
  40.2 3.5 %collective-permute-start.11 = (bf16[640,512]{1,0:T(8,128)(2,1)S(1)}, bf16[640,512]{1,0:T(8,128)(2,1)S(1)}, u32[]{:S(2)}, u32[]{:S(2)}) collective-permute-start(bf16[640,512]{1,0:T(8,128)(2,1)S(1)} %get-tuple-element.54), channel_id=1, source_target_pairs={{0,32},{1,9},{2,34},{3,11},{4,36},{5,13},{6,38},{7,15},{8,40},{9,1... | collective-permute-start | bytes 1966088 | tf_op jit(solution)/shard_map/ppermute | solution.py:31
  43.7 11.1 %shard_map.114 = (bf16[2048,1024]{1,0:T(8,128)(2,1)}, bf16[640,512]{1,0:T(8,128)(2,1)S(1)}, bf16[640,512]{1,0:T(8,128)(2,1)S(1)}, bf16[640,512]{1,0:T(8,128)(2,1)S(1)}, bf16[640,512]{1,0:T(8,128)(2,1)S(1)}) custom-call(s32[28]{0:T(128)S(1)} %get-tuple-element.39.numbers, ...), custom_call_target="tpu_custom_call", output_to_operand_aliasing={{0}: (7, {})} | custom-call | flops 10000000000 | bytes 10000000 | tf_op jit(solution)/shard_map/pallas_call | solution.py:262
  54.9 4.2 %collective-permute-done.11 = bf16[640,512]{1,0:T(8,128)(2,1)S(1)} collective-permute-done((bf16[640,512]{1,0:T(8,128)(2,1)S(1)}, bf16[640,512]{1,0:T(8,128)(2,1)S(1)}, u32[]{:S(2)}, u32[]{:S(2)}) %collective-permute-start.11) | collective-permute-done | bytes 655392 | tf_op jit(solution)/shard_map/ppermute | solution.py:31
  60.4 2.9 %collective-permute-start.17 = (bf16[640,512]{1,0:T(8,128)(2,1)S(1)}, bf16[640,512]{1,0:T(8,128)(2,1)S(1)}, u32[]{:S(2)}, u32[]{:S(2)}) collective-permute-start(bf16[640,512]{1,0:T(8,128)(2,1)S(1)} %get-tuple-element.63), channel_id=1, source_target_pairs={{0,32},{1,9},{2,34},{3,11},{4,36},{5,13},{6,38},{7,15},{8,40},{9,1... | collective-permute-start | bytes 1966088 | tf_op jit(solution)/shard_map/ppermute | solution.py:31
  63.7 5.6 %collective-permute-start.13 = (bf16[160,512]{1,0:T(8,128)(2,1)S(1)}, bf16[160,512]{1,0:T(8,128)(2,1)S(1)}, u32[]{:S(2)}, u32[]{:S(2)}) collective-permute-start(bf16[160,512]{1,0:T(8,128)(2,1)S(1)} %get-tuple-element.74), channel_id=1, source_target_pairs={{0,16},{1,65},{2,18},{3,67},{4,20},{5,69},{6,22},{7,71},{8,24},{9,... | collective-permute-start | bytes 491528 | tf_op jit(solution)/shard_map/ppermute | solution.py:31
  69.3 6.1 %collective-permute-done.16 = bf16[640,512]{1,0:T(8,128)(2,1)S(1)} collective-permute-done((bf16[640,512]{1,0:T(8,128)(2,1)S(1)}, bf16[640,512]{1,0:T(8,128)(2,1)S(1)}, u32[]{:S(2)}, u32[]{:S(2)}) %collective-permute-start.16) | collective-permute-done | bytes 655392 | tf_op jit(solution)/shard_map/ppermute | solution.py:31
  75.5 1.9 %collective-permute-start.15 = (bf16[160,512]{1,0:T(8,128)(2,1)S(1)}, bf16[160,512]{1,0:T(8,128)(2,1)S(1)}, u32[]{:S(2)}, u32[]{:S(2)}) collective-permute-start(bf16[160,512]{1,0:T(8,128)(2,1)S(1)} %get-tuple-element.72), channel_id=1, source_target_pairs={{0,24},{1,97},{2,26},{3,99},{4,28},{5,101},{6,30},{7,103},{8,0},{9... | collective-permute-start | bytes 491528 | tf_op jit(solution)/shard_map/ppermute | solution.py:31
  77.4 5.0 %collective-permute-done.17 = bf16[640,512]{1,0:T(8,128)(2,1)S(1)} collective-permute-done((bf16[640,512]{1,0:T(8,128)(2,1)S(1)}, bf16[640,512]{1,0:T(8,128)(2,1)S(1)}, u32[]{:S(2)}, u32[]{:S(2)}) %collective-permute-start.17) | collective-permute-done | bytes 655392 | tf_op jit(solution)/shard_map/ppermute | solution.py:31
  82.8 3.7 %collective-permute-start.19 = (bf16[160,512]{1,0:T(8,128)(2,1)S(1)}, bf16[160,512]{1,0:T(8,128)(2,1)S(1)}, u32[]{:S(2)}, u32[]{:S(2)}) collective-permute-start(bf16[160,512]{1,0:T(8,128)(2,1)S(1)} %get-tuple-element.71), channel_id=1, source_target_pairs={{0,16},{1,65},{2,18},{3,67},{4,20},{5,69},{6,22},{7,71},{8,24},{9,... | collective-permute-start | bytes 491528 | tf_op jit(solution)/shard_map/ppermute | solution.py:31
  86.5 3.2 %collective-permute-start.21 = (bf16[160,512]{1,0:T(8,128)(2,1)S(1)}, bf16[160,512]{1,0:T(8,128)(2,1)S(1)}, u32[]{:S(2)}, u32[]{:S(2)}) collective-permute-start(bf16[160,512]{1,0:T(8,128)(2,1)S(1)} %get-tuple-element.69), channel_id=1, source_target_pairs={{0,24},{1,97},{2,26},{3,99},{4,28},{5,101},{6,30},{7,103},{8,0},{9... | collective-permute-start | bytes 491528 | tf_op jit(solution)/shard_map/ppermute | solution.py:31
  89.9 3.2 %collective-permute-done.20.refs_6_ = bf16[160,512]{1,0:T(8,128)(2,1)S(1)} collective-permute-done((bf16[160,512]{1,0:T(8,128)(2,1)S(1)}, bf16[160,512]{1,0:T(8,128)(2,1)S(1)}, u32[]{:S(2)}, u32[]{:S(2)}) %collective-permute-start.20) | collective-permute-done | bytes 163872 | tf_op jit(solution)/shard_map/ppermute | solution.py:31
  93.1 0.9 shard_map.115
  (36 shorter events, 6.8 us)
Async XLA Ops:
  1.6 8.0 %collective-permute-start = (bf16[64,640]{1,0:T(8,128)(2,1)S(1)}, bf16[64,640]{1,0:T(8,128)(2,1)S(1)}, u32[]{:S(2)}, u32[]{:S(2)}) collective-permute-start(bf16[64,640]{1,0:T(8,128)(2,1)S(1)} %slice_select_fusion), channel_id=1, source_target_pairs={{0,32},{1,9},{2,34},{3,11},{4,36},{5,13},{6,38},{7,15},{8,40},{9,1... | collective-permute-start | bytes 245768 | tf_op jit(solution)/shard_map/ppermute | solution.py:31
  3.2 6.4 %collective-permute-start.1 = (bf16[64,640]{1,0:T(8,128)(2,1)S(1)}, bf16[64,640]{1,0:T(8,128)(2,1)S(1)}, u32[]{:S(2)}, u32[]{:S(2)}) collective-permute-start(bf16[64,640]{1,0:T(8,128)(2,1)S(1)} %slice_select_fusion), channel_id=1, source_target_pairs={{0,64},{1,17},{2,66},{3,19},{4,68},{5,21},{6,70},{7,23},{8,72},{9,... | collective-permute-start | bytes 245768 | tf_op jit(solution)/shard_map/ppermute | solution.py:31
  6.0 4.4 %collective-permute-start.2 = (bf16[64,640]{1,0:T(8,128)(2,1)S(1)}, bf16[64,640]{1,0:T(8,128)(2,1)S(1)}, u32[]{:S(2)}, u32[]{:S(2)}) collective-permute-start(bf16[64,640]{1,0:T(8,128)(2,1)S(1)} %slice_select_fusion), channel_id=1, source_target_pairs={{0,96},{1,25},{2,98},{3,27},{4,100},{5,29},{6,102},{7,31},{8,104},... | collective-permute-start | bytes 245768 | tf_op jit(solution)/shard_map/ppermute | solution.py:31
  10.4 12.8 %collective-permute-start.3 = (bf16[256,640]{1,0:T(8,128)(2,1)S(1)}, bf16[256,640]{1,0:T(8,128)(2,1)S(1)}, u32[]{:S(2)}, u32[]{:S(2)}) collective-permute-start(bf16[256,640]{1,0:T(8,128)(2,1)S(1)} %pad_maximum_fusion.refs_0_), channel_id=1, source_target_pairs={{0,8},{1,33},{2,10},{3,35},{4,12},{5,37},{6,14},{7,39},{8,16},{9,4... | collective-permute-start | bytes 983048 | tf_op jit(solution)/shard_map/ppermute | solution.py:31
  12.4 12.1 %collective-permute-start.4 = (bf16[256,640]{1,0:T(8,128)(2,1)S(1)}, bf16[256,640]{1,0:T(8,128)(2,1)S(1)}, u32[]{:S(2)}, u32[]{:S(2)}) collective-permute-start(bf16[256,640]{1,0:T(8,128)(2,1)S(1)} %pad_maximum_fusion.refs_0_), channel_id=1, source_target_pairs={{0,16},{1,65},{2,18},{3,67},{4,20},{5,69},{6,22},{7,71},{8,24},{9,... | collective-permute-start | bytes 983048 | tf_op jit(solution)/shard_map/ppermute | solution.py:31
  16.0 8.6 %collective-permute-start.5 = (bf16[256,640]{1,0:T(8,128)(2,1)S(1)}, bf16[256,640]{1,0:T(8,128)(2,1)S(1)}, u32[]{:S(2)}, u32[]{:S(2)}) collective-permute-start(bf16[256,640]{1,0:T(8,128)(2,1)S(1)} %pad_maximum_fusion.refs_0_), channel_id=1, source_target_pairs={{0,24},{1,97},{2,26},{3,99},{4,28},{5,101},{6,30},{7,103},{8,0},{9... | collective-permute-start | bytes 983048 | tf_op jit(solution)/shard_map/ppermute | solution.py:31
  24.6 1.6 %collective-permute-start.6 = (bf16[256,640]{1,0:T(8,128)(2,1)S(1)}, bf16[256,640]{1,0:T(8,128)(2,1)S(1)}, u32[]{:S(2)}, u32[]{:S(2)}) collective-permute-start(bf16[256,640]{1,0:T(8,128)(2,1)S(1)} %pad_maximum_fusion.refs_0_), channel_id=1, source_target_pairs={{0,1},{1,0},{2,3},{3,2},{4,5},{5,4},{6,7},{7,6},{8,9},{9,8},{10,11... | collective-permute-start | bytes 983048 | tf_op jit(solution)/shard_map/ppermute | solution.py:35
  24.6 2.1 %collective-permute-start.7 = (bf16[256,640]{1,0:T(8,128)(2,1)S(1)}, bf16[256,640]{1,0:T(8,128)(2,1)S(1)}, u32[]{:S(2)}, u32[]{:S(2)}) collective-permute-start(bf16[256,640]{1,0:T(8,128)(2,1)S(1)} %collective-permute-done.3.refs_1_), channel_id=1, source_target_pairs={{0,1},{1,0},{2,3},{3,2},{4,5},{5,4},{6,7},{7,6},{8,9},{9,8},{10,11... | collective-permute-start | bytes 983048 | tf_op jit(solution)/shard_map/ppermute | solution.py:35
  25.1 2.1 %collective-permute-start.8 = (bf16[256,640]{1,0:T(8,128)(2,1)S(1)}, bf16[256,640]{1,0:T(8,128)(2,1)S(1)}, u32[]{:S(2)}, u32[]{:S(2)}) collective-permute-start(bf16[256,640]{1,0:T(8,128)(2,1)S(1)} %collective-permute-done.4.refs_2_), channel_id=1, source_target_pairs={{0,1},{1,0},{2,3},{3,2},{4,5},{5,4},{6,7},{7,6},{8,9},{9,8},{10,11... | collective-permute-start | bytes 983048 | tf_op jit(solution)/shard_map/ppermute | solution.py:35
  25.1 2.5 %collective-permute-start.9 = (bf16[256,640]{1,0:T(8,128)(2,1)S(1)}, bf16[256,640]{1,0:T(8,128)(2,1)S(1)}, u32[]{:S(2)}, u32[]{:S(2)}) collective-permute-start(bf16[256,640]{1,0:T(8,128)(2,1)S(1)} %collective-permute-done.5.refs_3_), channel_id=1, source_target_pairs={{0,1},{1,0},{2,3},{3,2},{4,5},{5,4},{6,7},{7,6},{8,9},{9,8},{10,11... | collective-permute-start | bytes 983048 | tf_op jit(solution)/shard_map/ppermute | solution.py:35
  40.2 14.7 %collective-permute-start.10 = (bf16[640,512]{1,0:T(8,128)(2,1)S(1)}, bf16[640,512]{1,0:T(8,128)(2,1)S(1)}, u32[]{:S(2)}, u32[]{:S(2)}) collective-permute-start(bf16[640,512]{1,0:T(8,128)(2,1)S(1)} %get-tuple-element.53), channel_id=1, source_target_pairs={{0,64},{1,17},{2,66},{3,19},{4,68},{5,21},{6,70},{7,23},{8,72},{9,... | collective-permute-start | bytes 1966088 | tf_op jit(solution)/shard_map/ppermute | solution.py:31
  40.2 18.8 %collective-permute-start.11 = (bf16[640,512]{1,0:T(8,128)(2,1)S(1)}, bf16[640,512]{1,0:T(8,128)(2,1)S(1)}, u32[]{:S(2)}, u32[]{:S(2)}) collective-permute-start(bf16[640,512]{1,0:T(8,128)(2,1)S(1)} %get-tuple-element.54), channel_id=1, source_target_pairs={{0,32},{1,9},{2,34},{3,11},{4,36},{5,13},{6,38},{7,15},{8,40},{9,1... | collective-permute-start | bytes 1966088 | tf_op jit(solution)/shard_map/ppermute | solution.py:31
  43.7 15.6 %collective-permute-start.12 = (bf16[640,512]{1,0:T(8,128)(2,1)S(1)}, bf16[640,512]{1,0:T(8,128)(2,1)S(1)}, u32[]{:S(2)}, u32[]{:S(2)}) collective-permute-start(bf16[640,512]{1,0:T(8,128)(2,1)S(1)} %get-tuple-element.55), channel_id=1, source_target_pairs={{0,96},{1,25},{2,98},{3,27},{4,100},{5,29},{6,102},{7,31},{8,104},... | collective-permute-start | bytes 1966088 | tf_op jit(solution)/shard_map/ppermute | solution.py:31
  59.7 15.8 %collective-permute-start.16 = (bf16[640,512]{1,0:T(8,128)(2,1)S(1)}, bf16[640,512]{1,0:T(8,128)(2,1)S(1)}, u32[]{:S(2)}, u32[]{:S(2)}) collective-permute-start(bf16[640,512]{1,0:T(8,128)(2,1)S(1)} %get-tuple-element.62), channel_id=1, source_target_pairs={{0,64},{1,17},{2,66},{3,19},{4,68},{5,21},{6,70},{7,23},{8,72},{9,... | collective-permute-start | bytes 1966088 | tf_op jit(solution)/shard_map/ppermute | solution.py:31
  60.4 22.0 %collective-permute-start.17 = (bf16[640,512]{1,0:T(8,128)(2,1)S(1)}, bf16[640,512]{1,0:T(8,128)(2,1)S(1)}, u32[]{:S(2)}, u32[]{:S(2)}) collective-permute-start(bf16[640,512]{1,0:T(8,128)(2,1)S(1)} %get-tuple-element.63), channel_id=1, source_target_pairs={{0,32},{1,9},{2,34},{3,11},{4,36},{5,13},{6,38},{7,15},{8,40},{9,1... | collective-permute-start | bytes 1966088 | tf_op jit(solution)/shard_map/ppermute | solution.py:31
  63.3 19.1 %collective-permute-start.18 = (bf16[640,512]{1,0:T(8,128)(2,1)S(1)}, bf16[640,512]{1,0:T(8,128)(2,1)S(1)}, u32[]{:S(2)}, u32[]{:S(2)}) collective-permute-start(bf16[640,512]{1,0:T(8,128)(2,1)S(1)} %get-tuple-element.64), channel_id=1, source_target_pairs={{0,96},{1,25},{2,98},{3,27},{4,100},{5,29},{6,102},{7,31},{8,104},... | collective-permute-start | bytes 1966088 | tf_op jit(solution)/shard_map/ppermute | solution.py:31
  63.7 22.8 %collective-permute-start.13 = (bf16[160,512]{1,0:T(8,128)(2,1)S(1)}, bf16[160,512]{1,0:T(8,128)(2,1)S(1)}, u32[]{:S(2)}, u32[]{:S(2)}) collective-permute-start(bf16[160,512]{1,0:T(8,128)(2,1)S(1)} %get-tuple-element.74), channel_id=1, source_target_pairs={{0,16},{1,65},{2,18},{3,67},{4,20},{5,69},{6,22},{7,71},{8,24},{9,... | collective-permute-start | bytes 491528 | tf_op jit(solution)/shard_map/ppermute | solution.py:31
  69.3 20.5 %collective-permute-start.14 = (bf16[160,512]{1,0:T(8,128)(2,1)S(1)}, bf16[160,512]{1,0:T(8,128)(2,1)S(1)}, u32[]{:S(2)}, u32[]{:S(2)}) collective-permute-start(bf16[160,512]{1,0:T(8,128)(2,1)S(1)} %get-tuple-element.73), channel_id=1, source_target_pairs={{0,8},{1,33},{2,10},{3,35},{4,12},{5,37},{6,14},{7,39},{8,16},{9,4... | collective-permute-start | bytes 491528 | tf_op jit(solution)/shard_map/ppermute | solution.py:31
  75.5 14.4 %collective-permute-start.15 = (bf16[160,512]{1,0:T(8,128)(2,1)S(1)}, bf16[160,512]{1,0:T(8,128)(2,1)S(1)}, u32[]{:S(2)}, u32[]{:S(2)}) collective-permute-start(bf16[160,512]{1,0:T(8,128)(2,1)S(1)} %get-tuple-element.72), channel_id=1, source_target_pairs={{0,24},{1,97},{2,26},{3,99},{4,28},{5,101},{6,30},{7,103},{8,0},{9... | collective-permute-start | bytes 491528 | tf_op jit(solution)/shard_map/ppermute | solution.py:31
  82.8 7.0 %collective-permute-start.19 = (bf16[160,512]{1,0:T(8,128)(2,1)S(1)}, bf16[160,512]{1,0:T(8,128)(2,1)S(1)}, u32[]{:S(2)}, u32[]{:S(2)}) collective-permute-start(bf16[160,512]{1,0:T(8,128)(2,1)S(1)} %get-tuple-element.71), channel_id=1, source_target_pairs={{0,16},{1,65},{2,18},{3,67},{4,20},{5,69},{6,22},{7,71},{8,24},{9,... | collective-permute-start | bytes 491528 | tf_op jit(solution)/shard_map/ppermute | solution.py:31
  86.5 6.5 %collective-permute-start.20 = (bf16[160,512]{1,0:T(8,128)(2,1)S(1)}, bf16[160,512]{1,0:T(8,128)(2,1)S(1)}, u32[]{:S(2)}, u32[]{:S(2)}) collective-permute-start(bf16[160,512]{1,0:T(8,128)(2,1)S(1)} %get-tuple-element.70), channel_id=1, source_target_pairs={{0,8},{1,33},{2,10},{3,35},{4,12},{5,37},{6,14},{7,39},{8,16},{9,4... | collective-permute-start | bytes 491528 | tf_op jit(solution)/shard_map/ppermute | solution.py:31
  86.5 6.5 %collective-permute-start.21 = (bf16[160,512]{1,0:T(8,128)(2,1)S(1)}, bf16[160,512]{1,0:T(8,128)(2,1)S(1)}, u32[]{:S(2)}, u32[]{:S(2)}) collective-permute-start(bf16[160,512]{1,0:T(8,128)(2,1)S(1)} %get-tuple-element.69), channel_id=1, source_target_pairs={{0,24},{1,97},{2,26},{3,99},{4,28},{5,101},{6,30},{7,103},{8,0},{9... | collective-permute-start | bytes 491528 | tf_op jit(solution)/shard_map/ppermute | solution.py:31

commit v5 on v4

--- a/solution.py
+++ b/solution.py
@@ -13,7 +13,7 @@
 SIDE = 4
 HEADS = 4
 PAIR = HEADS * HEAD_DIM
-TOKEN_BLOCK = 256
+TOKEN_BLOCK = 512
 ONES = (((1,), (1,)), ((), ()))
 ZEROS = (((0,), (0,)), ((), ()))
 BF16 = jnp.bfloat16

time: 94 us -> 94.5 us (level); the launches traced: 94 us -> 92.8 us
  starting transfers between devices: 35.3 us -> 40.5 us
  Pallas kernels: 30.9 us -> 26 us
  waiting for transfers between devices: 23 us -> 21.4 us
    ppermute x18, starting transfers between devices: 34.2 us -> 39.5 us  [shift(): return lax.ppermute(array, ('seq', 'mp'), pairs)]
    pallas_call x2, Pallas kernels: 23.8 us -> 18.9 us  [attention(): pl.pallas_call(functools.partial(first_kernel if first else second_kernel...]
    ppermute x18, waiting for transfers between devices: 21 us -> 19.4 us  [shift(): return lax.ppermute(array, ('seq', 'mp'), pairs)]
  transfers between devices with their start and end apart: 22 -> 22, of which waited for: 11 -> 11; matrix products, arithmetic and copies ran while one was open for 3% -> 3% of each run, Pallas kernels for 18% -> 16%
where the time goes in v5:
time: 94.5 us; the launch traced here: 92.8 us
  starting transfers between devices  40.5 us (43%)
  Pallas kernels  26 us (28%)
  waiting for transfers between devices  21.4 us (23%)
  local copies, waits for them, and re-layouts  2.31 us (2%)
  other arithmetic  1.77 us (2%)
    ppermute x18, starting transfers between devices, shift(): return lax.ppermute(array, ('seq', 'mp'), pairs)  39.5 us
    ppermute x18, waiting for transfers between devices, shift(): return lax.ppermute(array, ('seq', 'mp'), pairs)  19.4 us
    pallas_call x2, Pallas kernels, attention(): pl.pallas_call(functools.partial(first_kernel if first else second_kernel...  18.9 us
    pallas_call x1, Pallas kernels, stage(): pl.pallas_call(functools.partial(stage_kernel, groups, named), in_specs=[...  6.2 us
    ppermute x4, waiting for transfers between devices, swap_cores(): return lax.ppermute(array, 'mp', [(m, m ^ 1) for m in range(mp)])  2.01 us
  transfers between devices with their start and end apart: 22, of which 11 were waited for; matrix products, arithmetic and copies ran while one was open for 3% of the time, Pallas kernels for 16%

profile of v5, /device:TPU:0, one launch (start us, length us, event | category | flops | bytes accessed | tf_op | source)
XLA Modules:
  0.0 92.8 jit_solution(3525117041032817424)
XLA Ops:
  1.6 1.6 %collective-permute-start = (bf16[64,640]{1,0:T(8,128)(2,1)S(1)}, bf16[64,640]{1,0:T(8,128)(2,1)S(1)}, u32[]{:S(2)}, u32[]{:S(2)}) collective-permute-start(bf16[64,640]{1,0:T(8,128)(2,1)S(1)} %slice_select_fusion), channel_id=1, source_target_pairs={{0,32},{1,9},{2,34},{3,11},{4,36},{5,13},{6,38},{7,15},{8,40},{9,1... | collective-permute-start | bytes 245768 | tf_op jit(solution)/shard_map/ppermute | solution.py:31
  3.2 2.7 %collective-permute-start.1 = (bf16[64,640]{1,0:T(8,128)(2,1)S(1)}, bf16[64,640]{1,0:T(8,128)(2,1)S(1)}, u32[]{:S(2)}, u32[]{:S(2)}) collective-permute-start(bf16[64,640]{1,0:T(8,128)(2,1)S(1)} %slice_select_fusion), channel_id=1, source_target_pairs={{0,64},{1,17},{2,66},{3,19},{4,68},{5,21},{6,70},{7,23},{8,72},{9,... | collective-permute-start | bytes 245768 | tf_op jit(solution)/shard_map/ppermute | solution.py:31
  6.0 1.4 %collective-permute-start.2 = (bf16[64,640]{1,0:T(8,128)(2,1)S(1)}, bf16[64,640]{1,0:T(8,128)(2,1)S(1)}, u32[]{:S(2)}, u32[]{:S(2)}) collective-permute-start(bf16[64,640]{1,0:T(8,128)(2,1)S(1)} %slice_select_fusion), channel_id=1, source_target_pairs={{0,96},{1,25},{2,98},{3,27},{4,100},{5,29},{6,102},{7,31},{8,104},... | collective-permute-start | bytes 245768 | tf_op jit(solution)/shard_map/ppermute | solution.py:31
  10.4 2.0 %collective-permute-start.3 = (bf16[256,640]{1,0:T(8,128)(2,1)S(1)}, bf16[256,640]{1,0:T(8,128)(2,1)S(1)}, u32[]{:S(2)}, u32[]{:S(2)}) collective-permute-start(bf16[256,640]{1,0:T(8,128)(2,1)S(1)} %pad_maximum_fusion.refs_0_), channel_id=1, source_target_pairs={{0,8},{1,33},{2,10},{3,35},{4,12},{5,37},{6,14},{7,39},{8,16},{9,4... | collective-permute-start | bytes 983048 | tf_op jit(solution)/shard_map/ppermute | solution.py:31
  12.4 3.6 %collective-permute-start.4 = (bf16[256,640]{1,0:T(8,128)(2,1)S(1)}, bf16[256,640]{1,0:T(8,128)(2,1)S(1)}, u32[]{:S(2)}, u32[]{:S(2)}) collective-permute-start(bf16[256,640]{1,0:T(8,128)(2,1)S(1)} %pad_maximum_fusion.refs_0_), channel_id=1, source_target_pairs={{0,16},{1,65},{2,18},{3,67},{4,20},{5,69},{6,22},{7,71},{8,24},{9,... | collective-permute-start | bytes 983048 | tf_op jit(solution)/shard_map/ppermute | solution.py:31
  16.0 1.0 %collective-permute-start.5 = (bf16[256,640]{1,0:T(8,128)(2,1)S(1)}, bf16[256,640]{1,0:T(8,128)(2,1)S(1)}, u32[]{:S(2)}, u32[]{:S(2)}) collective-permute-start(bf16[256,640]{1,0:T(8,128)(2,1)S(1)} %pad_maximum_fusion.refs_0_), channel_id=1, source_target_pairs={{0,24},{1,97},{2,26},{3,99},{4,28},{5,101},{6,30},{7,103},{8,0},{9... | collective-permute-start | bytes 983048 | tf_op jit(solution)/shard_map/ppermute | solution.py:31
  17.0 6.2 %shard_map.112 = (bf16[1280,1024]{1,0:T(8,128)(2,1)S(1)}, bf16[1280,1024]{1,0:T(8,128)(2,1)S(1)}, bf16[2048,1024]{1,0:T(8,128)(2,1)S(1)}, bf16[2048,1024]{1,0:T(8,128)(2,1)S(1)}, s32[28]{0:T(128)S(1)}) custom-call(s32[28]{0:T(128)S(1)} %concatenate.7.numbers, f32[1,1024]{1,0:T(1,128)S(1)} %bitcast.3, bf16[1280,1024]{1,0:T(8,128)(2,1)} %key_weight.1, ...), custom_call_target="tpu_custom_call" | custom-call | flops 10000000 | bytes 20000000 | tf_op jit(solution)/shard_map/pallas_call | solution.py:179
  23.2 1.3 %collective-permute-done.4.refs_2_ = bf16[256,640]{1,0:T(8,128)(2,1)S(1)} collective-permute-done((bf16[256,640]{1,0:T(8,128)(2,1)S(1)}, bf16[256,640]{1,0:T(8,128)(2,1)S(1)}, u32[]{:S(2)}, u32[]{:S(2)}) %collective-permute-start.4) | collective-permute-done | bytes 327712 | tf_op jit(solution)/shard_map/ppermute | solution.py:31
  27.6 10.3 %shard_map.113 = (bf16[2048,1024]{1,0:T(8,128)(2,1)}, bf16[640,512]{1,0:T(8,128)(2,1)S(1)}, bf16[640,512]{1,0:T(8,128)(2,1)S(1)}, bf16[640,512]{1,0:T(8,128)(2,1...) custom-call(s32[28]{0:T(128)S(1)} %get-tuple-element.39.numbers, ...), custom_call_target="tpu_custom_call" | custom-call | flops 10000000000 | bytes 10000000 | tf_op jit(solution)/shard_map/pallas_call | solution.py:262
  37.9 5.9 %collective-permute-start.10 = (bf16[640,512]{1,0:T(8,128)(2,1)S(1)}, bf16[640,512]{1,0:T(8,128)(2,1)S(1)}, u32[]{:S(2)}, u32[]{:S(2)}) collective-permute-start(bf16[640,512]{1,0:T(8,128)(2,1)S(1)} %get-tuple-element.53), channel_id=1, source_target_pairs={{0,64},{1,17},{2,66},{3,19},{4,68},{5,21},{6,70},{7,23},{8,72},{9,... | collective-permute-start | bytes 1966088 | tf_op jit(solution)/shard_map/ppermute | solution.py:31
  43.8 3.2 %collective-permute-start.12 = (bf16[640,512]{1,0:T(8,128)(2,1)S(1)}, bf16[640,512]{1,0:T(8,128)(2,1)S(1)}, u32[]{:S(2)}, u32[]{:S(2)}) collective-permute-start(bf16[640,512]{1,0:T(8,128)(2,1)S(1)} %get-tuple-element.55), channel_id=1, source_target_pairs={{0,96},{1,25},{2,98},{3,27},{4,100},{5,29},{6,102},{7,31},{8,104},... | collective-permute-start | bytes 1966088 | tf_op jit(solution)/shard_map/ppermute | solution.py:31
  47.0 8.6 %shard_map.114 = (bf16[2048,1024]{1,0:T(8,128)(2,1)}, bf16[640,512]{1,0:T(8,128)(2,1)S(1)}, bf16[640,512]{1,0:T(8,128)(2,1)S(1)}, bf16[640,512]{1,0:T(8,128)(2,1)S(1)}, bf16[640,512]{1,0:T(8,128)(2,1)S(1)}) custom-call(s32[28]{0:T(128)S(1)} %get-tuple-element.39.numbers, ...), custom_call_target="tpu_custom_call", output_to_operand_aliasing={{0}: (7, {})} | custom-call | flops 10000000000 | bytes 10000000 | tf_op jit(solution)/shard_map/pallas_call | solution.py:262
  55.6 3.7 %collective-permute-done.11 = bf16[640,512]{1,0:T(8,128)(2,1)S(1)} collective-permute-done((bf16[640,512]{1,0:T(8,128)(2,1)S(1)}, bf16[640,512]{1,0:T(8,128)(2,1)S(1)}, u32[]{:S(2)}, u32[]{:S(2)}) %collective-permute-start.11) | collective-permute-done | bytes 655392 | tf_op jit(solution)/shard_map/ppermute | solution.py:31
  59.7 2.1 %collective-permute-start.16 = (bf16[640,512]{1,0:T(8,128)(2,1)S(1)}, bf16[640,512]{1,0:T(8,128)(2,1)S(1)}, u32[]{:S(2)}, u32[]{:S(2)}) collective-permute-start(bf16[640,512]{1,0:T(8,128)(2,1)S(1)} %get-tuple-element.62), channel_id=1, source_target_pairs={{0,64},{1,17},{2,66},{3,19},{4,68},{5,21},{6,70},{7,23},{8,72},{9,... | collective-permute-start | bytes 1966088 | tf_op jit(solution)/shard_map/ppermute | solution.py:31
  61.8 1.2 %collective-permute-start.17 = (bf16[640,512]{1,0:T(8,128)(2,1)S(1)}, bf16[640,512]{1,0:T(8,128)(2,1)S(1)}, u32[]{:S(2)}, u32[]{:S(2)}) collective-permute-start(bf16[640,512]{1,0:T(8,128)(2,1)S(1)} %get-tuple-element.63), channel_id=1, source_target_pairs={{0,32},{1,9},{2,34},{3,11},{4,36},{5,13},{6,38},{7,15},{8,40},{9,1... | collective-permute-start | bytes 1966088 | tf_op jit(solution)/shard_map/ppermute | solution.py:31
  63.0 2.0 %collective-permute-start.18 = (bf16[640,512]{1,0:T(8,128)(2,1)S(1)}, bf16[640,512]{1,0:T(8,128)(2,1)S(1)}, u32[]{:S(2)}, u32[]{:S(2)}) collective-permute-start(bf16[640,512]{1,0:T(8,128)(2,1)S(1)} %get-tuple-element.64), channel_id=1, source_target_pairs={{0,96},{1,25},{2,98},{3,27},{4,100},{5,29},{6,102},{7,31},{8,104},... | collective-permute-start | bytes 1966088 | tf_op jit(solution)/shard_map/ppermute | solution.py:31
  65.1 3.7 %collective-permute-start.13 = (bf16[160,512]{1,0:T(8,128)(2,1)S(1)}, bf16[160,512]{1,0:T(8,128)(2,1)S(1)}, u32[]{:S(2)}, u32[]{:S(2)}) collective-permute-start(bf16[160,512]{1,0:T(8,128)(2,1)S(1)} %get-tuple-element.74), channel_id=1, source_target_pairs={{0,16},{1,65},{2,18},{3,67},{4,20},{5,69},{6,22},{7,71},{8,24},{9,... | collective-permute-start | bytes 491528 | tf_op jit(solution)/shard_map/ppermute | solution.py:31
  68.9 5.4 %collective-permute-done.16 = bf16[640,512]{1,0:T(8,128)(2,1)S(1)} collective-permute-done((bf16[640,512]{1,0:T(8,128)(2,1)S(1)}, bf16[640,512]{1,0:T(8,128)(2,1)S(1)}, u32[]{:S(2)}, u32[]{:S(2)}) %collective-permute-start.16) | collective-permute-done | bytes 655392 | tf_op jit(solution)/shard_map/ppermute | solution.py:31
  74.3 3.2 %collective-permute-start.15 = (bf16[160,512]{1,0:T(8,128)(2,1)S(1)}, bf16[160,512]{1,0:T(8,128)(2,1)S(1)}, u32[]{:S(2)}, u32[]{:S(2)}) collective-permute-start(bf16[160,512]{1,0:T(8,128)(2,1)S(1)} %get-tuple-element.72), channel_id=1, source_target_pairs={{0,24},{1,97},{2,26},{3,99},{4,28},{5,101},{6,30},{7,103},{8,0},{9... | collective-permute-start | bytes 491528 | tf_op jit(solution)/shard_map/ppermute | solution.py:31
  77.5 4.9 %collective-permute-done.17 = bf16[640,512]{1,0:T(8,128)(2,1)S(1)} collective-permute-done((bf16[640,512]{1,0:T(8,128)(2,1)S(1)}, bf16[640,512]{1,0:T(8,128)(2,1)S(1)}, u32[]{:S(2)}, u32[]{:S(2)}) %collective-permute-start.17) | collective-permute-done | bytes 655392 | tf_op jit(solution)/shard_map/ppermute | solution.py:31
  82.8 2.3 %collective-permute-start.19 = (bf16[160,512]{1,0:T(8,128)(2,1)S(1)}, bf16[160,512]{1,0:T(8,128)(2,1)S(1)}, u32[]{:S(2)}, u32[]{:S(2)}) collective-permute-start(bf16[160,512]{1,0:T(8,128)(2,1)S(1)} %get-tuple-element.71), channel_id=1, source_target_pairs={{0,16},{1,65},{2,18},{3,67},{4,20},{5,69},{6,22},{7,71},{8,24},{9,... | collective-permute-start | bytes 491528 | tf_op jit(solution)/shard_map/ppermute | solution.py:31
  86.0 2.6 %collective-permute-start.21 = (bf16[160,512]{1,0:T(8,128)(2,1)S(1)}, bf16[160,512]{1,0:T(8,128)(2,1)S(1)}, u32[]{:S(2)}, u32[]{:S(2)}) collective-permute-start(bf16[160,512]{1,0:T(8,128)(2,1)S(1)} %get-tuple-element.69), channel_id=1, source_target_pairs={{0,24},{1,97},{2,26},{3,99},{4,28},{5,101},{6,30},{7,103},{8,0},{9... | collective-permute-start | bytes 491528 | tf_op jit(solution)/shard_map/ppermute | solution.py:31
  88.7 1.1 %collective-permute-done.19.refs_5_ = bf16[160,512]{1,0:T(8,128)(2,1)S(1)} collective-permute-done((bf16[160,512]{1,0:T(8,128)(2,1)S(1)}, bf16[160,512]{1,0:T(8,128)(2,1)S(1)}, u32[]{:S(2)}, u32[]{:S(2)}) %collective-permute-start.19) | collective-permute-done | bytes 163872 | tf_op jit(solution)/shard_map/ppermute | solution.py:31
  89.7 2.1 %collective-permute-done.20.refs_6_ = bf16[160,512]{1,0:T(8,128)(2,1)S(1)} collective-permute-done((bf16[160,512]{1,0:T(8,128)(2,1)S(1)}, bf16[160,512]{1,0:T(8,128)(2,1)S(1)}, u32[]{:S(2)}, u32[]{:S(2)}) %collective-permute-start.20) | collective-permute-done | bytes 163872 | tf_op jit(solution)/shard_map/ppermute | solution.py:31
  (36 shorter events, 9.7 us)
Async XLA Ops:
  1.6 8.0 %collective-permute-start = (bf16[64,640]{1,0:T(8,128)(2,1)S(1)}, bf16[64,640]{1,0:T(8,128)(2,1)S(1)}, u32[]{:S(2)}, u32[]{:S(2)}) collective-permute-start(bf16[64,640]{1,0:T(8,128)(2,1)S(1)} %slice_select_fusion), channel_id=1, source_target_pairs={{0,32},{1,9},{2,34},{3,11},{4,36},{5,13},{6,38},{7,15},{8,40},{9,1... | collective-permute-start | bytes 245768 | tf_op jit(solution)/shard_map/ppermute | solution.py:31
  3.2 6.4 %collective-permute-start.1 = (bf16[64,640]{1,0:T(8,128)(2,1)S(1)}, bf16[64,640]{1,0:T(8,128)(2,1)S(1)}, u32[]{:S(2)}, u32[]{:S(2)}) collective-permute-start(bf16[64,640]{1,0:T(8,128)(2,1)S(1)} %slice_select_fusion), channel_id=1, source_target_pairs={{0,64},{1,17},{2,66},{3,19},{4,68},{5,21},{6,70},{7,23},{8,72},{9,... | collective-permute-start | bytes 245768 | tf_op jit(solution)/shard_map/ppermute | solution.py:31
  6.0 4.4 %collective-permute-start.2 = (bf16[64,640]{1,0:T(8,128)(2,1)S(1)}, bf16[64,640]{1,0:T(8,128)(2,1)S(1)}, u32[]{:S(2)}, u32[]{:S(2)}) collective-permute-start(bf16[64,640]{1,0:T(8,128)(2,1)S(1)} %slice_select_fusion), channel_id=1, source_target_pairs={{0,96},{1,25},{2,98},{3,27},{4,100},{5,29},{6,102},{7,31},{8,104},... | collective-permute-start | bytes 245768 | tf_op jit(solution)/shard_map/ppermute | solution.py:31
  10.4 12.8 %collective-permute-start.3 = (bf16[256,640]{1,0:T(8,128)(2,1)S(1)}, bf16[256,640]{1,0:T(8,128)(2,1)S(1)}, u32[]{:S(2)}, u32[]{:S(2)}) collective-permute-start(bf16[256,640]{1,0:T(8,128)(2,1)S(1)} %pad_maximum_fusion.refs_0_), channel_id=1, source_target_pairs={{0,8},{1,33},{2,10},{3,35},{4,12},{5,37},{6,14},{7,39},{8,16},{9,4... | collective-permute-start | bytes 983048 | tf_op jit(solution)/shard_map/ppermute | solution.py:31
  12.4 12.1 %collective-permute-start.4 = (bf16[256,640]{1,0:T(8,128)(2,1)S(1)}, bf16[256,640]{1,0:T(8,128)(2,1)S(1)}, u32[]{:S(2)}, u32[]{:S(2)}) collective-permute-start(bf16[256,640]{1,0:T(8,128)(2,1)S(1)} %pad_maximum_fusion.refs_0_), channel_id=1, source_target_pairs={{0,16},{1,65},{2,18},{3,67},{4,20},{5,69},{6,22},{7,71},{8,24},{9,... | collective-permute-start | bytes 983048 | tf_op jit(solution)/shard_map/ppermute | solution.py:31
  16.0 8.6 %collective-permute-start.5 = (bf16[256,640]{1,0:T(8,128)(2,1)S(1)}, bf16[256,640]{1,0:T(8,128)(2,1)S(1)}, u32[]{:S(2)}, u32[]{:S(2)}) collective-permute-start(bf16[256,640]{1,0:T(8,128)(2,1)S(1)} %pad_maximum_fusion.refs_0_), channel_id=1, source_target_pairs={{0,24},{1,97},{2,26},{3,99},{4,28},{5,101},{6,30},{7,103},{8,0},{9... | collective-permute-start | bytes 983048 | tf_op jit(solution)/shard_map/ppermute | solution.py:31
  24.6 1.6 %collective-permute-start.6 = (bf16[256,640]{1,0:T(8,128)(2,1)S(1)}, bf16[256,640]{1,0:T(8,128)(2,1)S(1)}, u32[]{:S(2)}, u32[]{:S(2)}) collective-permute-start(bf16[256,640]{1,0:T(8,128)(2,1)S(1)} %pad_maximum_fusion.refs_0_), channel_id=1, source_target_pairs={{0,1},{1,0},{2,3},{3,2},{4,5},{5,4},{6,7},{7,6},{8,9},{9,8},{10,11... | collective-permute-start | bytes 983048 | tf_op jit(solution)/shard_map/ppermute | solution.py:35
  24.6 2.1 %collective-permute-start.7 = (bf16[256,640]{1,0:T(8,128)(2,1)S(1)}, bf16[256,640]{1,0:T(8,128)(2,1)S(1)}, u32[]{:S(2)}, u32[]{:S(2)}) collective-permute-start(bf16[256,640]{1,0:T(8,128)(2,1)S(1)} %collective-permute-done.3.refs_1_), channel_id=1, source_target_pairs={{0,1},{1,0},{2,3},{3,2},{4,5},{5,4},{6,7},{7,6},{8,9},{9,8},{10,11... | collective-permute-start | bytes 983048 | tf_op jit(solution)/shard_map/ppermute | solution.py:35
  25.1 2.1 %collective-permute-start.8 = (bf16[256,640]{1,0:T(8,128)(2,1)S(1)}, bf16[256,640]{1,0:T(8,128)(2,1)S(1)}, u32[]{:S(2)}, u32[]{:S(2)}) collective-permute-start(bf16[256,640]{1,0:T(8,128)(2,1)S(1)} %collective-permute-done.4.refs_2_), channel_id=1, source_target_pairs={{0,1},{1,0},{2,3},{3,2},{4,5},{5,4},{6,7},{7,6},{8,9},{9,8},{10,11... | collective-permute-start | bytes 983048 | tf_op jit(solution)/shard_map/ppermute | solution.py:35
  25.1 2.5 %collective-permute-start.9 = (bf16[256,640]{1,0:T(8,128)(2,1)S(1)}, bf16[256,640]{1,0:T(8,128)(2,1)S(1)}, u32[]{:S(2)}, u32[]{:S(2)}) collective-permute-start(bf16[256,640]{1,0:T(8,128)(2,1)S(1)} %collective-permute-done.5.refs_3_), channel_id=1, source_target_pairs={{0,1},{1,0},{2,3},{3,2},{4,5},{5,4},{6,7},{7,6},{8,9},{9,8},{10,11... | collective-permute-start | bytes 983048 | tf_op jit(solution)/shard_map/ppermute | solution.py:35
  37.9 17.7 %collective-permute-start.10 = (bf16[640,512]{1,0:T(8,128)(2,1)S(1)}, bf16[640,512]{1,0:T(8,128)(2,1)S(1)}, u32[]{:S(2)}, u32[]{:S(2)}) collective-permute-start(bf16[640,512]{1,0:T(8,128)(2,1)S(1)} %get-tuple-element.53), channel_id=1, source_target_pairs={{0,64},{1,17},{2,66},{3,19},{4,68},{5,21},{6,70},{7,23},{8,72},{9,... | collective-permute-start | bytes 1966088 | tf_op jit(solution)/shard_map/ppermute | solution.py:31
  43.7 15.6 %collective-permute-start.11 = (bf16[640,512]{1,0:T(8,128)(2,1)S(1)}, bf16[640,512]{1,0:T(8,128)(2,1)S(1)}, u32[]{:S(2)}, u32[]{:S(2)}) collective-permute-start(bf16[640,512]{1,0:T(8,128)(2,1)S(1)} %get-tuple-element.54), channel_id=1, source_target_pairs={{0,32},{1,9},{2,34},{3,11},{4,36},{5,13},{6,38},{7,15},{8,40},{9,1... | collective-permute-start | bytes 1966088 | tf_op jit(solution)/shard_map/ppermute | solution.py:31
  43.8 15.6 %collective-permute-start.12 = (bf16[640,512]{1,0:T(8,128)(2,1)S(1)}, bf16[640,512]{1,0:T(8,128)(2,1)S(1)}, u32[]{:S(2)}, u32[]{:S(2)}) collective-permute-start(bf16[640,512]{1,0:T(8,128)(2,1)S(1)} %get-tuple-element.55), channel_id=1, source_target_pairs={{0,96},{1,25},{2,98},{3,27},{4,100},{5,29},{6,102},{7,31},{8,104},... | collective-permute-start | bytes 1966088 | tf_op jit(solution)/shard_map/ppermute | solution.py:31
  59.7 14.7 %collective-permute-start.16 = (bf16[640,512]{1,0:T(8,128)(2,1)S(1)}, bf16[640,512]{1,0:T(8,128)(2,1)S(1)}, u32[]{:S(2)}, u32[]{:S(2)}) collective-permute-start(bf16[640,512]{1,0:T(8,128)(2,1)S(1)} %get-tuple-element.62), channel_id=1, source_target_pairs={{0,64},{1,17},{2,66},{3,19},{4,68},{5,21},{6,70},{7,23},{8,72},{9,... | collective-permute-start | bytes 1966088 | tf_op jit(solution)/shard_map/ppermute | solution.py:31
  61.8 20.6 %collective-permute-start.17 = (bf16[640,512]{1,0:T(8,128)(2,1)S(1)}, bf16[640,512]{1,0:T(8,128)(2,1)S(1)}, u32[]{:S(2)}, u32[]{:S(2)}) collective-permute-start(bf16[640,512]{1,0:T(8,128)(2,1)S(1)} %get-tuple-element.63), channel_id=1, source_target_pairs={{0,32},{1,9},{2,34},{3,11},{4,36},{5,13},{6,38},{7,15},{8,40},{9,1... | collective-permute-start | bytes 1966088 | tf_op jit(solution)/shard_map/ppermute | solution.py:31
  63.0 19.4 %collective-permute-start.18 = (bf16[640,512]{1,0:T(8,128)(2,1)S(1)}, bf16[640,512]{1,0:T(8,128)(2,1)S(1)}, u32[]{:S(2)}, u32[]{:S(2)}) collective-permute-start(bf16[640,512]{1,0:T(8,128)(2,1)S(1)} %get-tuple-element.64), channel_id=1, source_target_pairs={{0,96},{1,25},{2,98},{3,27},{4,100},{5,29},{6,102},{7,31},{8,104},... | collective-permute-start | bytes 1966088 | tf_op jit(solution)/shard_map/ppermute | solution.py:31
  65.1 20.8 %collective-permute-start.13 = (bf16[160,512]{1,0:T(8,128)(2,1)S(1)}, bf16[160,512]{1,0:T(8,128)(2,1)S(1)}, u32[]{:S(2)}, u32[]{:S(2)}) collective-permute-start(bf16[160,512]{1,0:T(8,128)(2,1)S(1)} %get-tuple-element.74), channel_id=1, source_target_pairs={{0,16},{1,65},{2,18},{3,67},{4,20},{5,69},{6,22},{7,71},{8,24},{9,... | collective-permute-start | bytes 491528 | tf_op jit(solution)/shard_map/ppermute | solution.py:31
  68.9 19.7 %collective-permute-start.14 = (bf16[160,512]{1,0:T(8,128)(2,1)S(1)}, bf16[160,512]{1,0:T(8,128)(2,1)S(1)}, u32[]{:S(2)}, u32[]{:S(2)}) collective-permute-start(bf16[160,512]{1,0:T(8,128)(2,1)S(1)} %get-tuple-element.73), channel_id=1, source_target_pairs={{0,8},{1,33},{2,10},{3,35},{4,12},{5,37},{6,14},{7,39},{8,16},{9,4... | collective-permute-start | bytes 491528 | tf_op jit(solution)/shard_map/ppermute | solution.py:31
  74.3 14.3 %collective-permute-start.15 = (bf16[160,512]{1,0:T(8,128)(2,1)S(1)}, bf16[160,512]{1,0:T(8,128)(2,1)S(1)}, u32[]{:S(2)}, u32[]{:S(2)}) collective-permute-start(bf16[160,512]{1,0:T(8,128)(2,1)S(1)} %get-tuple-element.72), channel_id=1, source_target_pairs={{0,24},{1,97},{2,26},{3,99},{4,28},{5,101},{6,30},{7,103},{8,0},{9... | collective-permute-start | bytes 491528 | tf_op jit(solution)/shard_map/ppermute | solution.py:31
  82.8 6.9 %collective-permute-start.19 = (bf16[160,512]{1,0:T(8,128)(2,1)S(1)}, bf16[160,512]{1,0:T(8,128)(2,1)S(1)}, u32[]{:S(2)}, u32[]{:S(2)}) collective-permute-start(bf16[160,512]{1,0:T(8,128)(2,1)S(1)} %get-tuple-element.71), channel_id=1, source_target_pairs={{0,16},{1,65},{2,18},{3,67},{4,20},{5,69},{6,22},{7,71},{8,24},{9,... | collective-permute-start | bytes 491528 | tf_op jit(solution)/shard_map/ppermute | solution.py:31
  85.1 6.7 %collective-permute-start.20 = (bf16[160,512]{1,0:T(8,128)(2,1)S(1)}, bf16[160,512]{1,0:T(8,128)(2,1)S(1)}, u32[]{:S(2)}, u32[]{:S(2)}) collective-permute-start(bf16[160,512]{1,0:T(8,128)(2,1)S(1)} %get-tuple-element.70), channel_id=1, source_target_pairs={{0,8},{1,33},{2,10},{3,35},{4,12},{5,37},{6,14},{7,39},{8,16},{9,4... | collective-permute-start | bytes 491528 | tf_op jit(solution)/shard_map/ppermute | solution.py:31
  86.0 5.9 %collective-permute-start.21 = (bf16[160,512]{1,0:T(8,128)(2,1)S(1)}, bf16[160,512]{1,0:T(8,128)(2,1)S(1)}, u32[]{:S(2)}, u32[]{:S(2)}) collective-permute-start(bf16[160,512]{1,0:T(8,128)(2,1)S(1)} %get-tuple-element.69), channel_id=1, source_target_pairs={{0,24},{1,97},{2,26},{3,99},{4,28},{5,101},{6,30},{7,103},{8,0},{9... | collective-permute-start | bytes 491528 | tf_op jit(solution)/shard_map/ppermute | solution.py:31
